TPU v7x, 32 devices: a whole 2x2x4 slice. The times are simulated.
32 devices in a mesh: section: 2 (over core), row: 2 (over y), wide: 8 (over z, x).
Axes of the slice: x: 2, y: 2, z: 4, core: 2. Of those that a mesh axis runs over, the one named last changes fastest.
Arguments:
- inputs: bfloat16 [16, 1024, 768], P('wide', 'row'), may hold values from -6 to 6
- cotangent: bfloat16 [16, 1024, 768], P('wide', 'row'), may hold values from -6 to 6
- segment_ids: int32 [16, 1024], P('wide'), may hold values from 0 to 15, as said below
- step_number: int32 [1], replicated, may hold values from 0 to 999999
- redraw_every: int32 [1], replicated, may hold values from 1 to 1999
- bank_offset: int32 [1], replicated, may hold values from 0 to 999999
- ln1_gain: float32 [2, 768], P('section'), may hold values from 0.1 to 1.9
- ln1_bias: float32 [2, 768], P('section'), may hold values from -1.2 to 1.2
- w_qkv: bfloat16 [2, 768, 2304], P('section'), may hold values from -0.109375 to 0.109375
- b_qkv: float32 [2, 2304], P('section'), may hold values from -0.6 to 0.6
- w_out: bfloat16 [2, 768, 768], P('section'), may hold values from -0.875 to 0.875
- b_out: float32 [2, 768], P('section'), may hold values from -2 to 2
- ln2_gain: float32 [2, 768], P('section'), may hold values from 0.1 to 1.9
- ln2_bias: float32 [2, 768], P('section'), may hold values from -3 to 3
- w_up: bfloat16 [2, 768, 3072], P('section'), may hold values from -0.21875 to 0.21875
- b_up: float32 [2, 3072], P('section'), may hold values from -3 to 3
- w_down: bfloat16 [2, 3072, 768], P('section'), may hold values from -0.109375 to 0.109375
- b_down: float32 [2, 768], P('section'), may hold values from -2 to 2
- bank: float32 [2, 8, 64, 32], P('section'), may hold values from -6 to 6
Outputs:
- hidden: bfloat16 [2, 16, 1024, 768], P('section', 'wide', 'row')
- input_grads: bfloat16 [2, 16, 1024, 768], P('section', 'wide', 'row')
- grad_ln1_gain: float32 [2, 768], P('section')
- grad_ln1_bias: float32 [2, 768], P('section')
- grad_w_qkv: float32 [2, 768, 2304], P('section')
- grad_b_qkv: float32 [2, 2304], P('section')
- grad_w_out: float32 [2, 768, 768], P('section')
- grad_b_out: float32 [2, 768], P('section')
- grad_ln2_gain: float32 [2, 768], P('section')
- grad_ln2_bias: float32 [2, 768], P('section')
- grad_w_up: float32 [2, 768, 3072], P('section')
- grad_b_up: float32 [2, 3072], P('section')
- grad_w_down: float32 [2, 3072, 768], P('section')
- grad_b_down: float32 [2, 768], P('section')
Inputs may be any that keep to these rules, and one draw needn't show every extreme that they name: `segment_ids`: within a sequence the ids never fall, each of 0 to 15 names one run of 1 to 128 consecutive positions, and one run has exactly 128 positions and holds positions on both sides of the sequence's middle.
All inputs are finite; a program needn't handle non-finite values.
Results may differ from a plain program's by a relative error of at most 0.02.
Values may be sent and summed in bfloat16 or wider, within the bound.
No kernel may reach another device: no remote copies, remote signals or barrier semaphores. Data moves between devices by JAX's collectives and lax.ppermute only.
A program may use at most 256 MiB of HBM per device.

v0:
```python
from functools import partial
import math

import jax
import jax.numpy as jnp
from jax import lax
from jax.sharding import PartitionSpec as P

HEADS = 12
HEAD = 64
FEATS = 32
SEGS = 16


precise = lax.Precision.HIGHEST
epsilon = 1e-05


def passed_along(block, axis, distance):
    devices = range(lax.axis_size(axis))
    route = [(i - distance, i) for i in devices if i - distance in devices]
    return lax.ppermute(block, axis, route)


def layer_norm(values, gain_vec, offset):
    centered = values - jnp.mean(values, axis=-1, keepdims=True)
    variance = jnp.mean(centered * centered, axis=-1, keepdims=True)
    return centered * lax.rsqrt(variance + epsilon) * gain_vec + offset


def rotate(vectors, positions):
    halfway = vectors.shape[-1] // 2
    inverse = 10000.0 ** (-2.0 * jnp.arange(halfway, dtype=jnp.float32) / vectors.shape[-1])
    angles = positions[:, None] * inverse[None, :]
    cosine = jnp.cos(angles)[:, None, :]
    sine_part = jnp.sin(angles)[:, None, :]
    former = vectors[..., :halfway]
    latter = vectors[..., halfway:]
    return jnp.concatenate(
        [former * cosine - latter * sine_part, latter * cosine + former * sine_part], axis=-1
    )


def feature_map(vectors, positions, omega):
    turned = rotate(vectors, positions) * vectors.shape[-1] ** (-0.25)
    projected = jnp.einsum("thd,dm->thm", turned, omega, precision=precise)
    squared = 0.5 * jnp.sum(turned * turned, axis=-1, keepdims=True)
    return jnp.exp(projected - squared) / math.sqrt(omega.shape[-1])


def gelu_exact(values):
    return jax.nn.gelu(values, approximate=False)


def over_rows(left, right):
    return lax.dot_general(
        left, right, (((0,), (0,)), ((), ())), preferred_element_type=jnp.float32
    )


def times_transposed(left, right):
    return lax.dot_general(
        left, right, (((1,), (1,)), ((), ())), preferred_element_type=jnp.float32
    )


def column_sum(values):
    return jnp.sum(values.astype(jnp.float32), axis=0)


def pick(flag, former, latter):
    return jnp.where(flag, former, latter)


def spread(onehot, per_token):
    return onehot[:, :, None] * per_token[None, :, :]


def segment_states(onehot, feat_k, values_b):
    seg_count, tokens = onehot.shape
    weighted = spread(onehot, feat_k).reshape(seg_count, tokens, HEADS, FEATS)
    seg_state = jnp.einsum(
        "sthm,thd->shmd",
        weighted,
        values_b.reshape(tokens, HEADS, HEAD),
        preferred_element_type=jnp.float32,
    )
    totals = jnp.einsum("st,tx->sx", onehot, feat_k, preferred_element_type=jnp.float32)
    return (seg_state.reshape(seg_count * HEADS, FEATS * HEAD), totals)


def attention_inputs(weights, layer_in, positions, omega):
    model_width = layer_in.shape[1]
    normed = layer_norm(layer_in.astype(jnp.float32), weights[0], weights[1]).astype(jnp.bfloat16)
    projected = jnp.dot(normed, weights[2], preferred_element_type=jnp.float32) + weights[3]
    queries = projected[:, :model_width].reshape(-1, HEADS, HEAD)
    key_part = projected[:, model_width : 2 * model_width].reshape(-1, HEADS, HEAD)
    values_b = projected[:, 2 * model_width :].astype(jnp.bfloat16)
    feat_q = feature_map(queries, positions, omega).reshape(-1, HEADS * FEATS).astype(jnp.bfloat16)
    feat_k = feature_map(key_part, positions, omega).reshape(-1, HEADS * FEATS).astype(jnp.bfloat16)
    return (normed, queries, key_part, values_b, feat_q, feat_k)


def attention_out(onehot, feat_q, state_b, totals_b):
    seg_count, tokens = onehot.shape
    weighted = spread(onehot, feat_q).reshape(seg_count, tokens, HEADS, FEATS)
    numerator = jnp.einsum(
        "sthm,shmd->thd",
        weighted,
        state_b.reshape(seg_count, HEADS, FEATS, HEAD),
        preferred_element_type=jnp.float32,
    )
    denominator = jnp.einsum(
        "sthm,shm->th",
        weighted,
        totals_b.reshape(seg_count, HEADS, FEATS),
        preferred_element_type=jnp.float32,
    )
    return (numerator, denominator)


def back_ffn(weights, saved, grad_out):
    middle, normed_two, up_pre, active = (saved[12], saved[13], saved[14], saved[15])
    d_down = grad_out.astype(jnp.bfloat16)
    grad_w_down = over_rows(active, d_down)
    grad_b_down = column_sum(d_down)
    d_active = times_transposed(d_down, weights[10])
    gelu_back = jax.vjp(gelu_exact, up_pre)[1]
    d_up = gelu_back(d_active)[0].astype(jnp.bfloat16)
    grad_w_up = over_rows(normed_two, d_up)
    grad_b_up = column_sum(d_up)
    d_normed_two = times_transposed(d_up, weights[8])
    norm_back = jax.vjp(layer_norm, middle, weights[6], weights[7])[1]
    d_mid_norm, grad_gain, grad_shift = norm_back(d_normed_two)
    return (
        grad_out + d_mid_norm,
        (grad_gain, grad_shift, grad_w_up, grad_b_up, grad_w_down, grad_b_down),
    )


def back_attention(weights, saved, d_middle, positions, omega):
    layer_in, normed, queries, key_part, values_b, feat_q, feat_k, state_b, totals_b = saved[:9]
    numerator, denominator, attended, onehot = (saved[9], saved[10], saved[11], saved[16])
    seg_count, tokens = onehot.shape
    d_branch = d_middle.astype(jnp.bfloat16)
    grad_w_out = over_rows(attended, d_branch)
    grad_b_out = column_sum(d_branch)
    d_att = times_transposed(d_branch, weights[4]).reshape(tokens, HEADS, HEAD)
    d_num = (d_att / denominator[:, :, None]).astype(jnp.bfloat16)
    d_den = (-jnp.sum(d_att * numerator, axis=-1) / (denominator * denominator)).astype(
        jnp.bfloat16
    )
    weighted_q = spread(onehot, feat_q).reshape(seg_count, tokens, HEADS, FEATS)
    part_state = jnp.einsum("sthm,thd->shmd", weighted_q, d_num, preferred_element_type=jnp.float32)
    part_totals = jnp.einsum("sthm,th->shm", weighted_q, d_den, preferred_element_type=jnp.float32)
    sum_state, sum_totals = (
        lax.psum(
            part_state.reshape(seg_count * HEADS, FEATS * HEAD).astype(jnp.bfloat16), "row"
        ).astype(jnp.float32),
        lax.psum(part_totals.reshape(seg_count, HEADS * FEATS).astype(jnp.bfloat16), "row").astype(
            jnp.float32
        ),
    )
    d_state = sum_state.astype(jnp.bfloat16).reshape(seg_count, HEADS, FEATS, HEAD)
    d_totals = sum_totals.astype(jnp.bfloat16)
    spread_num = spread(onehot, d_num.reshape(tokens, HEADS * HEAD)).reshape(
        seg_count, tokens, HEADS, HEAD
    )
    token_totals = jnp.einsum(
        "st,sx->tx", onehot, totals_b, preferred_element_type=jnp.float32
    ).reshape(tokens, HEADS, FEATS)
    d_feat_q = jnp.einsum(
        "sthd,shmd->thm",
        spread_num,
        state_b.reshape(seg_count, HEADS, FEATS, HEAD),
        preferred_element_type=jnp.float32,
    )
    d_feat_q = d_feat_q + token_totals * d_den.astype(jnp.float32)[:, :, None]
    spread_val = spread(onehot, values_b).reshape(seg_count, tokens, HEADS, HEAD)
    d_feat_k = jnp.einsum("sthd,shmd->thm", spread_val, d_state, preferred_element_type=jnp.float32)
    d_feat_k = d_feat_k + jnp.einsum(
        "st,sx->tx", onehot, d_totals, preferred_element_type=jnp.float32
    ).reshape(tokens, HEADS, FEATS)
    weighted_k = spread(onehot, feat_k).reshape(seg_count, tokens, HEADS, FEATS)
    d_values = jnp.einsum("sthm,shmd->thd", weighted_k, d_state, preferred_element_type=jnp.float32)
    query_back = jax.vjp(partial(feature_map, positions=positions, omega=omega), queries)[1]
    key_back = jax.vjp(partial(feature_map, positions=positions, omega=omega), key_part)[1]
    d_queries = query_back(d_feat_q)[0].reshape(tokens, HEADS * HEAD)
    d_keys = key_back(d_feat_k)[0].reshape(tokens, HEADS * HEAD)
    d_projected = jnp.concatenate(
        [d_queries, d_keys, d_values.reshape(tokens, HEADS * HEAD)], axis=1
    ).astype(jnp.bfloat16)
    grad_w_qkv = over_rows(normed, d_projected)
    grad_b_qkv = column_sum(d_projected)
    d_normed = times_transposed(d_projected, weights[2])
    norm_back = jax.vjp(layer_norm, layer_in.astype(jnp.float32), weights[0], weights[1])[1]
    d_in_norm, grad_gain, grad_shift = norm_back(d_normed)
    return (
        d_middle + d_in_norm,
        (grad_gain, grad_shift, grad_w_qkv, grad_b_qkv, grad_w_out, grad_b_out),
    )


def local(
    inputs,
    cotangent,
    segment_ids,
    step_number,
    redraw_every,
    bank_offset,
    ln1_gain,
    ln1_bias,
    w_qkv,
    b_qkv,
    w_out,
    b_out,
    ln2_gain,
    ln2_bias,
    w_up,
    b_up,
    w_down,
    b_down,
    bank,
):
    weights = tuple(
        (
            member[0]
            for member in (
                ln1_gain,
                ln1_bias,
                w_qkv,
                b_qkv,
                w_out,
                b_out,
                ln2_gain,
                ln2_bias,
                w_up,
                b_up,
                w_down,
                b_down,
            )
        )
    )
    section_index = lax.axis_index("section")
    first_section = section_index == 0
    micro_count = inputs.shape[0]
    local_len = inputs.shape[1]
    row_start = lax.axis_index("row") * local_len
    positions = (row_start + jnp.arange(local_len, dtype=jnp.int32)).astype(jnp.float32)
    chosen = (bank_offset[0] + step_number[0] // redraw_every[0]) % bank.shape[1]
    omega = lax.dynamic_index_in_dim(bank[0], chosen, 0, keepdims=False)
    labels = jnp.arange(SEGS, dtype=jnp.int32)[:, None]
    received = jnp.zeros_like(inputs[0])
    tick_saved = []
    tick_out = []
    for tick_num in range(micro_count + 1):
        batch_index = jnp.clip(tick_num - section_index, 0, micro_count - 1)
        sequence_ids = lax.dynamic_index_in_dim(segment_ids, batch_index, 0, keepdims=False)
        local_ids = lax.dynamic_slice_in_dim(sequence_ids, row_start, local_len)
        onehot = (labels == local_ids[None, :]).astype(jnp.bfloat16)
        layer_in = jnp.where(first_section, inputs[min(tick_num, micro_count - 1)], received)
        normed, queries, key_part, values_b, feat_q, feat_k = attention_inputs(
            weights, layer_in, positions, omega
        )
        part_state, part_totals = segment_states(onehot, feat_k, values_b)
        sum_state, sum_totals = (
            lax.psum(part_state.astype(jnp.bfloat16), "row").astype(jnp.float32),
            lax.psum(part_totals.astype(jnp.bfloat16), "row").astype(jnp.float32),
        )
        state_b = sum_state.astype(jnp.bfloat16)
        totals_b = sum_totals.astype(jnp.bfloat16)
        numerator, denominator = attention_out(onehot, feat_q, state_b, totals_b)
        attended = (numerator / denominator[:, :, None]).reshape(local_len, -1).astype(jnp.bfloat16)
        middle = (
            layer_in.astype(jnp.float32)
            + jnp.dot(attended, weights[4], preferred_element_type=jnp.float32)
            + weights[5]
        )
        normed_two = layer_norm(middle, weights[6], weights[7]).astype(jnp.bfloat16)
        up_pre = jnp.dot(normed_two, weights[8], preferred_element_type=jnp.float32) + weights[9]
        active = gelu_exact(up_pre).astype(jnp.bfloat16)
        result = (
            middle + jnp.dot(active, weights[10], preferred_element_type=jnp.float32) + weights[11]
        ).astype(jnp.bfloat16)
        if tick_num < micro_count:
            received = passed_along(result, "section", 1)
        tick_saved.append(
            (
                layer_in,
                normed,
                queries,
                key_part,
                values_b,
                feat_q,
                feat_k,
                state_b,
                totals_b,
                numerator,
                denominator,
                attended,
                middle,
                normed_two,
                up_pre,
                active,
                onehot,
            )
        )
        tick_out.append(result)
    hidden = jnp.stack(
        [pick(first_section, tick_out[batch], tick_out[batch + 1]) for batch in range(micro_count)]
    )[None]
    received_back = jnp.zeros_like(inputs[0])
    back_out = []
    ffn_total = None
    attn_total = None
    for tick_num in range(micro_count + 1):
        earlier = tick_saved[max(tick_num - 1, 0)]
        later = tick_saved[min(tick_num + 1, micro_count)]
        saved = jax.tree.map(partial(pick, first_section), earlier, later)
        valid = jnp.where(first_section, float(tick_num >= 1), float(tick_num < micro_count))
        grad_out = (
            jnp.where(
                first_section, received_back, cotangent[min(tick_num, micro_count - 1)]
            ).astype(jnp.float32)
            * valid
        )
        d_middle, ffn_grads = back_ffn(weights, saved, grad_out)
        ffn_total = ffn_grads if ffn_total is None else jax.tree.map(jnp.add, ffn_total, ffn_grads)
        d_input, attn_grads = back_attention(weights, saved, d_middle, positions, omega)
        attn_total = (
            attn_grads if attn_total is None else jax.tree.map(jnp.add, attn_total, attn_grads)
        )
        d_input_b = d_input.astype(jnp.bfloat16)
        if tick_num < micro_count:
            received_back = passed_along(d_input_b, "section", -1)
        back_out.append(d_input_b)
    input_grads = jnp.stack(
        [pick(first_section, back_out[batch + 1], back_out[batch]) for batch in range(micro_count)]
    )[None]
    grad_all = tuple(attn_total) + tuple(ffn_total)
    parts = (
        lax.psum_scatter(grad_all[0][None], ("row", "wide"), scatter_dimension=1, tiled=True),
        lax.psum_scatter(grad_all[1][None], ("row", "wide"), scatter_dimension=1, tiled=True),
        lax.psum_scatter(grad_all[2][None], ("row", "wide"), scatter_dimension=1, tiled=True),
        lax.psum_scatter(grad_all[3][None], ("row", "wide"), scatter_dimension=1, tiled=True),
        lax.psum_scatter(grad_all[4][None], ("row", "wide"), scatter_dimension=1, tiled=True),
        lax.psum_scatter(grad_all[5][None], ("row", "wide"), scatter_dimension=1, tiled=True),
        lax.psum_scatter(grad_all[6][None], ("row", "wide"), scatter_dimension=1, tiled=True),
        lax.psum_scatter(grad_all[7][None], ("row", "wide"), scatter_dimension=1, tiled=True),
        lax.psum_scatter(grad_all[8][None], ("row", "wide"), scatter_dimension=1, tiled=True),
        lax.psum_scatter(grad_all[9][None], ("row", "wide"), scatter_dimension=1, tiled=True),
        lax.psum_scatter(grad_all[10][None], ("row", "wide"), scatter_dimension=1, tiled=True),
        lax.psum_scatter(grad_all[11][None], ("row", "wide"), scatter_dimension=1, tiled=True),
    )
    grad_all = tuple(
        (
            lax.all_gather(
                parts[0].astype(jnp.bfloat16), ("row", "wide"), axis=1, tiled=True
            ).astype(jnp.float32),
            lax.all_gather(
                parts[1].astype(jnp.bfloat16), ("row", "wide"), axis=1, tiled=True
            ).astype(jnp.float32),
            lax.all_gather(
                parts[2].astype(jnp.bfloat16), ("row", "wide"), axis=1, tiled=True
            ).astype(jnp.float32),
            lax.all_gather(
                parts[3].astype(jnp.bfloat16), ("row", "wide"), axis=1, tiled=True
            ).astype(jnp.float32),
            lax.all_gather(
                parts[4].astype(jnp.bfloat16), ("row", "wide"), axis=1, tiled=True
            ).astype(jnp.float32),
            lax.all_gather(
                parts[5].astype(jnp.bfloat16), ("row", "wide"), axis=1, tiled=True
            ).astype(jnp.float32),
            lax.all_gather(
                parts[6].astype(jnp.bfloat16), ("row", "wide"), axis=1, tiled=True
            ).astype(jnp.float32),
            lax.all_gather(
                parts[7].astype(jnp.bfloat16), ("row", "wide"), axis=1, tiled=True
            ).astype(jnp.float32),
            lax.all_gather(
                parts[8].astype(jnp.bfloat16), ("row", "wide"), axis=1, tiled=True
            ).astype(jnp.float32),
            lax.all_gather(
                parts[9].astype(jnp.bfloat16), ("row", "wide"), axis=1, tiled=True
            ).astype(jnp.float32),
            lax.all_gather(
                parts[10].astype(jnp.bfloat16), ("row", "wide"), axis=1, tiled=True
            ).astype(jnp.float32),
            lax.all_gather(
                parts[11].astype(jnp.bfloat16), ("row", "wide"), axis=1, tiled=True
            ).astype(jnp.float32),
        )
    )
    return (
        hidden,
        input_grads,
        grad_all[0],
        grad_all[1],
        grad_all[2],
        grad_all[3],
        grad_all[4],
        grad_all[5],
        grad_all[6],
        grad_all[7],
        grad_all[8],
        grad_all[9],
        grad_all[10],
        grad_all[11],
    )


def solution(mesh):
    return jax.shard_map(
        local,
        mesh=mesh,
        in_specs=(
            P("wide", "row", None),
            P("wide", "row", None),
            P("wide", None),
            P(),
            P(),
            P(),
            P("section", None),
            P("section", None),
            P("section", None, None),
            P("section", None),
            P("section", None, None),
            P("section", None),
            P("section", None),
            P("section", None),
            P("section", None, None),
            P("section", None),
            P("section", None, None),
            P("section", None),
            P("section", None, None, None),
        ),
        out_specs=(
            P("section", "wide", "row", None),
            P("section", "wide", "row", None),
            P("section", None),
            P("section", None),
            P("section", None, None),
            P("section", None),
            P("section", None, None),
            P("section", None),
            P("section", None),
            P("section", None),
            P("section", None, None),
            P("section", None),
            P("section", None, None),
            P("section", None),
        ),
        check_vma=False,
    )
```

profile of v0, /device:TPU:0, one launch (start us, length us, event | category | flops | bytes accessed | tf_op | source)
XLA Modules:
  0.0 2708.6 jit_solution(8531044276127377365)
XLA Ops:
  47.4 4.9 broadcast_multiply_fusion.10
  63.2 11.2 psum.85
  75.9 3.9 fusion.40
  83.0 15.1 all-reduce.29.cloned.1.call-done
  101.5 4.1 fusion.196
  107.0 30.8 %fusion.14 = (bf16[512,3072]{1,0:T(8,128)(2,1)S(1)}, f32[512,3072]{1,0:T(8,128)}) fusion(f32[3072]{0:T(1024)S(1)} %bitcast.719, bf16[1,768,3072]{2,1,0:T(8,128)(2,1)} %param.33, f32[512,768]{1,0:T(8,128)S(1)} %get-tuple-element.206, f32[768]{0:T(1024)S(1)} %reduce.5, f32[768]{0:T(1024)S(1)} %reduce.4, f32[512]{0:T(512)S(1)} %add_rsqrt_fusion.4, ...), kind=kOutput, calls=%fused_computation.23 | convolution fusion | flops 2521694208 | bytes 15751168 | tf_op jit(solution)/shard_map/dot_general | solution.py:280
  172.3 8.4 psum.87
  184.4 4.9 broadcast_multiply_fusion.9
  197.8 3.8 fusion.38
  208.4 24.8 all-reduce.31.cloned.1.call-done
  233.2 3.8 reshape.1070
  237.0 4.6 broadcast_select_fusion.5
  244.1 18.0 fusion.17
  266.8 21.7 convert_reduce_fusion.2
  312.1 5.0 broadcast_select_fusion.7
  320.2 5.5 multiply_subtract_fusion.1
  329.5 3.8 broadcast_select_fusion.20
  339.9 4.2 fusion.415
  346.3 8.4 all-reduce.21
  373.9 4.9 fusion.550
  406.7 56.0 %all-reduce.37.cloned.1.call-done = (bf16[192,2048]{1,0:T(8,128)(2,1)}, bf16[16,12,32,64]{3,2,0,1:T(8,128)(2,1)}) async-done(((bf16[192,2048]{1,0:T(8,128)(2,1)}, bf16[16,12,32,64]{3,2,0,1:T(8,128)(2,1)}), (bf16[192,2048]{1,0:T(8,128)(2,1)}, bf16[16,12,32,64]{3,2,0,1:T(8,128)(2,1)})) %all-reduce.37.cloned.1.call-update) | async-done | bytes 1572880 | tf_op jit(solution)/shard_map/psum | solution.py:267
  466.2 4.5 broadcast_select_fusion.4
  482.5 4.3 fusion.337
  501.5 5.7 fusion.387
  527.2 4.8 fusion.114
  534.7 35.3 %convert_reduce_fusion.1 = (f32[3072]{0:T(1024)}, bf16[512,3072]{1,0:T(8,128)(2,1)S(1)}, bf16[512,3072]{1,0:T(8,128)(2,1)}) fusion(f32[512,3072]{1,0:T(8,128)S(1)} %fusion.114, f32[512,3072]{1,0:T(8,128)} %get-tuple-element.208, f32[3072]{0:T(1024)S(1)} %bitcast.722, pred[]{:T(512)S(6)} %eq.80, bf16[512,768]{1,0:T(8,128)(2,1)S(1)} %get-tuple-element.55, ...), kind=kOutput, calls=%fused_computation.52 | convolution fusion | flops 2639262720 | bytes 24403968 | tf_op jit(solution)/shard_map/dot_general | solution.py:62
  582.3 4.3 fusion.331
  593.1 4.2 fusion.416
  599.5 8.7 psum.93
  614.1 21.2 all-reduce.33.cloned.1.call-done
  635.3 4.3 fusion.343
  655.8 5.7 fusion.385
  662.7 18.1 convert_reduce_fusion
  693.3 5.2 fusion.417
  700.7 8.5 psum.95
  714.0 4.3 fusion.325
  727.5 18.5 all-reduce.35.cloned.1.call-done
  746.0 4.3 fusion.346
  759.0 5.7 add_bitcast_fusion.2
  765.4 5.5 fusion.382
  773.9 9.1 add_bitcast_fusion.1
  783.5 8.8 fusion.132
  795.2 11.9 add_bitcast_fusion
  824.3 4.2 fusion.518
  834.9 44.8 %reduce-scatter.31.cloned.1.call-done = f32[1,48,768]{2,1,0:T(8,128)} async-done(((f32[1,768,768]{2,1,0:T(8,128)}), f32[1,48,768]{2,1,0:T(8,128)}) %reduce-scatter.31.cloned.1.call-update) | async-done | bytes 147472 | tf_op jit(solution)/shard_map/reduce_scatter | solution.py:346
  881.3 153.8 %reduce-scatter.29.cloned.1.call-done = f32[1,48,2304]{2,1,0:T(8,128)} async-done(((f32[1,768,2304]{2,1,0:T(8,128)}), f32[1,48,2304]{2,1,0:T(8,128)}) %reduce-scatter.29.cloned.1.call-update) | async-done | bytes 442384 | tf_op jit(solution)/shard_map/reduce_scatter | solution.py:344
  1036.9 174.5 %reduce-scatter.33.cloned.1.call-done = f32[1,48,3072]{2,1,0:T(8,128)} async-done(((f32[1,768,3072]{2,1,0:T(8,128)}), f32[1,48,3072]{2,1,0:T(8,128)}) %reduce-scatter.33.cloned.1.call-update) | async-done | bytes 589840 | tf_op jit(solution)/shard_map/reduce_scatter | solution.py:350
  1213.3 175.2 %reduce-scatter.35.cloned.1.call-done = f32[1,192,768]{2,1,0:T(8,128)} async-done(((f32[1,3072,768]{2,1,0:T(8,128)}), f32[1,192,768]{2,1,0:T(8,128)}) %reduce-scatter.35.cloned.1.call-update) | async-done | bytes 589840 | tf_op jit(solution)/shard_map/reduce_scatter | solution.py:352
  1394.3 5.9 fusion.358
  1401.5 112.1 %reduce-scatter.43.cloned.1.call-done = f32[48,1]{1,0:T(8,128)} async-done(((f32[768,1]{1,0:T(8,128)}), f32[48,1]{1,0:T(8,128)}) %reduce-scatter.43.cloned.1.call-update) | async-done | bytes 208
  1515.7 124.0 %reduce-scatter.45.cloned.1.call-done = f32[48,1]{1,0:T(8,128)} async-done(((f32[768,1]{1,0:T(8,128)}), f32[48,1]{1,0:T(8,128)}) %reduce-scatter.45.cloned.1.call-update) | async-done | bytes 208
  1642.4 122.7 %reduce-scatter.47.cloned.1.call-done = f32[48,1]{1,0:T(8,128)} async-done(((f32[768,1]{1,0:T(8,128)}), f32[48,1]{1,0:T(8,128)}) %reduce-scatter.47.cloned.1.call-update) | async-done | bytes 208
  1767.7 123.5 %reduce-scatter.51.cloned.1.call-done = f32[48,1]{1,0:T(8,128)} async-done(((f32[768,1]{1,0:T(8,128)}), f32[48,1]{1,0:T(8,128)}) %reduce-scatter.51.cloned.1.call-update) | async-done | bytes 208
  1898.7 120.7 %reduce-scatter.49.cloned.1.call-done = f32[192,1]{1,0:T(8,128)} async-done(((f32[3072,1]{1,0:T(8,128)}), f32[192,1]{1,0:T(8,128)}) %reduce-scatter.49.cloned.1.call-update) | async-done | bytes 784
  2028.4 116.2 %reduce-scatter.37.cloned.1.call-done = f32[48,1]{1,0:T(8,128)} async-done(((f32[768,1]{1,0:T(8,128)}), f32[48,1]{1,0:T(8,128)}) %reduce-scatter.37.cloned.1.call-update) | async-done | bytes 208
  2146.0 124.6 %reduce-scatter.39.cloned.1.call-done = f32[48,1]{1,0:T(8,128)} async-done(((f32[768,1]{1,0:T(8,128)}), f32[48,1]{1,0:T(8,128)}) %reduce-scatter.39.cloned.1.call-update) | async-done | bytes 208
  2273.6 125.1 %reduce-scatter.41.cloned.1.call-done = f32[144,1]{1,0:T(8,128)} async-done(((f32[2304,1]{1,0:T(8,128)}), f32[144,1]{1,0:T(8,128)}) %reduce-scatter.41.cloned.1.call-update) | async-done | bytes 592
  2401.1 75.3 %all-reduce.20 = (bf16[768]{0:T(1024)(128)(2,1)}, bf16[768]{0:T(1024)(128)(2,1)}, bf16[2304]{0:T(1024)(128)(2,1)}, bf16[768]{0:T(1024)(128)(2,1)}, bf16[768]{0:T...) all-reduce(bf16[768]{0:T(1024)(128)(2,1)} %copy-done.243, ...), channel_id=1, replica_groups=mesh['section'=2,'row'=2,'wide'=8] {'row','wide'}, use_global_device_ids=true, to_apply=%add.12 | all-reduce | flops 9984 | bytes 39936
  2489.4 41.3 %all-gather.5.cloned.1.call-done = bf16[1,768,2304]{2,1,0:T(8,128)(2,1)} async-done(((bf16[1,48,2304]{2,1,0:T(8,128)(2,1)}), bf16[1,768,2304]{2,1,0:T(8,128)(2,1)}) %all-gather.5.cloned.1.call-update) | async-done | bytes 3538960 | tf_op jit(solution)/shard_map/all_gather | solution.py:363
  2530.7 5.5 convert_element_type.621
  2536.1 76.7 %all-gather.9.cloned.1.call-done = bf16[1,768,3072]{2,1,0:T(8,128)(2,1)} async-done(((bf16[1,48,3072]{2,1,0:T(8,128)(2,1)}), bf16[1,768,3072]{2,1,0:T(8,128)(2,1)}) %all-gather.9.cloned.1.call-update) | async-done | bytes 4718608 | tf_op jit(solution)/shard_map/all_gather | solution.py:381
  2612.9 7.4 convert_element_type.639
  2620.2 74.5 %all-gather.11.cloned.1.call-done = bf16[1,3072,768]{2,1,0:T(8,128)(2,1)} async-done(((bf16[1,192,768]{2,1,0:T(8,128)(2,1)}), bf16[1,3072,768]{2,1,0:T(8,128)(2,1)}) %all-gather.11.cloned.1.call-update) | async-done | bytes 4718608 | tf_op jit(solution)/shard_map/all_gather | solution.py:387
  2694.8 6.8 convert_element_type.647
  (956 shorter events, 420.9 us)
Async XLA Ops:
  7.2 90.9 %all-reduce.29.cloned.1.call-start = ((), (), s32[]{:S(2)}) async-start(), calls=%async_computation.12 | async-start | bytes 1572864 | tf_op jit(solution)/shard_map/psum | solution.py:267
  12.4 499.5 %copy-start.151 = (f32[768]{0:T(1024)}, f32[768]{0:T(1024)S(1)}, u32[]{:S(2)}) copy-start(f32[768]{0:T(1024)S(1)} %reduce) | copy-start | bytes 9220
  35.8 25.5 copy-start.173
  35.8 110.2 %copy-start.168 = (s32[1,512]{1,0:T(1,128)}, s32[1,512]{1,0:T(1,128)S(1)}, u32[]{:S(2)}) copy-start(s32[1,512]{1,0:T(1,128)S(1)} %get-tuple-element.189) | copy-start | bytes 6148
  60.7 172.5 %all-reduce.31.cloned.1.call-start = ((), (), s32[]{:S(2)}) async-start(), calls=%async_computation.13 | async-start | bytes 1572864 | tf_op jit(solution)/shard_map/psum | solution.py:267
  81.0 161.9 %copy-start.138 = (f32[768]{0:T(1024)}, f32[768]{0:T(1024)S(1)}, u32[]{:S(2)}) copy-start(f32[768]{0:T(1024)S(1)} %reduce.5) | copy-start | bytes 9220
  81.7 392.0 %copy-start.136 = (f32[768]{0:T(1024)}, f32[768]{0:T(1024)S(1)}, u32[]{:S(2)}) copy-start(f32[768]{0:T(1024)S(1)} %reduce.4) | copy-start | bytes 9220
  105.7 32.2 %slice-start.16 = ((s8[4718592]{0:T(1024)(128)(4,1)}), s8[4194304]{0:T(1024)(128)(4,1)S(1)}, s32[]{:S(2)}) async-start(s8[4718592]{0:T(1024)(128)(4,1)} %bitcast.713), calls=%async_computation.49 | async-start | bytes 8388608
  106.6 31.2 %copy-start.1 = (f32[512,768]{1,0:T(8,128)}, f32[512,768]{1,0:T(8,128)S(1)}, u32[]{:S(2)}) copy-start(f32[512,768]{1,0:T(8,128)S(1)} %get-tuple-element.206) | copy-start | bytes 4718596
  106.7 31.2 %copy-start.166 = (f32[512]{0:T(512)}, f32[512]{0:T(512)S(1)}, u32[]{:S(2)}) copy-start(f32[512]{0:T(512)S(1)} %broadcast_multiply_fusion.40) | copy-start | bytes 6148
  107.0 30.9 %copy-start.186 = (f32[512]{0:T(512)}, f32[512]{0:T(512)S(1)}, u32[]{:S(2)}) copy-start(f32[512]{0:T(512)S(1)} %add_rsqrt_fusion.4) | copy-start | bytes 6148
  107.0 30.9 %copy-start.244 = (f32[768]{0:T(1024)S(1)}, f32[768]{0:T(1024)}, u32[]{:S(2)}) copy-start(f32[768]{0:T(1024)} %reduce.6) | copy-start | bytes 9220
  107.0 30.9 %slice-start.17 = ((s8[4718592]{0:T(1024)(128)(4,1)}), s8[524288]{0:T(1024)(128)(4,1)S(1)}, s32[]{:S(2)}) async-start(s8[4718592]{0:T(1024)(128)(4,1)} %bitcast.713), calls=%async_computation.50 | async-start | bytes 1048576
  141.5 5.9 collective-permute-start
  197.7 264.9 %all-reduce.37.cloned.1.call-start = ((), (), s32[]{:S(2)}) async-start(), calls=%async_computation.32 | async-start | bytes 4718592 | tf_op jit(solution)/shard_map/psum | solution.py:267
  242.6 19.5 copy-start.28
  243.3 18.8 slice-start.18
  243.4 23.4 slice-start.22
  243.9 18.2 copy-start.55
  244.1 18.0 copy-start.245
  244.1 18.0 slice-start.19
  244.1 22.6 slice-start.23
  264.8 23.7 copy-start.141
  264.8 27.8 %collective-permute-start.1 = (bf16[512,768]{1,0:T(8,128)(2,1)S(1)}, bf16[512,768]{1,0:T(8,128)(2,1)S(1)}, u32[]{:S(2)}, u32[]{:S(2)}) collective-permute-start(bf16[512,768]{1,0:T(8,128)(2,1)S(1)} %add_convert_fusion.11), channel_id=1, source_target_pairs={{0,16},{1,17},{2,18},{3,19},{4,20},{5,21},{6,22},{7,23},{8,24},{9,... | collective-permute-start | bytes 2359304 | tf_op jit(solution)/shard_map/ppermute | solution.py:22
  392.5 242.8 %all-reduce.33.cloned.1.call-start = ((), (), s32[]{:S(2)}) async-start(), calls=%async_computation.14 | async-start | bytes 3145728 | tf_op jit(solution)/shard_map/psum | solution.py:157
  513.7 18.4 collective-permute-start.2
  527.2 42.7 %slice-start.12 = ((s8[4718592]{0:T(1024)(128)(4,1)}), s8[4194304]{0:T(1024)(128)(4,1)S(1)}, s32[]{:S(2)}) async-start(s8[4718592]{0:T(1024)(128)(4,1)} %bitcast.628), calls=%async_computation.45 | async-start | bytes 8388608
  532.0 37.9 %copy-start.88 = (f32[512,3072]{1,0:T(8,128)}, f32[512,3072]{1,0:T(8,128)S(1)}, u32[]{:S(2)}) copy-start(f32[512,3072]{1,0:T(8,128)S(1)} %fusion.114) | copy-start | bytes 18874372
  534.6 39.5 %copy-start.32 = (bf16[512,768]{1,0:T(8,128)(2,1)}, bf16[512,768]{1,0:T(8,128)(2,1)S(1)}, u32[]{:S(2)}) copy-start(bf16[512,768]{1,0:T(8,128)(2,1)S(1)} %get-tuple-element.55) | copy-start | bytes 2359300
  534.6 35.3 %copy-start.31 = (f32[512,768]{1,0:T(8,128)S(1)}, f32[512,768]{1,0:T(8,128)}, u32[]{:S(2)}) copy-start(f32[512,768]{1,0:T(8,128)} %get-tuple-element.153) | copy-start | bytes 4718596
  534.6 35.3 %slice-start.13 = ((s8[4718592]{0:T(1024)(128)(4,1)}), s8[524288]{0:T(1024)(128)(4,1)S(1)}, s32[]{:S(2)}) async-start(s8[4718592]{0:T(1024)(128)(4,1)} %bitcast.628), calls=%async_computation.46 | async-start | bytes 1048576
  534.6 35.3 %copy-start.137 = (f32[768]{0:T(1024)S(1)}, f32[768]{0:T(1024)}, u32[]{:S(2)}) copy-start(f32[768]{0:T(1024)} %copy-done.136) | copy-start | bytes 9220
  534.6 35.3 %copy-start.239 = (f32[512]{0:T(512)S(1)}, f32[512]{0:T(512)}, u32[]{:S(2)}) copy-start(f32[512]{0:T(512)} %fusion.472) | copy-start | bytes 6148
  582.2 163.8 %all-reduce.35.cloned.1.call-start = ((), (), s32[]{:S(2)}) async-start(), calls=%async_computation.15 | async-start | bytes 3145728 | tf_op jit(solution)/shard_map/psum | solution.py:157
  653.7 7.9 collective-permute-start.3
  655.8 25.0 slice-start.14
  662.6 22.4 copy-start.47
  662.7 18.1 copy-start.27
  662.7 18.1 slice-start.15
  662.7 18.1 copy-start.219
  693.1 186.6 %reduce-scatter.31.cloned.1.call-start = ((), (), s32[]{:S(2)}) async-start(), calls=%async_computation.18 | async-start | bytes 2506752 | tf_op jit(solution)/shard_map/reduce_scatter | solution.py:346
  713.9 321.2 %reduce-scatter.29.cloned.1.call-start = ((), (), s32[]{:S(2)}) async-start(), calls=%async_computation.16 | async-start | bytes 7520256 | tf_op jit(solution)/shard_map/reduce_scatter | solution.py:344
  764.8 446.6 %reduce-scatter.33.cloned.1.call-start = ((), (), s32[]{:S(2)}) async-start(), calls=%async_computation.20 | async-start | bytes 10027008 | tf_op jit(solution)/shard_map/reduce_scatter | solution.py:350
  783.0 605.5 %reduce-scatter.35.cloned.1.call-start = ((), (), s32[]{:S(2)}) async-start(), calls=%async_computation.22 | async-start | bytes 10027008 | tf_op jit(solution)/shard_map/reduce_scatter | solution.py:352
  807.0 706.6 %reduce-scatter.43.cloned.1.call-start = ((), (), s32[]{:S(2)}) async-start(), calls=%async_computation.27 | async-start | bytes 417792
  807.7 20.8 copy-start.217
  812.4 827.4 %reduce-scatter.45.cloned.1.call-start = ((), (), s32[]{:S(2)}) async-start(), calls=%async_computation.28 | async-start | bytes 417792
  814.1 950.9 %reduce-scatter.47.cloned.1.call-start = ((), (), s32[]{:S(2)}) async-start(), calls=%async_computation.29 | async-start | bytes 417792
  815.8 1075.3 %reduce-scatter.51.cloned.1.call-start = ((), (), s32[]{:S(2)}) async-start(), calls=%async_computation.31 | async-start | bytes 417792
  817.5 1202.0 %reduce-scatter.49.cloned.1.call-start = ((), (), s32[]{:S(2)}) async-start(), calls=%async_computation.30 | async-start | bytes 1671168
  821.3 1323.4 %reduce-scatter.37.cloned.1.call-start = ((), (), s32[]{:S(2)}) async-start(), calls=%async_computation.24 | async-start | bytes 417792
  830.9 1439.7 %reduce-scatter.39.cloned.1.call-start = ((), (), s32[]{:S(2)}) async-start(), calls=%async_computation.25 | async-start | bytes 417792
  832.6 1566.1 %reduce-scatter.41.cloned.1.call-start = ((), (), s32[]{:S(2)}) async-start(), calls=%async_computation.26 | async-start | bytes 1253376
  834.8 555.5 %copy-start.264 = (u32[32]{0:T(128)S(1)}, u32[32]{0:T(128)}, u32[]{:S(2)}) copy-start(u32[32]{0:T(128)} %constant.269) | copy-start | bytes 388
  834.9 1651.7 %all-gather.7.cloned.1.call-start = ((), (), s32[]{:S(2)}) async-start(), calls=%async_computation.19 | async-start | bytes 1253376 | tf_op jit(solution)/shard_map/all_gather | solution.py:369
  881.2 1649.4 %all-gather.5.cloned.1.call-start = ((), (), s32[]{:S(2)}) async-start(), calls=%async_computation.17 | async-start | bytes 3760128 | tf_op jit(solution)/shard_map/all_gather | solution.py:363
  1036.8 357.4 %copy-start.246 = (f32[768]{0:T(1024)S(1)}, f32[768]{0:T(1024)}, u32[]{:S(2)}) copy-start(f32[768]{0:T(1024)} %reduce.6) | copy-start | bytes 9220
  1036.9 1576.0 %all-gather.9.cloned.1.call-start = ((), (), s32[]{:S(2)}) async-start(), calls=%async_computation.21 | async-start | bytes 5013504 | tf_op jit(solution)/shard_map/all_gather | solution.py:381
  1213.2 1481.5 %all-gather.11.cloned.1.call-start = ((), (), s32[]{:S(2)}) async-start(), calls=%async_computation.23 | async-start | bytes 5013504 | tf_op jit(solution)/shard_map/all_gather | solution.py:387
  1400.2 623.6 %copy-start.215 = (f32[512]{0:T(512)S(1)}, f32[512]{0:T(512)}, u32[]{:S(2)}) copy-start(f32[512]{0:T(512)} %copy-done.214) | copy-start | bytes 6148
  1894.0 128.2 %copy-start.240 = (bf16[768]{0:T(1024)(128)(2,1)}, bf16[768]{0:T(1024)(128)(2,1)S(1)}, u32[]{:S(2)}) copy-start(bf16[768]{0:T(1024)(128)(2,1)S(1)} %dynamic-update-slice.3) | copy-start | bytes 4612
  1894.9 127.4 %copy-start.242 = (bf16[768]{0:T(1024)(128)(2,1)}, bf16[768]{0:T(1024)(128)(2,1)S(1)}, u32[]{:S(2)}) copy-start(bf16[768]{0:T(1024)(128)(2,1)S(1)} %dynamic-update-slice.4) | copy-start | bytes 4612
  2027.1 373.9 %copy-start.241 = (bf16[768]{0:T(1024)(128)(2,1)S(1)}, bf16[768]{0:T(1024)(128)(2,1)}, u32[]{:S(2)}) copy-start(bf16[768]{0:T(1024)(128)(2,1)} %copy-done.240) | copy-start | bytes 4612
  2272.7 127.5 %copy-start.243 = (bf16[768]{0:T(1024)(128)(2,1)}, bf16[768]{0:T(1024)(128)(2,1)S(1)}, u32[]{:S(2)}) copy-start(bf16[768]{0:T(1024)(128)(2,1)S(1)} %dynamic-update-slice) | copy-start | bytes 4612
  (252 other events, 888.0 us)
Sparse Core Ops, SparseCore 0:
  60.8 37.2 all-reduce.28
  197.9 35.2 all-reduce.30
  392.7 69.9 all-reduce.36
  582.3 52.9 all-reduce.32
  693.2 52.7 all-reduce.34
  752.1 127.5 reduce-scatter.30
  885.6 149.4 reduce-scatter.28
  1041.4 170.0 reduce-scatter.32
  1218.6 169.8 reduce-scatter.34
  1393.0 120.5 reduce-scatter.42
  1519.0 120.7 reduce-scatter.44
  1644.2 120.7 reduce-scatter.46
  1770.4 120.7 reduce-scatter.50
  1895.8 123.6 reduce-scatter.48
  2024.0 120.5 reduce-scatter.36
  2149.8 120.6 reduce-scatter.38
  2275.2 123.4 reduce-scatter.40
  2401.9 55.4 all-gather.6
  2460.8 69.8 all-gather.4
  2533.9 78.9 all-gather.8
  2615.6 79.0 all-gather.10
where the time goes:
time: 2720 us; the launch traced here: 2710 us
  waiting for transfers between devices  1850 us (68%)
  matrix products  373 us (14%)
  other arithmetic  186 us (7%)
  local copies, waits for them, and re-layouts  151 us (6%)
  blocking collectives  121 us (4%)
    unnamed x29, waiting for transfers between devices  969 us
    reduce_scatter x1, waiting for transfers between devices, local(): lax.psum_scatter(grad_all[10][None], ('row', 'wide'), scatter_dimension=1...  175 us
    reduce_scatter x1, waiting for transfers between devices, local(): lax.psum_scatter(grad_all[8][None], ('row', 'wide'), scatter_dimension=1,...  175 us
    reduce_scatter x1, waiting for transfers between devices, local(): lax.psum_scatter(grad_all[2][None], ('row', 'wide'), scatter_dimension=1,...  154 us
    dot_general x12, matrix products, times_transposed(): lax.dot_general(left, right, (((1,), (1,)), ((), ())), preferred_element_...  99.5 us
    psum x3, waiting for transfers between devices, local(): lax.psum(part_state.astype(jnp.bfloat16), 'row').astype(jnp.float32)  95.9 us
    all_gather x1, waiting for transfers between devices, local(): lax.all_gather(parts[8].astype(jnp.bfloat16), ('row', 'wide'), axis=1, ti...  76.7 us
    unnamed x1, blocking collectives  75.3 us
  transfers between devices with their start and end apart: 25, of which 20 were waited for; matrix products, arithmetic and copies ran while one was open for 11% of the time, Pallas kernels for 0%

commit v1 on v0

v1 whole, which is shorter than its diff:
```python
from functools import partial
import math

import jax
import jax.numpy as jnp
from jax import lax
from jax.experimental import pallas as pl
from jax.experimental.pallas import tpu as pltpu
from jax.sharding import PartitionSpec as P

HEADS = 12
HEAD = 64
FEATS = 32
EPS = 1e-05
F32 = jnp.float32
BF = jnp.bfloat16
LANES = 128
GROUP = 4
GV = GROUP * HEAD
GF = GROUP * FEATS
FCHUNK = 512
COST = 30


def dot(a, b, dims=((1,), (0,))):
    return lax.dot_general(a, b, (dims, ((), ())), preferred_element_type=F32)


def dot_t(a, b):
    return dot(a, b, ((1,), (1,)))


def tdot(a, b):
    return dot(a, b, ((0,), (0,)))


def expanded(om):
    shape = (GV, GF)
    same = (
        lax.broadcasted_iota(jnp.int32, shape, 0) // HEAD
        == lax.broadcasted_iota(jnp.int32, shape, 1) // FEATS
    )
    return jnp.where(same, jnp.concatenate([om] * GROUP, axis=0), 0.0)


def crossing(sc, ids):
    return jnp.where((ids == sc[5]) & (sc[5] == sc[6]), 1.0, 0.0)


def split(v):
    high = v.astype(BF)
    return high, (v - high.astype(F32)).astype(BF)


def norm_parts(v):
    c = v - jnp.mean(v, axis=-1, keepdims=True)
    r = lax.rsqrt(jnp.mean(c * c, axis=-1, keepdims=True) + EPS)
    return c * r, r


def norm_back(d, xhat, r, gain):
    e = d * gain
    m1 = jnp.mean(e, axis=-1, keepdims=True)
    m2 = jnp.mean(e * xhat, axis=-1, keepdims=True)
    return (e - m1 - xhat * m2) * r


def gelu_parts(x):
    z = jnp.abs(x) * (1.0 / math.sqrt(2.0))
    ex = jnp.exp(-z * z)
    t = pl.reciprocal(1.0 + 0.3275911 * z, approx=True)
    p = 0.5 * 1.061405429
    for c in (-1.453152027, 1.421413741, -0.284496736, 0.254829592):
        p = p * t + 0.5 * c
    q = p * t * ex
    return jnp.where(x < 0, q, 1.0 - q), ex


def lane_is(shape, width, k):
    return lax.broadcasted_iota(jnp.int32, shape, 1) // width == k


def half_turn(a):
    low = lax.broadcasted_iota(jnp.int32, a.shape, 1) % HEAD < HEAD // 2
    return jnp.where(low, pltpu.roll(a, 96, 1), pltpu.roll(a, 32, 1))


def block_mask(dtype):
    shape = (GF, GV)
    same = (
        lax.broadcasted_iota(jnp.int32, shape, 0) // FEATS
        == lax.broadcasted_iota(jnp.int32, shape, 1) // HEAD
    )
    return same.astype(dtype)


def squeeze_state(st):
    st = st * block_mask(F32)
    return st[0:32] + st[32:64] + st[64:96] + st[96:128]


def widen_state(st):
    return jnp.concatenate([st] * GROUP, axis=0) * block_mask(st.dtype)


def pack_kernel(*refs):
    out, at = refs[-1], 0
    for ref in refs[:-1]:
        width = ref.shape[1]
        out[:, at : at + width] = ref[...]
        at += width


def pack(arrays):
    width = sum(a.shape[1] for a in arrays)
    return pl.pallas_call(
        pack_kernel,
        grid=(1,),
        in_specs=[pl.BlockSpec(a.shape, lambda i: (0, 0)) for a in arrays],
        out_specs=pl.BlockSpec((1, width), lambda i: (0, 0)),
        out_shape=jax.ShapeDtypeStruct((1, width), F32),
        compiler_params=params(),
        cost_estimate=pl.CostEstimate(flops=10**10, bytes_accessed=10**8, transcendentals=0),
        name="pack",
    )(*arrays)


def copies(own, other, mine, at, dst, sem):
    @pl.when(mine)
    def _():
        pltpu.make_async_copy(own.at[at], dst, sem).start()

    @pl.when(jnp.logical_not(mine))
    def _():
        pltpu.make_async_copy(other.at[at], dst, sem).start()


def arrived(own, at, dst, sem):
    pltpu.make_async_copy(own.at[at], dst, sem).wait()


ANY = pl.BlockSpec(memory_space=pl.ANY)


def params(mib=60):
    return pltpu.CompilerParams(vmem_limit_bytes=mib * 1024 * 1024)


def inputs_kernel(
    sc, x, gain, bias, w, w_other, bq, cos, sin, om, idc,
    normed, u, f, vals, st, ws, oma, sqm, sems, *, layer,
):
    j = pl.program_id(0)
    d = x.shape[2]
    at = lambda i: (slice(None), pl.ds(i * d, d))

    @pl.when(j == 0)
    def _():
        for i in range(3):
            copies(w, w_other, sc[0] == layer, at(i), ws.at[i], sems.at[i])
        xhat, _ = norm_parts(x[0].astype(F32))
        normed[...] = (xhat * gain[...] + bias[...]).astype(BF)
        hi, lo = split(expanded(om[...]))
        oma[:, :GF] = hi
        oma[:, GF:] = lo
        sqm[...] = expanded(jnp.full((HEAD, GF), -0.5, F32)).astype(BF)

    for i in range(3):

        @pl.when(j == i)
        def _():
            arrived(w, at(i), ws.at[i], sems.at[i])

    @pl.when(j < 2)
    def _():
        for g in range(HEADS // GROUP):
            cols = slice(g * GV, (g + 1) * GV)
            pr = dot(normed[...], ws[j, :, cols]) + bq[:, cols]
            parts = []
            for e in range(2):
                a = pr[:, e * LANES : (e + 1) * LANES]
                parts.append(a * cos[...] + half_turn(a) * sin[...])
            turned = jnp.concatenate(parts, axis=1)
            u[0, :, cols] = turned
            uh, ul = split(turned)
            sh, sl = split(turned * turned)
            ex = dot(uh, oma[...])
            ex = ex[:, :GF] + ex[:, GF:] + dot(ul, oma[:, :GF])
            ex = ex + dot(sh, sqm[...]) + dot(sl, sqm[...])
            f[0, :, g * GF : (g + 1) * GF] = (jnp.exp(ex) * (1.0 / math.sqrt(FEATS))).astype(BF)

    @pl.when(j == 2)
    def _():
        cross = crossing(sc, idc[...]).astype(BF)
        for g in range(HEADS // GROUP):
            cols = slice(g * GV, (g + 1) * GV)
            v = (dot(normed[...], ws[2, :, cols]) + bq[:, cols]).astype(BF)
            vals[:, cols] = v
            fk = f[0, :, g * GF : (g + 1) * GF] * cross
            one = jnp.ones_like(v)
            st[:, cols] = squeeze_state(tdot(fk, v)).astype(BF)
            st[:, d + g * GV : d + (g + 1) * GV] = squeeze_state(tdot(fk, one)).astype(BF)


UNIT = 768
G1, B1, BQ, BO, G2, B2, BU, BD = 0, 1, 2, 5, 6, 7, 8, 12


def vec_at(block):
    return pl.BlockSpec((1, UNIT), lambda j, s: (0, block))


def forward_inputs(layer, sc, x, vec, w, w_other, tables, om, idc, which):
    cos, sin = tables
    t, d = x.shape[1:]
    fw = HEADS * FEATS
    c2 = lambda j, s: (0, 0)
    part = lambda j, s: (jnp.minimum(j, 1), 0, 0)
    return pl.pallas_call(
        partial(inputs_kernel, layer=layer),
        out_shape=[
            jax.ShapeDtypeStruct((t, d), BF),
            jax.ShapeDtypeStruct((2, t, d), F32),
            jax.ShapeDtypeStruct((2, t, fw), BF),
            jax.ShapeDtypeStruct((t, d), BF),
            jax.ShapeDtypeStruct((FEATS, 2 * d), BF),
        ],
        grid_spec=pltpu.PrefetchScalarGridSpec(
            num_scalar_prefetch=1,
            grid=(3,),
            in_specs=[
                pl.BlockSpec((1, t, d), which),
                vec_at(G1),
                vec_at(B1),
                ANY,
                ANY,
                pl.BlockSpec((1, UNIT), lambda j, s: (0, BQ + j)),
                pl.BlockSpec((t, LANES), c2),
                pl.BlockSpec((t, LANES), c2),
                pl.BlockSpec((HEAD, GF), c2),
                pl.BlockSpec((t, 1), c2),
            ],
            out_specs=[
                pl.BlockSpec((t, d), c2),
                pl.BlockSpec((1, t, d), part),
                pl.BlockSpec((1, t, fw), part),
                pl.BlockSpec((t, d), c2),
                pl.BlockSpec((FEATS, 2 * d), c2),
            ],
            scratch_shapes=[
                pltpu.VMEM((3, d, d), BF),
                pltpu.VMEM((GV, GV), BF),
                pltpu.VMEM((GV, GF), BF),
                pltpu.SemaphoreType.DMA((3,)),
            ],
        ),
        compiler_params=params(),
        cost_estimate=pl.CostEstimate(
            flops=COST * 20 * t * d * d, bytes_accessed=COST * (16 * t * d + 6 * d * d), transcendentals=0
        ),
        name="attention_inputs",
    )(sc, x, vec, vec, w, w_other, vec, cos, sin, om, idc)


def own_half_kernel(fq, fk, vals, idc, idr, num, den):
    t = fq.shape[1]
    same = idc[...] == idr[...]
    zero = jnp.zeros((t, LANES), BF)
    q, k = fq[0], fk[0]
    for p in range(GROUP // 2):
        v = vals[:, p * LANES : (p + 1) * LANES]
        total = None
        for e in range(2):
            fh = jnp.where(lane_is((t, GF), FEATS, 2 * p + e), q, zero)
            s = jnp.where(same, dot_t(fh, k), 0.0).astype(BF)
            mine = lane_is((t, LANES), HEAD, e)
            va = jnp.concatenate(
                [jnp.where(mine, v, zero), jnp.where(mine, jnp.ones_like(v), zero)], axis=1
            )
            more = dot(s, va)
            total = more if total is None else total + more
        num[:, p * LANES : (p + 1) * LANES] = total[:, :LANES]
        den[:, p * LANES : (p + 1) * LANES] = total[:, LANES:]


def own_half(f, vals, ids):
    idc, idr = ids
    t, d = vals.shape
    c2 = lambda g: (0, 0)
    col = lambda g: (0, g)
    return pl.pallas_call(
        own_half_kernel,
        grid=(HEADS // GROUP,),
        out_shape=[jax.ShapeDtypeStruct((t, d), F32)] * 2,
        in_specs=[
            pl.BlockSpec((1, t, GF), lambda g: (0, 0, g)),
            pl.BlockSpec((1, t, GF), lambda g: (1, 0, g)),
            pl.BlockSpec((t, GV), col),
            pl.BlockSpec((t, 1), c2),
            pl.BlockSpec((1, t), c2),
        ],
        out_specs=[pl.BlockSpec((t, GV), col)] * 2,
        compiler_params=params(),
        cost_estimate=pl.CostEstimate(flops=COST * (16 * t * t * d), bytes_accessed=COST * (12 * t * d), transcendentals=0),
        name="own_half",
    )(f, f, vals, idc, idr)


def outputs_kernel(
    sc, num, den, f, x, st, idc, bo, g2, b2, bu, bd, wo, wu, wd, wo_r, wu_r, wd_r,
    att, rden, mid, n2, act, gp, res, acc, ups, ups_too, wos, wus, wds, sems, *, layer,
):
    j = pl.program_id(0)
    steps = wus.shape[0]
    t, d = x.shape[1:]
    full = (slice(None), slice(None))
    up_at = lambda c: (slice(None), pl.ds(c * FCHUNK, FCHUNK))
    down_at = lambda c: (pl.ds(c * FCHUNK, FCHUNK), slice(None))

    @pl.when(j == 0)
    def _():
        copies(wo, wo_r, sc[0] == layer, full, wos, sems.at[0])
        for c in range(steps):
            copies(wu, wu_r, sc[0] == layer, up_at(c), wus.at[c], sems.at[1 + c])
            copies(wd, wd_r, sc[0] == layer, down_at(c), wds.at[c], sems.at[1 + steps + c])
        cross = crossing(sc, idc[...]).astype(BF)
        for g in range(HEADS // GROUP):
            cols = slice(g * GV, (g + 1) * GV)
            fqc = f[0, :, g * GF : (g + 1) * GF] * cross
            n = num[:, cols] + dot(fqc, widen_state(st[:, cols]))
            m = den[:, cols] + dot(fqc, widen_state(st[:, d + g * GV : d + (g + 1) * GV]))
            rd = 1.0 / m
            rden[:, cols] = rd
            att[:, cols] = (n * rd).astype(BF)
        arrived(wo, full, wos, sems.at[0])
        m = x[0].astype(F32) + dot(att[...], wos[...]) + bo[...]
        mid[...] = m
        xhat, _ = norm_parts(m)
        n2[...] = (xhat * g2[...] + b2[...]).astype(BF)
        acc[...] = m + bd[...]

    for c in range(steps):

        @pl.when(j == c)
        def _():
            arrived(wu, up_at(c), wus.at[c], sems.at[1 + c])

        @pl.when(j == c + 1)
        def _():
            arrived(wd, down_at(c), wds.at[c], sems.at[1 + steps + c])

    def product(into):
        into[...] = dot(n2[...], wus[jnp.minimum(j, steps - 1)]) + bu[...]

    def rest(ref):
        up = ref[...]
        phi, ex = gelu_parts(up)
        a = (up * phi).astype(BF)
        act[0] = a
        gp[...] = (phi + up * ex * (1.0 / math.sqrt(2.0 * math.pi))).astype(BF)
        acc[...] += dot(a, wds[jnp.maximum(j - 1, 0)])

    @pl.when(j == 0)
    def _():
        product(ups)

    @pl.when((j > 0) & (j < steps) & (j % 2 == 1))
    def _():
        product(ups_too)
        rest(ups)

    @pl.when((j > 0) & (j < steps) & (j % 2 == 0))
    def _():
        product(ups)
        rest(ups_too)

    @pl.when(j == steps)
    def _():
        rest(ups if steps % 2 == 1 else ups_too)
        res[...] = acc[...].astype(BF)


def forward_outputs(layer, sc, num, den, f, x, st, idc, vec, wts, which):
    wo, wu, wd = wts[:3]
    t, d = x.shape[1:]
    ff = wu.shape[1]
    steps = ff // FCHUNK
    c2 = lambda j, s: (0, 0)
    col = lambda j, s: (0, jnp.maximum(j - 1, 0))
    half_at = lambda j, s: (jnp.maximum(j - 1, 0) // (steps // 2), 0, jnp.maximum(j - 1, 0) % (steps // 2))
    ahead = BU * UNIT // FCHUNK
    return pl.pallas_call(
        partial(outputs_kernel, layer=layer),
        out_shape=[
            jax.ShapeDtypeStruct((t, d), BF),
            jax.ShapeDtypeStruct((t, d), F32),
            jax.ShapeDtypeStruct((t, d), F32),
            jax.ShapeDtypeStruct((t, d), BF),
            jax.ShapeDtypeStruct((2, t, ff // 2), BF),
            jax.ShapeDtypeStruct((t, ff), BF),
            jax.ShapeDtypeStruct((t, d), BF),
        ],
        grid_spec=pltpu.PrefetchScalarGridSpec(
            num_scalar_prefetch=1,
            grid=(steps + 1,),
            in_specs=[
                pl.BlockSpec((t, d), c2),
                pl.BlockSpec((t, d), c2),
                pl.BlockSpec((1, t, HEADS * FEATS), lambda j, s: (0, 0, 0)),
                pl.BlockSpec((1, t, d), which),
                pl.BlockSpec((FEATS, 2 * d), c2),
                pl.BlockSpec((t, 1), c2),
                vec_at(BO),
                vec_at(G2),
                vec_at(B2),
                pl.BlockSpec((1, FCHUNK), lambda j, s: (0, ahead + jnp.minimum(j, steps - 1))),
                vec_at(BD),
            ]
            + [ANY] * 6,
            out_specs=[
                pl.BlockSpec((t, d), c2),
                pl.BlockSpec((t, d), c2),
                pl.BlockSpec((t, d), c2),
                pl.BlockSpec((t, d), c2),
                pl.BlockSpec((1, t, FCHUNK), half_at),
                pl.BlockSpec((t, FCHUNK), col),
                pl.BlockSpec((t, d), c2),
            ],
            scratch_shapes=[
                pltpu.VMEM((t, d), F32),
                pltpu.VMEM((t, FCHUNK), F32),
                pltpu.VMEM((t, FCHUNK), F32),
                pltpu.VMEM((d, d), BF),
                pltpu.VMEM((steps, d, FCHUNK), BF),
                pltpu.VMEM((steps, FCHUNK, d), BF),
                pltpu.SemaphoreType.DMA((1 + 2 * steps,)),
            ],
        ),
        compiler_params=params(),
        cost_estimate=pl.CostEstimate(
            flops=COST * (4 * t * d * ff + 2 * t * d * d), bytes_accessed=COST * (4 * d * ff + 40 * t * d), transcendentals=0
        ),
        name="attention_out_and_ffn",
    )(sc, num, den, f, x, st, idc, vec, vec, vec, vec, vec, *wts)


def ffn_back_kernel(
    sc, g, gp, mid, g2, att, rden, f, idc, wd, wu, wo, wd_r, wu_r, wo_r,
    d_up, d_mid, d_br, d_num, d_den, dst, s_bd, s_bu, s_g2, s_b2, s_bo,
    acc, wos, wus, wds, sems, *, layer,
):
    j = pl.program_id(0)
    steps = wus.shape[0]
    t, d = g.shape[1:]
    full = (slice(None), slice(None))
    up_at = lambda c: (slice(None), pl.ds(c * FCHUNK, FCHUNK))
    down_at = lambda c: (pl.ds(c * FCHUNK, FCHUNK), slice(None))

    @pl.when(j == 0)
    def _():
        for c in range(steps):
            copies(wd, wd_r, sc[0] == layer, down_at(c), wds.at[c], sems.at[1 + steps + c])
            copies(wu, wu_r, sc[0] == layer, up_at(c), wus.at[c], sems.at[1 + c])
        copies(wo, wo_r, sc[0] == layer, full, wos, sems.at[0])
        acc[...] = jnp.zeros_like(acc)
        s_bd[...] = jnp.sum(g[0].astype(F32), axis=0, keepdims=True)

    for c in range(steps):

        @pl.when(j == c)
        def _():
            arrived(wu, up_at(c), wus.at[c], sems.at[1 + c])
            arrived(wd, down_at(c), wds.at[c], sems.at[1 + steps + c])

    d_act = dot_t(g[0], wds[j])
    up = (d_act * gp[...].astype(F32)).astype(BF)
    d_up[...] = up
    s_bu[...] = jnp.sum(up.astype(F32), axis=0, keepdims=True)
    acc[...] += dot_t(up, wus[j])

    @pl.when(j == pl.num_programs(0) - 1)
    def _():
        arrived(wo, full, wos, sems.at[0])
        shape = (GV, GV)
        ones = (
            lax.broadcasted_iota(jnp.int32, shape, 0) // HEAD
            == lax.broadcasted_iota(jnp.int32, shape, 1) // HEAD
        ).astype(BF)
        dn2 = acc[...]
        xhat, r = norm_parts(mid[...])
        dm = g[0].astype(F32) + norm_back(dn2, xhat, r, g2[...])
        s_g2[...] = jnp.sum(dn2 * xhat, axis=0, keepdims=True)
        s_b2[...] = jnp.sum(dn2, axis=0, keepdims=True)
        d_mid[...] = dm
        db = dm.astype(BF)
        d_br[...] = db
        s_bo[...] = jnp.sum(db.astype(F32), axis=0, keepdims=True)
        cr = crossing(sc, idc[...]).astype(BF)
        for k in range(HEADS // GROUP):
            cols = slice(k * GV, (k + 1) * GV)
            da = dot_t(db, wos[cols, :]) * rden[:, cols]
            dnb = da.astype(BF)
            d_num[:, cols] = dnb
            hi, lo = split(da * att[:, cols].astype(F32))
            ddb = (-(dot(hi, ones) + dot(lo, ones))).astype(BF)
            d_den[:, cols] = ddb
            fq = f[0, :, k * GF : (k + 1) * GF] * cr
            dst[:, cols] = squeeze_state(tdot(fq, dnb)).astype(BF)
            dst[:, d + k * GV : d + (k + 1) * GV] = squeeze_state(tdot(fq, ddb)).astype(BF)


def ffn_back(layer, sc, g, gp, mid, vec, att, rden, f, idc, wts, which):
    wu = wts[1]
    t, d = g.shape[1:]
    ff = wu.shape[1]
    steps = ff // FCHUNK
    c2 = lambda j, s: (0, 0)
    col = lambda j, s: (0, j)
    line_shape = jax.ShapeDtypeStruct((1, d), F32)
    wide = jax.ShapeDtypeStruct((t, d), BF)
    tile = pl.BlockSpec((t, d), c2)
    line = pl.BlockSpec((1, d), c2)
    return pl.pallas_call(
        partial(ffn_back_kernel, layer=layer),
        out_shape=[
            jax.ShapeDtypeStruct((t, ff), BF),
            jax.ShapeDtypeStruct((t, d), F32),
            wide,
            wide,
            wide,
            jax.ShapeDtypeStruct((FEATS, 2 * d), BF),
            line_shape,
            jax.ShapeDtypeStruct((1, ff), F32),
            line_shape,
            line_shape,
            line_shape,
        ],
        grid_spec=pltpu.PrefetchScalarGridSpec(
            num_scalar_prefetch=1,
            grid=(steps,),
            in_specs=[
                pl.BlockSpec((1, t, d), which),
                pl.BlockSpec((t, FCHUNK), col),
                tile,
                vec_at(G2),
                tile,
                tile,
                pl.BlockSpec((1, t, HEADS * FEATS), lambda j, s: (0, 0, 0)),
                pl.BlockSpec((t, 1), c2),
            ]
            + [ANY] * 6,
            out_specs=[
                pl.BlockSpec((t, FCHUNK), col),
                tile,
                tile,
                tile,
                tile,
                pl.BlockSpec((FEATS, 2 * d), c2),
                line,
                pl.BlockSpec((1, FCHUNK), col),
                line,
                line,
                line,
            ],
            scratch_shapes=[
                pltpu.VMEM((t, d), F32),
                pltpu.VMEM((d, d), BF),
                pltpu.VMEM((steps, d, FCHUNK), BF),
                pltpu.VMEM((steps, FCHUNK, d), BF),
                pltpu.SemaphoreType.DMA((1 + 2 * steps,)),
            ],
        ),
        compiler_params=params(),
        cost_estimate=pl.CostEstimate(
            flops=COST * (4 * t * d * ff + 4 * t * d * d), bytes_accessed=COST * (4 * d * ff + 40 * t * d), transcendentals=0
        ),
        name="ffn_back",
    )(sc, g, gp, mid, vec, att, rden, f, idc, *wts)


def attention_back_kernel(
    sc, f, vals, d_num, d_den, u, st, dst, idc, idr, cos, sin, om, *rest, layer
):
    t, d = vals.shape
    both_parts = len(rest) > 2
    if both_parts:
        x, gain, d_mid, w, w_other, d_proj, s_bq, d_in, s_g1, s_b1, ws, sems = rest
        fetch_weights(sc[0] == layer, w, w_other, ws, sems)
    else:
        d_proj, s_bq = rest
    hi, lo = split(expanded(om[...]))
    ones = expanded(jnp.ones((HEAD, GF), F32)).astype(BF)
    cross = crossing(sc, idc[...])
    same = idc[...] == idr[...]
    cr = cross.astype(BF)
    head_lane = lax.broadcasted_iota(jnp.int32, (t, GV), 1) % HEAD == 0
    one_lane = jnp.where(head_lane, cross, 0.0).astype(BF)

    hi_hi = jnp.concatenate([hi, hi], axis=1)
    one_one = jnp.concatenate([ones, ones], axis=1)

    for k in range(HEADS // GROUP):
        cols = slice(k * GV, (k + 1) * GV)
        tail = slice(d + k * GV, d + (k + 1) * GV)
        fcols = slice(k * GF, (k + 1) * GF)
        fq, fk = f[0, :, fcols], f[1, :, fcols]
        zf = jnp.zeros_like(fq)
        vg, dn, dd = vals[:, cols], d_num[:, cols], d_den[:, cols]
        dd1 = jnp.where(head_lane, dd, jnp.zeros_like(dd))
        state, tots = widen_state(st[:, cols]), widen_state(st[:, tail])
        d_state, d_tots = widen_state(dst[:, cols]), widen_state(dst[:, tail])
        dfq = dot_t(dn * cr, state) + dot_t(dd1 * cr, tots)
        dfk = dot_t(vg * cr, d_state) + dot_t(one_lane, d_tots)
        dv = dot(fk * cr, d_state)
        dvs = []
        for p in range(GROUP // 2):
            own = slice(p * LANES, (p + 1) * LANES)
            v1 = jnp.concatenate([vg[:, own], jnp.ones((t, LANES), BF)], axis=1)
            dvp = dv[:, own]
            for e in range(2):
                feat_lane = lane_is((t, GF), FEATS, 2 * p + e)
                mine = lane_is((t, LANES), HEAD, e)
                zero = jnp.zeros((t, LANES), BF)
                fqh, fkh = jnp.where(feat_lane, fq, zf), jnp.where(feat_lane, fk, zf)
                dnh = jnp.where(mine, dn[:, own], zero)
                ah = jnp.concatenate([dnh, jnp.where(mine, dd1[:, own], zero)], axis=1)
                pt = jnp.where(same, dot_t(ah, v1), 0.0).astype(BF)
                dfq = dfq + dot(pt, fkh)
                dfk = dfk + tdot(pt, fqh)
                pt = jnp.where(same, dot_t(fkh, fq), 0.0).astype(BF)
                dvp = dvp + dot(pt, dnh)
            dvs.append(dvp)
        parts = [jnp.concatenate(dvs, axis=1).astype(BF)]
        for q, (df, ft) in enumerate(((dfq, fq), (dfk, fk))):
            dz = df * ft.astype(F32)
            zh, zl = split(dz)
            both = jnp.concatenate([zh, zl], axis=1)
            du = dot_t(both, hi_hi) + dot_t(zh, lo) - u[q, :, cols] * dot_t(both, one_one)
            for e in range(2):
                a = du[:, e * LANES : (e + 1) * LANES]
                parts.append((a * cos[...] - half_turn(a) * sin[...]).astype(BF))
        for at, part in ((2 * d, parts[0]), (0, jnp.concatenate(parts[1:3], axis=1)), (d, jnp.concatenate(parts[3:], axis=1))):
            here = slice(at + k * GV, at + (k + 1) * GV)
            d_proj[:, here] = part
            s_bq[:, here] = jnp.sum(part.astype(F32), axis=0, keepdims=True)

    if both_parts:
        finish_inputs(d_proj, x, gain, d_mid, w, d_in, s_g1, s_b1, ws, sems)


def third(i, d):
    return (slice(None), pl.ds(i * d, d))


def fetch_weights(mine, w, w_other, ws, sems):
    for i in range(3):
        copies(w, w_other, mine, third(i, ws.shape[1]), ws.at[i], sems.at[i])


def finish_inputs(d_proj, x, gain, d_mid, w, d_in, s_g1, s_b1, ws, sems):
    d = ws.shape[1]
    dn1 = None
    for i in range(3):
        arrived(w, third(i, d), ws.at[i], sems.at[i])
        part = dot_t(d_proj[:, i * d : (i + 1) * d], ws[i])
        dn1 = part if dn1 is None else dn1 + part
    xhat, r = norm_parts(x[0].astype(F32))
    d_in[...] = (d_mid[...] + norm_back(dn1, xhat, r, gain[...])).astype(BF)
    s_g1[...] = jnp.sum(dn1 * xhat, axis=0, keepdims=True)
    s_b1[...] = jnp.sum(dn1, axis=0, keepdims=True)


def inputs_back_kernel(sc, d_proj, x, gain, d_mid, w, w_other, d_in, s_g1, s_b1, ws, sems, *, layer):
    fetch_weights(sc[0] == layer, w, w_other, ws, sems)
    finish_inputs(d_proj, x, gain, d_mid, w, d_in, s_g1, s_b1, ws, sems)


def whole(a):
    return pl.BlockSpec(a.shape, lambda j, s: (0,) * len(a.shape))


def input_specs(d_mid, which):
    t, d = d_mid.shape
    shapes = [
        jax.ShapeDtypeStruct((t, d), BF),
        jax.ShapeDtypeStruct((1, d), F32),
        jax.ShapeDtypeStruct((1, d), F32),
    ]
    specs = [pl.BlockSpec((1, t, d), which), vec_at(G1), whole(d_mid), ANY, ANY]
    return shapes, specs, [pltpu.VMEM((3, d, d), BF), pltpu.SemaphoreType.DMA((3,))]


def attention_back(layer, sc, f, vals, d_num, d_den, u, st, dst, ids, tables, om, inputs):
    t, d = vals.shape
    operands = [f, vals, d_num, d_den, u, st, dst, *ids, *tables, om]
    specs = [whole(a) for a in operands]
    shapes = [jax.ShapeDtypeStruct((t, 3 * d), BF), jax.ShapeDtypeStruct((1, 3 * d), F32)]
    scratch = []
    if inputs is not None:
        x, vec, d_mid, w, w_other, which = inputs
        more, more_specs, scratch = input_specs(d_mid, which)
        operands += [x, vec, d_mid, w, w_other]
        specs += more_specs
        shapes += more
    return pl.pallas_call(
        partial(attention_back_kernel, layer=layer),
        out_shape=shapes,
        grid_spec=pltpu.PrefetchScalarGridSpec(
            num_scalar_prefetch=1,
            grid=(1,),
            in_specs=specs,
            out_specs=[whole(a) for a in shapes],
            scratch_shapes=scratch,
        ),
        compiler_params=params(),
        cost_estimate=pl.CostEstimate(
            flops=COST * 48 * t * t * d, bytes_accessed=COST * 40 * t * d, transcendentals=0
        ),
        name="attention_back",
    )(sc, *operands)


def inputs_back(layer, sc, d_proj, x, vec, d_mid, w, w_other, which):
    t, d = d_mid.shape
    shapes, specs, scratch = input_specs(d_mid, which)
    return pl.pallas_call(
        partial(inputs_back_kernel, layer=layer),
        out_shape=shapes,
        grid_spec=pltpu.PrefetchScalarGridSpec(
            num_scalar_prefetch=1,
            grid=(1,),
            in_specs=[whole(d_proj)] + specs,
            out_specs=[whole(a) for a in shapes],
            scratch_shapes=scratch,
        ),
        compiler_params=params(),
        cost_estimate=pl.CostEstimate(
            flops=COST * 6 * t * d * d, bytes_accessed=COST * 16 * t * d, transcendentals=0
        ),
        name="inputs_back",
    )(sc, d_proj, x, vec, d_mid, w, w_other)


ROWS = UNIT // 2


def weight_grad_kernel(sc, *refs, sizes, dims):
    send, keep = refs[-2:]
    at = 0
    for m, size in enumerate(sizes):
        left, left_r, right, right_r = refs[4 * m : 4 * m + 4]

        @pl.when((pl.program_id(0) >= at) & (pl.program_id(0) < at + size))
        def _():
            total = tdot(left[0], right[0]) + tdot(left_r[0], right_r[0])
            low, high = total[:, :ROWS].astype(BF), total[:, ROWS:].astype(BF)

            @pl.when(bit_of(sc, dims) == 0)
            def _():
                keep[0] = low
                send[0] = high

            @pl.when(bit_of(sc, dims) == 1)
            def _():
                keep[0] = high
                send[0] = low

        at += size


def weight_grad(sc, members, dims):
    sizes = [m[-1] for m in members]
    operands, specs, at = [], [], 0
    for left, lp, left_r, lrp, right, rp, right_r, rrp, size in members:
        t = left.shape[1]
        here = lambda i, at=at, size=size: jnp.clip(i - at, 0, size - 1)
        operands += [left, left_r, right, right_r]
        specs += [
            pl.BlockSpec((1, t, ROWS), lambda i, s, f=lp, h=here: f(h(i), s[0])),
            pl.BlockSpec((1, t, ROWS), lambda i, s, f=lrp, h=here: f(h(i), s[0])),
            pl.BlockSpec((1, t, UNIT), lambda i, s, f=rp, h=here: f(h(i), s[0])),
            pl.BlockSpec((1, t, UNIT), lambda i, s, f=rrp, h=here: f(h(i), s[0])),
        ]
        at += size
    shape = jax.ShapeDtypeStruct((at, ROWS, ROWS), BF)
    spec = pl.BlockSpec((1, ROWS, ROWS), lambda i, s: (i, 0, 0))
    return pl.pallas_call(
        partial(weight_grad_kernel, sizes=sizes, dims=dims),
        out_shape=[shape, shape],
        grid_spec=pltpu.PrefetchScalarGridSpec(
            num_scalar_prefetch=1, grid=(at,), in_specs=specs, out_specs=[spec, spec]
        ),
        compiler_params=params(),
        cost_estimate=pl.CostEstimate(
            flops=COST * 2 * at * t * UNIT * UNIT, bytes_accessed=COST * at * 4 * t * UNIT, transcendentals=0
        ),
        name="weight_grad",
    )(sc, *operands)


def chip_bits():
    wide, row = lax.axis_index("wide"), lax.axis_index("row")
    return {"x": wide % 2, "y": row, "z0": wide // 2 % 2, "z1": wide // 4}


def bit_of(sc, dims):
    if dims is None:
        return 0
    at = [1 + ("x", "y", "z0", "z1").index(d) for d in dims]
    return jnp.where(sc[0] == 0, sc[at[0]], sc[at[1]])


class Links:
    def __init__(self):
        self.section = lax.axis_index("section")
        self.bits = chip_bits()

    def bit(self, dims):
        return jnp.where(self.section == 0, self.bits[dims[0]], self.bits[dims[1]])

    def swap(self, value, dims):
        flips = {"x": (0, 1), "y": (1, 0), "z0": (0, 2), "z1": (0, 4)}
        pairs = []
        for s in range(2):
            fr, fw = flips[dims[s]]
            for r in range(2):
                for w in range(8):
                    pairs.append(((s * 2 + r) * 8 + w, (s * 2 + (r ^ fr)) * 8 + (w ^ fw)))
        return lax.ppermute(value, ("section", "row", "wide"), pairs)


AXES = {"x": "x", "y": "y", "z": "z0", "w": "z1"}


def pick(parts, bit):
    total = None
    for p in parts:
        one = lax.dynamic_index_in_dim(p, bit, 0, keepdims=False).astype(F32)
        total = one if total is None else total + one
    return total.astype(BF)


def add(parts):
    return parts[0] + parts[1]


def join(own, other, bit):
    return jnp.stack([jnp.where(bit == 0, own, other), jnp.where(bit == 0, other, own)])


def fence_kernel(token, out):
    pass


def fence(token, values):
    (token,) = after([token], values)
    return pl.pallas_call(
        fence_kernel,
        out_shape=jax.ShapeDtypeStruct(token.shape, token.dtype),
        in_specs=[pl.BlockSpec(memory_space=pl.ANY)],
        out_specs=pl.BlockSpec(memory_space=pl.ANY),
        input_output_aliases={0: 0},
        compiler_params=params(1),
        cost_estimate=pl.CostEstimate(flops=10**12, bytes_accessed=10**9, transcendentals=0),
        name="fence",
    )(token)


def scattered_sum(value):
    part = lax.psum_scatter(value, ("row", "wide"), scatter_dimension=0, tiled=True)
    return lax.all_gather(part, ("row", "wide"), axis=0, tiled=True)


def after(values, others):
    values, others = list(values), list(others)
    if not others:
        return values
    return list(lax.optimization_barrier(tuple(values + others)))[: len(values)]


SWAP = [(0, 1), (1, 0)]


class Flow:
    def __init__(self, links, kinds, owner):
        self.links, self.owner = links, owner
        self.step = 0
        self.order = None if links is None else [tuple(AXES[a] for a in dims) for dims in zip(*kinds)]

    def first_dims(self):
        return None if self.links is None else self.order[0]

    def begin(self, send, keep):
        self.shape = send.shape
        self.parts = keep
        if self.links is None:
            self.flight = send
        else:
            self.flight = self.links.swap(send, self.order[0])

    def advance(self, others=()):
        (came,) = after([self.flight], others)
        self.step += 1
        step = self.step
        if self.links is None:
            return self.plain(came)
        if step == 6:
            self.flight = self.over(came)
            self.mine = (self.parts, came)
            return [came]
        if step == 7:
            (early,) = after([self.early], others)
            self.result = (*self.mine, early, came)
            return [came, early]
        if step == 1:
            shape = (2, self.shape[0] * self.shape[1] // 2, self.shape[2])
            self.parts = [self.parts.reshape(shape), came.reshape(shape)]
            dims = self.order[1]
            send = pick(self.parts, 1 - self.links.bit(dims))
        elif step == 2:
            dims = self.order[2]
            send = self.parts = add([pick(self.parts, self.links.bit(self.order[1])), came])
        elif step == 3:
            dims = self.order[3]
            send = self.parts = add([self.parts, came])
        elif step == 4:
            dims = self.order[1]
            send = self.parts = add([self.parts, came])
        else:
            dims = self.order[0]
            send = self.parts = join(self.parts, came, self.links.bit(self.order[1])).reshape(self.shape)
        self.flight = self.links.swap(send, dims)
        if step == 5:
            self.early = self.over(send)
        return [send]

    def over(self, value):
        return lax.ppermute(value, "section", [(1 - self.owner, self.owner)])

    def plain(self, came):
        total = jnp.concatenate([self.parts, came], axis=0)
        mine = scattered_sum(total.reshape(-1, ROWS)).reshape((2,) + self.shape)
        self.result = (mine[0], mine[1], self.over(mine[0]), self.over(mine[1]))
        return []


def finish_kernel(sc, *refs, by_row, dims):
    out = refs[-1]
    for layer in range(2):
        for side in range(2):
            half = layer if side == 0 else 1 - layer
            base = 0 if by_row else half * ROWS
            ends = dims[layer] if side == 0 or dims[layer] is None else dims[layer][::-1]
            for bit in range(2):
                here = (sc[0] == layer) & (bit_of(sc, ends) == bit)
                if by_row:
                    here = here & (pl.program_id(1) == half)

                @pl.when(here)
                def _():
                    at = 4 * layer + 2 * side
                    out[base : base + ROWS, :ROWS] = refs[at + bit][0].astype(F32)
                    out[base : base + ROWS, ROWS:] = refs[at + 1 - bit][0].astype(F32)


def finish(sc, first, second, start, units, by_row, dims):
    spec = lambda layer: pl.BlockSpec(
        (1, ROWS, ROWS), lambda u, h, s: (start + jnp.where(s[0] == layer, u, 0), 0, 0)
    )
    if by_row:
        shape, grid = (2 * units * ROWS, UNIT), (units, 2)
        out = pl.BlockSpec((ROWS, UNIT), lambda u, h, s: (h * units + u, 0))
    else:
        shape, grid = (UNIT, units * UNIT), (units, 1)
        out = pl.BlockSpec((UNIT, UNIT), lambda u, h, s: (0, u))
    return pl.pallas_call(
        partial(finish_kernel, by_row=by_row, dims=dims),
        out_shape=jax.ShapeDtypeStruct(shape, F32),
        grid_spec=pltpu.PrefetchScalarGridSpec(
            num_scalar_prefetch=1,
            grid=grid,
            in_specs=[spec(0)] * 4 + [spec(1)] * 4,
            out_specs=out,
        ),
        compiler_params=params(),
        cost_estimate=pl.CostEstimate(
            flops=COST * units * UNIT * UNIT, bytes_accessed=COST * units * 8 * UNIT * UNIT, transcendentals=0
        ),
        name="finish",
    )(sc, *first, *second)[None]


def local(
    inputs, cotangent, segment_ids, step_number, redraw_every, bank_offset,
    ln1_gain, ln1_bias, w_qkv, b_qkv, w_out, b_out, ln2_gain, ln2_bias,
    w_up, b_up, w_down, b_down, bank,
):
    section = lax.axis_index("section")
    row = lax.axis_index("row")
    first = section == 0
    t, d = inputs.shape[1:]
    ff = w_up.shape[2]
    swap = [(0, 1), (1, 0)]

    def both(own):
        other = lax.ppermute(own, "section", swap)
        return own, other

    w_qkv, w_qkv_r = both(w_qkv[0])
    chosen = (bank_offset[0] + step_number[0] // redraw_every[0]) % bank.shape[1]
    omega = lax.dynamic_index_in_dim(bank[0], chosen, 0, keepdims=False)
    vectors = pack([ln1_gain, ln1_bias, b_qkv, b_out, ln2_gain, ln2_bias, b_up, b_down])
    vectors_r = lax.ppermute(vectors, "section", swap)
    omega, omega_r = both(jnp.concatenate([omega] * GROUP, axis=1))
    w_out, w_out_r = both(w_out[0])
    w_up, w_up_r = both(w_up[0])
    w_down, w_down_r = both(w_down[0])

    lane = lax.broadcasted_iota(jnp.int32, (t, LANES), 1) % HEAD
    place = (row * t + lax.broadcasted_iota(jnp.int32, (t, LANES), 0)).astype(F32)
    angles = place * (10000.0 ** (-2.0 * (lane % (HEAD // 2)).astype(F32) / HEAD))
    scale = HEAD ** (-0.25)
    tables = (jnp.cos(angles) * scale, jnp.sin(angles) * jnp.where(lane < HEAD // 2, -scale, scale))

    own_ids = lax.dynamic_slice(segment_ids, (section, row * t), (1, t))
    edge = lax.dynamic_slice(segment_ids, (section, jnp.int32(t - 1)), (1, 2))[0]
    ids = (own_ids.reshape(t, 1), own_ids)
    other_row = [(i, i ^ 1) for i in range(2)]
    by_section = lambda j, s: (s[0], 0, 0)
    only = lambda j, s: (0, 0, 0)

    sc = jnp.concatenate([jnp.stack([section, *chip_bits().values()]), edge]).astype(jnp.int32)
    saved, given = [], []
    x, which = inputs, by_section
    for layer in range(2):
        mine = section == layer
        vec = jnp.where(mine, vectors, vectors_r)
        om = jnp.where(mine, omega, omega_r)
        normed, u, f, vals, st = forward_inputs(layer, sc, x, vec, w_qkv, w_qkv_r, tables, om, ids[0], which)
        st = lax.ppermute(st, "row", other_row)
        num, den = own_half(f, vals, ids)
        att, rden, mid, n2, act, gp, res = forward_outputs(
            layer, sc, num, den, f, x, st, ids[0], vec, (w_out, w_up, w_down, w_out_r, w_up_r, w_down_r), which
        )
        saved.append((sc, x, vec, om, which, normed, u, f, vals, st, att, rden, mid, n2, act, gp))
        x, which = res[None], only
        given.append([lax.ppermute(g, "section", swap) for g in (n2, att, normed, act)])
    outs = (saved[1][1][0], x[0])

    def to_owner(of_layer):
        mine = jnp.where(first, of_layer[0], of_layer[1])
        other = lax.ppermute(jnp.where(first, of_layer[1], of_layer[0]), "section", swap)
        return join(mine, other, section)[None]

    hidden = to_owner(outs)

    links = Links() if lax.axis_size("wide") == 8 else None
    flows = {
        name + str(layer): Flow(links, KINDS[name + str(layer)], layer)
        for layer in range(2)
        for name in "duq"
    }
    at_own = lambda i, s: (s, 0, 0)
    at_other = lambda i, s: (1 - s, 0, 0)
    at_first = lambda i, s: (0, 0, 0)
    at_unit = lambda i, s: (0, 0, i)
    grads = {1: (cotangent, at_own, cotangent, at_other)}
    parts, back, done = {}, {}, {}
    shown = []

    def tied(value):
        (value,) = after([value], shown)
        shown.clear()
        return value

    def members(name):
        layer = int(name[1])
        normed, att, n2, act = (saved[layer][i] for i in (5, 10, 13, 14))
        gave_n2, gave_att, gave_normed, gave_act = given[layer]
        if name[0] == "d":
            left = (act, lambda i, s: (s, 0, i), gave_act, lambda i, s: (s, 0, i))
            return [(*left, *grads[layer], ff // UNIT)]

        def one(own, other, right, units):
            return (
                own[None], lambda i, s: (0, 0, s), other[None], lambda i, s: (0, 0, s),
                right[0][None], at_unit, right[1][None], at_unit, units,
            )

        if name[0] == "u":
            return [
                one(n2, gave_n2, done["up", layer], ff // UNIT),
                one(att, gave_att, done["br", layer], 1),
            ]
        return [one(normed, gave_normed, done["proj", layer], 3)]

    def run(item):
        name, layer = item[:2], int(item[1])
        if name in flows and len(item) == 2:
            before = list(shown)
            shown.clear()
            shown.extend(flows[name].advance(before))
        elif name in flows:
            send, keep = weight_grad(tied(sc), members(name), flows[name].first_dims())
            shown.append(send)
            flows[name].begin(send, keep)
        elif name[0] == "f":
            _, x, vec, om, which, normed, u, f, vals, st, att, rden, mid, n2, act, gp = saved[layer]
            g = grads[layer][0]
            back[layer] = ffn_back(
                layer, sc, g, tied(gp), mid, vec, att, rden, f, ids[0],
                (w_down, w_up, w_out, w_down_r, w_up_r, w_out_r),
                by_section if layer == 1 else only,
            )
            shown.append(back[layer][0])
            done["dst", layer] = lax.ppermute(back[layer][5], "row", other_row)
            done["up", layer] = both(back[layer][0])
            done["br", layer] = both(back[layer][2])
        elif name[0] == "a":
            _, x, vec, om, which, normed, u, f, vals, st = saved[layer][:10]
            d_mid, _, d_num, d_den = back[layer][1:5]
            out = attention_back(
                layer, sc, f, vals, tied(d_num), d_den, u, st, done["dst", layer], ids, tables, om,
                (x, vec, d_mid, w_qkv, w_qkv_r, which) if layer == 1 else None,
            )
            shown.append(out[0])
            done["proj", layer] = both(out[0])
            parts[layer] = out[1]
            if layer == 1:
                done["in", 1] = out[2:]
                own, other = both(out[2])
                grads[0] = (own[None], at_first, other[None], at_first)
        elif name[0] == "i":
            _, x, vec, om, which = saved[layer][:5]
            done["in", 0] = inputs_back(
                layer, sc, tied(done["proj", 0][0]), x, vec, back[0][1], w_qkv, w_qkv_r, which
            )
            shown.append(done["in", 0][0])
        elif name[0] == "s":
            smalls = []
            for k in range(2):
                s_bd, s_bu, s_g2, s_b2, s_bo = back[k][6:]
                smalls += [*done["in", k][1:], parts[k], s_bo, s_g2, s_b2, s_bu, s_bd]
            done["small"] = lax.psum(tied(pack(smalls)), ("section", "row", "wide"))
        else:
            kind, start, units, by_row = MATRICES[name]
            firsts, seconds = flows[kind + "0"].result, flows[kind + "1"].result
            dims = [flows[kind + str(k)].first_dims() for k in range(2)]
            done[name] = finish(tied(sc), firsts, seconds, start, units, by_row, dims)
            shown.append(done[name])

    token, fenced = jnp.zeros((8, LANES), F32), False
    for item in ORDER if links is not None else PLAIN:
        run(item)
        fenced = fenced or item == LAST
        if fenced and links is not None:
            token = fence(token, shown)
            shown[:] = [token]
    both_layers = done["small"].reshape(2, -1) + token[:1, :1]
    small = lax.dynamic_slice_in_dim(both_layers, section, 1)
    input_grads = to_owner((done["in", 0][0], done["in", 1][0]))
    g1, b1, bq, bo, gain2, bias2, bu, bd = cut(small, d, ff)
    return (
        hidden, input_grads, g1, b1, done["m0"], bq, done["m1"], bo,
        gain2, bias2, done["m2"], bu, done["m3"], bd,
    )


MATRICES = {"m0": ("q", 0, 3, False), "m1": ("u", 4, 1, False), "m2": ("u", 0, 4, False), "m3": ("d", 0, 4, True)}

KINDS = {
    "d1": ("yxwz", "xyzw"),
    "u1": ("xzwy", "zywx"),
    "q1": ("wyxz", "yxzw"),
    "d0": ("yxzw", "xywz"),
    "u0": ("xyzw", "yxwz"),
    "q0": ("yxwz", "xyzw"),
}

ORDER = (
    "f1", "d1w", "a1", "d1", "u1w", "d1", "d0w", "f0", "d0", "d1", "q1w", "d0", "a0", "u1", "u0w", "d0", "u1",
    "q0w", "q1", "u0", "i0", "d1", "q0", "q1", "u0", "d0", "s0", "d1", "q1", "d0", "u0", "u1", "d1", "q0",
    "q1", "d0", "u1", "u0", "q0", "u1", "q1", "u0", "q0", "d1", "d0", "m3", "q0", "u1", "u0", "q1", "u1",
    "u0", "m1", "q1", "q0", "m2", "q0", "m0",
)

LAST = "i0"

PLAIN = (
    "d1w", "d1", "f1", "u1w", "u1", "a1", "q1w", "q1", "d0w", "d0", "f0", "u0w", "u0", "a0", "q0w", "q0",
    "i0", "s0", "m3", "m2", "m1", "m0",
)


def cut(vec, d, ff):
    out, at = [], 0
    for size in (d, d, 3 * d, d, d, d, ff, d):
        out.append(vec[:, at : at + size])
        at += size
    return out


def solution(mesh):
    return jax.shard_map(
        local,
        mesh=mesh,
        in_specs=(
            P("wide", "row", None),
            P("wide", "row", None),
            P("wide", None),
            P(),
            P(),
            P(),
            P("section", None),
            P("section", None),
            P("section", None, None),
            P("section", None),
            P("section", None, None),
            P("section", None),
            P("section", None),
            P("section", None),
            P("section", None, None),
            P("section", None),
            P("section", None, None),
            P("section", None),
            P("section", None, None, None),
        ),
        out_specs=(
            P("section", "wide", "row", None),
            P("section", "wide", "row", None),
            P("section", None),
            P("section", None),
            P("section", None, None),
            P("section", None),
            P("section", None, None),
            P("section", None),
            P("section", None),
            P("section", None),
            P("section", None, None),
            P("section", None),
            P("section", None, None),
            P("section", None),
        ),
        check_vma=False,
    )
```

time: 2720 us -> 538 us (0.20)
  waiting for transfers between devices: 1850 us -> 83.6 us
  matrix products: 373 us -> 0 us
  Pallas kernels: 0 us -> 238 us
  local copies, waits for them, and re-layouts: 151 us -> 11.7 us
  blocking collectives: 121 us -> 0 us
  other arithmetic: 186 us -> 77 us
  starting transfers between devices: 9.35 us -> 101 us
    unnamed x29 -> x1, waiting for transfers between devices: 969 us -> 0.02 us
    reduce_scatter x4 -> x0, waiting for transfers between devices: 548 us -> none  [the longest x1 175 us: local(): lax.psum_scatter(grad_all[10][None], ('row', 'wide'), scatter_dimension=1...]
    dot_general x81 -> x0, matrix products: 360 us -> none  [the longest x12 99.5 us: times_transposed(): lax.dot_general(left, right, (((1,), (1,)), ((), ())), preferred_element_...]
    pallas_call x0 -> x61, Pallas kernels: none -> 238 us  [the longest x6 47 us: weight_grad(): pl.pallas_call(partial(weight_grad_kernel, sizes=sizes, dims=dims), out_s...]
    all_gather x4 -> x0, waiting for transfers between devices: 193 us -> none  [the longest x1 76.7 us: local(): lax.all_gather(parts[8].astype(jnp.bfloat16), ('row', 'wide'), axis=1, ti...]
    psum x5 -> x1, waiting for transfers between devices: 136 us -> 0.01 us  [run(): done['small'] = lax.psum(tied(pack(smalls)), ('section', 'row', 'wide'))]
    ppermute x4 -> x75, starting transfers between devices: 7.51 us -> 101 us  [the longest x36 48.2 us: swap(): return lax.ppermute(value, ('section', 'row', 'wide'), pairs)]
    ppermute x4 -> x75, waiting for transfers between devices: 0.01 us -> 83.5 us  [the longest x36 80.7 us: swap(): return lax.ppermute(value, ('section', 'row', 'wide'), pairs)]
  transfers between devices with their start and end apart: 25 -> 76, of which waited for: 20 -> 17; matrix products, arithmetic and copies ran while one was open for 11% -> 15% of each run, Pallas kernels for 0% -> 35%
where the time goes in v1:
time: 538 us; the launch traced here: 528 us
  Pallas kernels  238 us (44%)
  starting transfers between devices  101 us (19%)
  waiting for transfers between devices  83.6 us (16%)
  other arithmetic  77 us (14%)
  between operations  16.9 us (3%)
  local copies, waits for them, and re-layouts  11.7 us (2%)
    ppermute x36, waiting for transfers between devices, swap(): return lax.ppermute(value, ('section', 'row', 'wide'), pairs)  80.7 us
    ppermute x36, starting transfers between devices, swap(): return lax.ppermute(value, ('section', 'row', 'wide'), pairs)  48.2 us
    pallas_call x6, Pallas kernels, weight_grad(): pl.pallas_call(partial(weight_grad_kernel, sizes=sizes, dims=dims), out_s...  47 us
    pallas_call x2, Pallas kernels, forward_outputs(): pl.pallas_call(partial(outputs_kernel, layer=layer), out_shape=[jax.Shape...  40.3 us
    add x18, other arithmetic, add(): return parts[0] + parts[1]  39.2 us
    ppermute x12, starting transfers between devices, over(): return lax.ppermute(value, 'section', [(1 - self.owner, self.owner)])  38.3 us
    pallas_call x2, Pallas kernels, attention_back(): pl.pallas_call(partial(attention_back_kernel, layer=layer), out_shape=sha...  37.9 us
    pallas_call x2, Pallas kernels, ffn_back(): pl.pallas_call(partial(ffn_back_kernel, layer=layer), out_shape=[jax.Shap...  35.9 us
  transfers between devices with their start and end apart: 76, of which 17 were waited for; matrix products, arithmetic and copies ran while one was open for 15% of the time, Pallas kernels for 35%

profile of v1, /device:TPU:0, one launch (start us, length us, event | category | flops | bytes accessed | tf_op | source)
XLA Modules:
  0.0 527.8 jit_solution(15599703878197018606)
XLA Ops:
  18.8 10.9 %attention_inputs.2 = (bf16[512,768]{1,0:T(8,128)(2,1)}, f32[2,512,768]{2,1,0:T(8,128)}, bf16[2,512,384]{2,1,0:T(8,128)(2,1)}, bf16[512,768]{1,0:T(8,128)(2,1)}, bf16[32,1536]{1,0:T(8,128)(2,1)}) custom-call(s32[7]{0:T(128)} %concatenate.6.sc, bf16[2,512,768]{2,1,0:T(8,128)(2,1)} %x.5, f32[1,9984]{1,0:T(1,128)} %get-tuple-element.381.gain.bias.bq.bo.g2.b2.bu.bd, ...), custom_call_target="tpu_custom_call" | custom-call | flops 181193932800 | bytes 294912000 | tf_op jit(solution)/shard_map/attention_inputs/pallas_call | solution.py:219
  29.7 3.0 collective-permute-start.3
  32.7 7.1 %own_half.2 = (f32[512,768]{1,0:T(8,128)}, f32[512,768]{1,0:T(8,128)}) custom-call(bf16[2,512,384]{2,1,0:T(8,128)(2,1)} %get-tuple-element.186.fq.fk.f, bf16[2,512,384]{2,1,0:T(8,128)(2,1)} %get-tuple-element.186.fq.fk.f, bf16[512,768]{1,0:T(8,128)(2,1)} %get-tuple-element.187.vals, s32[512,1]{1,0:T(8,128)} %copy.73.idc, s32[1,512]{1,0:T(1,128)} %dynamic_slice.90.idr), custom_call_target="tpu_custom_call" | custom-call | flops 96636764160 | bytes 141557760 | tf_op jit(solution)/shard_map/own_half/pallas_call | solution.py:291
  40.5 20.1 %attention_out_and_ffn.2 = (bf16[512,768]{1,0:T(8,128)(2,1)}, f32[512,768]{1,0:T(8,128)}, f32[512,768]{1,0:T(8,128)}, bf16[512,768]{1,0:T(8,128)(2,1)}, bf16[2,5...) custom-call(s32[7]{0:T(128)} %concatenate.6.sc, f32[512,768]{1,0:T(8,128)} %get-tuple-element.188.num, ...), custom_call_target="tpu_custom_call" | custom-call | flops 163074539520 | bytes 754974720 | tf_op jit(solution)/shard_map/attention_out_and_ffn/pallas_call | solution.py:392
  60.6 10.9 %attention_inputs.3 = (bf16[512,768]{1,0:T(8,128)(2,1)}, f32[2,512,768]{2,1,0:T(8,128)}, bf16[2,512,384]{2,1,0:T(8,128)(2,1)}, bf16[512,768]{1,0:T(8,128)(2,1)}, bf16[32,1536]{1,0:T(8,128)(2,1)}) custom-call(s32[7]{0:T(128)} %concatenate.6.sc, bf16[1,512,768]{2,1,0:T(8,128)(2,1)} %bitcast.145, ...), custom_call_target="tpu_custom_call" | custom-call | flops 181193932800 | bytes 294912000 | tf_op jit(solution)/shard_map/attention_inputs/pallas_call | solution.py:219
  71.6 7.5 %own_half.3 = (f32[512,768]{1,0:T(8,128)}, f32[512,768]{1,0:T(8,128)}) custom-call(bf16[2,512,384]{2,1,0:T(8,128)(2,1)} %get-tuple-element.192.fq.fk.f, bf16[2,512,384]{2,1,0:T(8,128)(2,1)} %get-tuple-element.192.fq.fk.f, bf16[512,768]{1,0:T(8,128)(2,1)} %get-tuple-element.193.vals, s32[512,1]{1,0:T(8,128)} %copy.73.idc, s32[1,512]{1,0:T(1,128)} %dynamic_slice.90.idr), custom_call_target="tpu_custom_call" | custom-call | flops 96636764160 | bytes 141557760 | tf_op jit(solution)/shard_map/own_half/pallas_call | solution.py:291
  79.8 20.2 %attention_out_and_ffn.3 = (bf16[512,768]{1,0:T(8,128)(2,1)}, f32[512,768]{1,0:T(8,128)}, f32[512,768]{1,0:T(8,128)}, bf16[512,768]{1,0:T(8,128)(2,1)}, bf16[2,5...) custom-call(s32[7]{0:T(128)} %concatenate.6.sc, f32[512,768]{1,0:T(8,128)} %get-tuple-element.194.num, ...), custom_call_target="tpu_custom_call" | custom-call | flops 163074539520 | bytes 754974720 | tf_op jit(solution)/shard_map/attention_out_and_ffn/pallas_call | solution.py:392
  100.0 2.1 broadcast_select_fusion.2
  102.1 18.0 %ffn_back.2 = (bf16[512,3072]{1,0:T(8,128)(2,1)}, f32[512,768]{1,0:T(8,128)}, bf16[512,768]{1,0:T(8,128)(2,1)}, bf16[512,768]{1,0:T(8,128)(2,1)}, bf16[512,768]{...) custom-call(s32[7]{0:T(128)} %concatenate.6.sc, ...), custom_call_target="tpu_custom_call" | custom-call | flops 181193932800 | bytes 754974720 | tf_op jit(solution)/shard_map/ffn_back/pallas_call | solution.py:523
  125.8 7.4 %weight_grad.6 = (bf16[4,384,384]{2,1,0:T(8,128)(2,1)}, bf16[4,384,384]{2,1,0:T(8,128)(2,1)}) custom-call(s32[7]{0:T(128)} %concatenate.6.sc, bf16[2,512,1536]{2,1,0:T(8,128)(2,1)} %get-tuple-element.205.refs_0_, bf16[2,512,1536]{2,1,0:T(8,128)(2,1)} %collective-permute-done.9.refs_1_, bf16[2,512,768]{2,1,0:T(8,128)(2,1)} %refs_3_.3, ...), custom_call_target="tpu_custom_call" | custom-call | flops 72477573120 | bytes 188743680 | tf_op jit(solution)/shard_map/weight_grad/pallas_call | solution.py:787
  133.9 21.1 %attention_back.2 = (bf16[512,2304]{1,0:T(8,128)(2,1)}, f32[1,2304]{1,0:T(1,128)}, bf16[512,768]{1,0:T(8,128)(2,1)}, f32[1,768]{1,0:T(1,128)}, f32[1,768]{1,0:T(1,128)}) custom-call(s32[7]{0:T(128)} %concatenate.6.sc, bf16[2,512,384]{2,1,0:T(8,128)(2,1)} %get-tuple-element.192.fq.fk.f, bf16[512,768]{1,0:T(8,128)(2,1)} %get-tuple-element.193.vals, ...), custom_call_target="tpu_custom_call" | custom-call | flops 289910292480 | bytes 471859200 | tf_op jit(solution)/shard_map/attention_back/pallas_call | solution.py:705
  158.9 9.5 %weight_grad.7 = (bf16[5,384,384]{2,1,0:T(8,128)(2,1)}, bf16[5,384,384]{2,1,0:T(8,128)(2,1)}) custom-call(s32[7]{0:T(128)} %concatenate.6.sc, bf16[1,512,768]{2,1,0:T(8,128)(2,1)} %bitcast.24.refs_0_, bf16[1,512,768]{2,1,0:T(8,128)(2,1)} %bitcast.25.refs_1_, bf16[1,512,3072]{2,1,0:T(8,128)(2,1)} %bitcast.180, bf16[1,512,3072]{2,1,0:T(8,128)(2,1)} %bitcast.27.refs_3_, ...), custom_call_target="tpu_custom_call" | custom-call | flops 90596966400 | bytes 235929600 | tf_op jit(solution)/shard_map/weight_grad/pallas_call | solution.py:787
  168.5 2.1 fusion.7
  170.6 2.6 collective-permute-start.21
  174.1 7.2 %weight_grad.8 = (bf16[4,384,384]{2,1,0:T(8,128)(2,1)}, bf16[4,384,384]{2,1,0:T(8,128)(2,1)}) custom-call(s32[7]{0:T(128)} %concatenate.6.sc, bf16[2,512,1536]{2,1,0:T(8,128)(2,1)} %get-tuple-element.223.refs_0_, bf16[2,512,1536]{2,1,0:T(8,128)(2,1)} %collective-permute-done.17.refs_1_, bf16[1,512,768]{2,1,0:T(8,128)(2,1)} %bitcast.143, ...), custom_call_target="tpu_custom_call" | custom-call | flops 72477573120 | bytes 188743680 | tf_op jit(solution)/shard_map/weight_grad/pallas_call | solution.py:787
  182.7 17.9 %ffn_back.3 = (bf16[512,3072]{1,0:T(8,128)(2,1)}, f32[512,768]{1,0:T(8,128)}, bf16[512,768]{1,0:T(8,128)(2,1)}, bf16[512,768]{1,0:T(8,128)(2,1)}, bf16[512,768]{...) custom-call(s32[7]{0:T(128)} %concatenate.6.sc, ...), custom_call_target="tpu_custom_call" | custom-call | flops 181193932800 | bytes 754974720 | tf_op jit(solution)/shard_map/ffn_back/pallas_call | solution.py:523
  202.6 2.2 add.227
  206.6 7.0 %weight_grad.9 = (bf16[3,384,384]{2,1,0:T(8,128)(2,1)}, bf16[3,384,384]{2,1,0:T(8,128)(2,1)}) custom-call(s32[7]{0:T(128)} %concatenate.6.sc, bf16[1,512,768]{2,1,0:T(8,128)(2,1)} %bitcast.37.refs_0_, bf16[1,512,768]{2,1,0:T(8,128)(2,1)} %bitcast.38.refs_1_, bf16[1,512,2304]{2,1,0:T(8,128)(2,1)} %bitcast.181, bf16[1,512,2304]{2,1,0:T(8,128)(2,1)} %bitcast.40.refs_3_), custom_call_target="tpu_custom_call" | custom-call | flops 54358179840 | bytes 141557760 | tf_op jit(solution)/shard_map/weight_grad/pallas_call | solution.py:787
  213.6 14.4 %collective-permute-done.20 = bf16[768,384]{1,0:T(8,128)(2,1)S(1)} collective-permute-done((bf16[768,384]{1,0:T(8,128)(2,1)S(1)}, bf16[768,384]{1,0:T(8,128)(2,1)S(1)}, u32[]{:S(2)}, u32[]{:S(2)}) %collective-permute-start.20) | collective-permute-done | bytes 589856 | tf_op jit(solution)/shard_map/ppermute | solution.py:829
  228.5 2.1 fusion.10
  233.2 16.8 %attention_back.3 = (bf16[512,2304]{1,0:T(8,128)(2,1)}, f32[1,2304]{1,0:T(1,128)}) custom-call(s32[7]{0:T(128)} %concatenate.6.sc, bf16[2,512,384]{2,1,0:T(8,128)(2,1)} %get-tuple-element.186.fq.fk.f, bf16[512,768]{1,0:T(8,128)(2,1)} %get-tuple-element.187.vals, bf16[512,768]{1,0:T(8,128)(2,1)} %get-tuple-element.238.d_num, ...), custom_call_target="tpu_custom_call" | custom-call | flops 289910292480 | bytes 471859200 | tf_op jit(solution)/shard_map/attention_back/pallas_call | solution.py:705
  254.7 9.4 %weight_grad.10 = (bf16[5,384,384]{2,1,0:T(8,128)(2,1)}, bf16[5,384,384]{2,1,0:T(8,128)(2,1)}) custom-call(s32[7]{0:T(128)} %concatenate.6.sc, bf16[1,512,768]{2,1,0:T(8,128)(2,1)} %bitcast.44.refs_0_, bf16[1,512,768]{2,1,0:T(8,128)(2,1)} %bitcast.45.refs_1_, bf16[1,512,3072]{2,1,0:T(8,128)(2,1)} %bitcast.46.refs_2_, bf16[1,512,3072]{2,1,0:T(8,128)(2,1)} %bitcast.47.refs_3_, ...), custom_call_target="tpu_custom_call" | custom-call | flops 90596966400 | bytes 235929600 | tf_op jit(solution)/shard_map/weight_grad/pallas_call | solution.py:787
  264.1 11.8 %collective-permute-done.33 = bf16[768,384]{1,0:T(8,128)(2,1)} collective-permute-done((bf16[768,384]{1,0:T(8,128)(2,1)S(1)}, bf16[768,384]{1,0:T(8,128)(2,1)}, u32[]{:S(2)}, u32[]{:S(2)}) %collective-permute-start.33) | collective-permute-done | bytes 589856 | tf_op jit(solution)/shard_map/ppermute | solution.py:829
  275.9 2.6 collective-permute-start.37
  278.5 2.0 add.234
  280.5 3.3 collective-permute-done.32
  285.0 2.3 fusion.2
  287.2 3.4 collective-permute-start.41
  290.7 6.6 %weight_grad.11 = (bf16[3,384,384]{2,1,0:T(8,128)(2,1)}, bf16[3,384,384]{2,1,0:T(8,128)(2,1)}) custom-call(s32[7]{0:T(128)} %concatenate.6.sc, bf16[1,512,768]{2,1,0:T(8,128)(2,1)} %bitcast.55.refs_0_, bf16[1,512,768]{2,1,0:T(8,128)(2,1)} %bitcast.56.refs_1_, bf16[1,512,2304]{2,1,0:T(8,128)(2,1)} %bitcast.182, bf16[1,512,2304]{2,1,0:T(8,128)(2,1)} %bitcast.58.refs_3_), custom_call_target="tpu_custom_call" | custom-call | flops 54358179840 | bytes 141557760 | tf_op jit(solution)/shard_map/weight_grad/pallas_call | solution.py:787
  300.5 4.4 collective-permute-done.30
  307.7 8.7 %inputs_back.1 = (bf16[512,768]{1,0:T(8,128)(2,1)}, f32[1,768]{1,0:T(1,128)}, f32[1,768]{1,0:T(1,128)}) custom-call(s32[7]{0:T(128)} %concatenate.6.sc, bf16[512,2304]{1,0:T(8,128)(2,1)} %get-tuple-element.258.d_proj, bf16[2,512,768]{2,1,0:T(8,128)(2,1)} %x.5, f32[1,9984]{1,0:T(1,128)} %get-tuple-element.381.gain.bias.bq.bo.g2.b2.bu.bd, ...), custom_call_target="tpu_custom_call" | custom-call | flops 54358179840 | bytes 188743680 | tf_op jit(solution)/shard_map/inputs_back/pallas_call | solution.py:726
  319.0 2.2 add.238
  322.8 2.1 collective-permute-start.42
  326.8 3.0 collective-permute-start.36
  329.8 2.1 fusion.15
  333.7 2.3 fusion.5
  336.5 2.2 add.245
  342.8 3.0 collective-permute-start.45
  348.3 2.5 collective-permute-start.47
  352.8 2.4 collective-permute-done.44
  355.3 7.7 %collective-permute-start.59 = (bf16[4,384,384]{2,1,0:T(8,128)(2,1)}, bf16[4,384,384]{2,1,0:T(8,128)(2,1)}, u32[]{:S(2)}, u32[]{:S(2)}) collective-permute-start(bf16[4,384,384]{2,1,0:T(8,128)(2,1)} %bitcast.73.refs_4_), channel_id=1, source_target_pairs={{0,16},{1,17},{2,18},{3,19},{4,20},{5,21},{6,22},{7,23},{8,24},{9,... | collective-permute-start | bytes 3538952 | tf_op jit(solution)/shard_map/ppermute | solution.py:938
  366.6 2.4 add.247
  370.6 2.4 add.248
  375.5 2.1 fusion.17
  378.0 5.0 collective-permute-start.52
  385.6 3.2 collective-permute-start.53
  388.8 4.7 collective-permute-done.51
  395.1 2.4 add.252
  397.5 3.6 collective-permute-done.52
  401.1 2.5 collective-permute-start.58
  403.6 2.4 add.253
  406.0 4.8 collective-permute-done.53
  413.2 9.5 %collective-permute-done.54 = bf16[960,384]{1,0:T(8,128)(2,1)} collective-permute-done((bf16[960,384]{1,0:T(8,128)(2,1)}, bf16[960,384]{1,0:T(8,128)(2,1)}, u32[]{:S(2)}, u32[]{:S(2)}) %collective-permute-start.54) | collective-permute-done | bytes 737312 | tf_op jit(solution)/shard_map/ppermute | solution.py:829
  429.1 5.3 %collective-permute-done.56 = bf16[960,384]{1,0:T(8,128)(2,1)} collective-permute-done((bf16[960,384]{1,0:T(8,128)(2,1)}, bf16[960,384]{1,0:T(8,128)(2,1)}, u32[]{:S(2)}, u32[]{:S(2)}) %collective-permute-start.56) | collective-permute-done | bytes 737312 | tf_op jit(solution)/shard_map/ppermute | solution.py:829
  444.5 3.5 collective-permute-start.67
  448.0 10.6 %finish.4 = f32[3072,768]{1,0:T(8,128)} custom-call(s32[7]{0:T(128)} %concatenate.6.sc, bf16[4,384,384]{2,1,0:T(8,128)(2,1)} %bitcast.76.refs_0_, bf16[4,384,384]{2,1,0:T(8,128)(2,1)} %collective-permute-done.50.refs_1_, bf16[4,384,384]{2,1,0:T(8,128)(2,1)} %collective-permute-done.61.refs_2_, bf16[4,384,384]{2,1,0:T(8,128)(2,1)} %collective-permute-done.60.refs_3_, ...), custom_call_target="tpu_custom_call" | custom-call | flops 70778880 | bytes 566231040 | tf_op jit(solution)/shard_map/finish/pallas_call | solution.py:976
  462.3 2.9 collective-permute-done.63.refs_5_
  465.1 9.2 %collective-permute-start.71 = (bf16[3,384,384]{2,1,0:T(8,128)(2,1)}, bf16[3,384,384]{2,1,0:T(8,128)(2,1)}, u32[]{:S(2)}, u32[]{:S(2)}) collective-permute-start(bf16[3,384,384]{2,1,0:T(8,128)(2,1)} %bitcast.83.refs_4_), channel_id=1, source_target_pairs={{0,16},{1,17},{2,18},{3,19},{4,20},{5,21},{6,22},{7,23},{8,24},{9,... | collective-permute-start | bytes 2654216 | tf_op jit(solution)/shard_map/ppermute | solution.py:938
  474.3 11.8 %collective-permute-done.64.refs_1_ = bf16[5,384,384]{2,1,0:T(8,128)(2,1)} collective-permute-done((bf16[5,384,384]{2,1,0:T(8,128)(2,1)}, bf16[5,384,384]{2,1,0:T(8,128)(2,1)}, u32[]{:S(2)}, u32[]{:S(2)}) %collective-permute-start.64) | collective-permute-done | bytes 1474592 | tf_op jit(solution)/shard_map/ppermute | solution.py:829
  486.2 2.4 collective-permute-start.66
  492.0 5.2 collective-permute-start.70
  497.2 3.9 finish.5
  502.4 7.5 %finish.6 = f32[768,3072]{1,0:T(8,128)} custom-call(s32[7]{0:T(128)} %concatenate.6.sc, bf16[5,384,384]{2,1,0:T(8,128)(2,1)} %bitcast.86.refs_0_, bf16[5,384,384]{2,1,0:T(8,128)(2,1)} %collective-permute-done.64.refs_1_, bf16[5,384,384]{2,1,0:T(8,128)(2,1)} %collective-permute-done.69.refs_2_, bf16[5,384,384]{2,1,0:T(8,128)(2,1)} %collective-permute-done.68.refs_3_, ...), custom_call_target="tpu_custom_call" | custom-call | flops 70778880 | bytes 566231040 | tf_op jit(solution)/shard_map/finish/pallas_call | solution.py:976
  510.0 6.3 %finish.7 = f32[768,2304]{1,0:T(8,128)} custom-call(s32[7]{0:T(128)} %concatenate.6.sc, bf16[3,384,384]{2,1,0:T(8,128)(2,1)} %bitcast.90.refs_0_, bf16[3,384,384]{2,1,0:T(8,128)(2,1)} %collective-permute-done.72.refs_1_, bf16[3,384,384]{2,1,0:T(8,128)(2,1)} %collective-permute-done.74.refs_2_, bf16[3,384,384]{2,1,0:T(8,128)(2,1)} %collective-permute-done.73.refs_3_, ...), custom_call_target="tpu_custom_call" | custom-call | flops 53084160 | bytes 424673280 | tf_op jit(solution)/shard_map/finish/pallas_call | solution.py:976
  (271 shorter events, 103.3 us)
Async XLA Ops:
  7.2 509.6 %all-reduce.2.cloned.1.call-start = ((), (), s32[]{:S(2)}) async-start(), calls=%async_computation | async-start | bytes 159744 | tf_op jit(solution)/shard_map/psum | solution.py:1144
  11.9 27.9 %collective-permute-start.5 = (bf16[768,3072]{1,0:T(8,128)(2,1)}, bf16[768,3072]{1,0:T(8,128)(2,1)}, u32[]{:S(2)}, u32[]{:S(2)}) collective-permute-start(bf16[768,3072]{1,0:T(8,128)(2,1)} %bitcast.165), channel_id=1, source_target_pairs={{0,16},{16,0},{1,17},{17,1},{2,18},{18,2},{3,19},{19,3},{4,20},{20... | collective-permute-start | bytes 14155784 | tf_op jit(solution)/shard_map/ppermute | solution.py:1006
  12.0 27.9 %collective-permute-start.6 = (bf16[3072,768]{1,0:T(8,128)(2,1)}, bf16[3072,768]{1,0:T(8,128)(2,1)}, u32[]{:S(2)}, u32[]{:S(2)}) collective-permute-start(bf16[3072,768]{1,0:T(8,128)(2,1)} %bitcast.170), channel_id=1, source_target_pairs={{0,16},{16,0},{1,17},{17,1},{2,18},{18,2},{3,19},{19,3},{4,20},{20... | collective-permute-start | bytes 14155784 | tf_op jit(solution)/shard_map/ppermute | solution.py:1006
  16.6 23.3 %collective-permute-start.4 = (bf16[768,768]{1,0:T(8,128)(2,1)}, bf16[768,768]{1,0:T(8,128)(2,1)}, u32[]{:S(2)}, u32[]{:S(2)}) collective-permute-start(bf16[768,768]{1,0:T(8,128)(2,1)} %bitcast.12.wo), channel_id=1, source_target_pairs={{0,16},{16,0},{1,17},{17,1},{2,18},{18,2},{3,19},{19,3},{4,20},{20... | collective-permute-start | bytes 3538952 | tf_op jit(solution)/shard_map/ppermute | solution.py:1006
  99.9 25.6 %collective-permute-start.9 = (bf16[2,512,1536]{2,1,0:T(8,128)(2,1)}, bf16[2,512,1536]{2,1,0:T(8,128)(2,1)}, u32[]{:S(2)}, u32[]{:S(2)}) collective-permute-start(bf16[2,512,1536]{2,1,0:T(8,128)(2,1)} %get-tuple-element.205.refs_0_), channel_id=1, source_target_pairs={{0,16},{16,0},{1,17},{17,1},{2,18},{18,2},{3,19},{19,3},{4,20},{20... | collective-permute-start | bytes 9437192 | tf_op jit(solution)/shard_map/ppermute | solution.py:1047
  102.1 20.6 %collective-permute-start.8 = (bf16[512,768]{1,0:T(8,128)(2,1)}, bf16[512,768]{1,0:T(8,128)(2,1)}, u32[]{:S(2)}, u32[]{:S(2)}) collective-permute-start(bf16[512,768]{1,0:T(8,128)(2,1)} %broadcast_select_fusion.2), channel_id=1, source_target_pairs={{0,16},{16,0},{1,17},{17,1},{2,18},{18,2},{3,19},{19,3},{4,20},{20... | collective-permute-start | bytes 2359304 | tf_op jit(solution)/shard_map/ppermute | solution.py:1052
  120.1 37.6 %collective-permute-start.14 = (bf16[512,3072]{1,0:T(8,128)(2,1)}, bf16[512,3072]{1,0:T(8,128)(2,1)}, u32[]{:S(2)}, u32[]{:S(2)}) collective-permute-start(bf16[512,3072]{1,0:T(8,128)(2,1)} %get-tuple-element.203), channel_id=1, source_target_pairs={{0,16},{16,0},{1,17},{17,1},{2,18},{18,2},{3,19},{19,3},{4,20},{20... | collective-permute-start | bytes 9437192 | tf_op jit(solution)/shard_map/ppermute | solution.py:1006
  120.7 37.0 %collective-permute-start.15 = (bf16[512,768]{1,0:T(8,128)(2,1)}, bf16[512,768]{1,0:T(8,128)(2,1)}, u32[]{:S(2)}, u32[]{:S(2)}) collective-permute-start(bf16[512,768]{1,0:T(8,128)(2,1)} %get-tuple-element.200.att), channel_id=1, source_target_pairs={{0,16},{16,0},{1,17},{17,1},{2,18},{18,2},{3,19},{19,3},{4,20},{20... | collective-permute-start | bytes 2359304 | tf_op jit(solution)/shard_map/ppermute | solution.py:1047
  120.8 12.4 %collective-permute-start.10 = (bf16[32,1536]{1,0:T(8,128)(2,1)}, bf16[32,1536]{1,0:T(8,128)(2,1)S(1)}, u32[]{:S(2)}, u32[]{:S(2)}) collective-permute-start(bf16[32,1536]{1,0:T(8,128)(2,1)} %get-tuple-element.210), channel_id=1, source_target_pairs={{0,8},{8,0},{1,9},{9,1},{2,10},{10,2},{3,11},{11,3},{4,12},{12,4},... | collective-permute-start | bytes 294920 | tf_op jit(solution)/shard_map/ppermute | solution.py:1116
  122.8 34.3 %collective-permute-start.16 = (bf16[512,768]{1,0:T(8,128)(2,1)}, bf16[512,768]{1,0:T(8,128)(2,1)}, u32[]{:S(2)}, u32[]{:S(2)}) collective-permute-start(bf16[512,768]{1,0:T(8,128)(2,1)} %get-tuple-element.219), channel_id=1, source_target_pairs={{0,16},{16,0},{1,17},{17,1},{2,18},{18,2},{3,19},{19,3},{4,20},{20... | collective-permute-start | bytes 2359304 | tf_op jit(solution)/shard_map/ppermute | solution.py:1006
  125.5 31.8 %collective-permute-start.13 = (bf16[512,768]{1,0:T(8,128)(2,1)}, bf16[512,768]{1,0:T(8,128)(2,1)}, u32[]{:S(2)}, u32[]{:S(2)}) collective-permute-start(bf16[512,768]{1,0:T(8,128)(2,1)} %get-tuple-element.218), channel_id=1, source_target_pairs={{0,16},{16,0},{1,17},{17,1},{2,18},{18,2},{3,19},{19,3},{4,20},{20... | collective-permute-start | bytes 2359304 | tf_op jit(solution)/shard_map/ppermute | solution.py:1047
  133.2 21.8 %collective-permute-start.11 = (bf16[4,384,384]{2,1,0:T(8,128)(2,1)}, bf16[4,384,384]{2,1,0:T(8,128)(2,1)}, u32[]{:S(2)}, u32[]{:S(2)}) collective-permute-start(bf16[4,384,384]{2,1,0:T(8,128)(2,1)} %get-tuple-element.206), channel_id=1, source_target_pairs={{0,8},{1,9},{2,10},{3,11},{4,12},{5,13},{6,14},{7,15},{8,0},{9,1},... | collective-permute-start | bytes 3538952 | tf_op jit(solution)/shard_map/ppermute | solution.py:829
  155.0 15.6 %collective-permute-start.17 = (bf16[2,512,1536]{2,1,0:T(8,128)(2,1)}, bf16[2,512,1536]{2,1,0:T(8,128)(2,1)}, u32[]{:S(2)}, u32[]{:S(2)}) collective-permute-start(bf16[2,512,1536]{2,1,0:T(8,128)(2,1)} %get-tuple-element.223.refs_0_), channel_id=1, source_target_pairs={{0,16},{16,0},{1,17},{17,1},{2,18},{18,2},{3,19},{19,3},{4,20},{20... | collective-permute-start | bytes 9437192 | tf_op jit(solution)/shard_map/ppermute | solution.py:1047
  157.1 47.7 %collective-permute-start.22 = (bf16[512,768]{1,0:T(8,128)(2,1)}, bf16[512,768]{1,0:T(8,128)(2,1)}, u32[]{:S(2)}, u32[]{:S(2)}) collective-permute-start(bf16[512,768]{1,0:T(8,128)(2,1)} %get-tuple-element.235), channel_id=1, source_target_pairs={{0,16},{16,0},{1,17},{17,1},{2,18},{18,2},{3,19},{19,3},{4,20},{20... | collective-permute-start | bytes 2359304 | tf_op jit(solution)/shard_map/ppermute | solution.py:1047
  157.3 95.2 %collective-permute-start.28 = (bf16[512,768]{1,0:T(8,128)(2,1)}, bf16[512,768]{1,0:T(8,128)(2,1)}, u32[]{:S(2)}, u32[]{:S(2)}) collective-permute-start(bf16[512,768]{1,0:T(8,128)(2,1)} %get-tuple-element.227.att), channel_id=1, source_target_pairs={{0,16},{16,0},{1,17},{17,1},{2,18},{18,2},{3,19},{19,3},{4,20},{20... | collective-permute-start | bytes 2359304 | tf_op jit(solution)/shard_map/ppermute | solution.py:1047
  157.7 15.5 %collective-permute-start.18 = (bf16[512,768]{1,0:T(8,128)(2,1)S(1)}, bf16[512,768]{1,0:T(8,128)(2,1)S(1)}, u32[]{:S(2)}, u32[]{:S(2)}) collective-permute-start(bf16[512,768]{1,0:T(8,128)(2,1)S(1)} %copy-done.2), channel_id=1, source_target_pairs={{0,16},{16,0},{1,17},{17,1},{2,18},{18,2},{3,19},{19,3},{4,20},{20... | collective-permute-start | bytes 2359304 | tf_op jit(solution)/shard_map/ppermute | solution.py:1006
  168.4 37.7 %collective-permute-start.23 = (bf16[512,2304]{1,0:T(8,128)(2,1)}, bf16[512,2304]{1,0:T(8,128)(2,1)}, u32[]{:S(2)}, u32[]{:S(2)}) collective-permute-start(bf16[512,2304]{1,0:T(8,128)(2,1)} %get-tuple-element.215), channel_id=1, source_target_pairs={{0,16},{16,0},{1,17},{17,1},{2,18},{18,2},{3,19},{19,3},{4,20},{20... | collective-permute-start | bytes 7077896 | tf_op jit(solution)/shard_map/ppermute | solution.py:1006
  170.6 31.4 %collective-permute-start.21 = (bf16[768,384]{1,0:T(8,128)(2,1)}, bf16[768,384]{1,0:T(8,128)(2,1)}, u32[]{:S(2)}, u32[]{:S(2)}) collective-permute-start(bf16[768,384]{1,0:T(8,128)(2,1)} %fusion.7), channel_id=1, source_target_pairs={{0,4},{1,5},{2,6},{3,7},{4,0},{5,1},{6,2},{7,3},{8,12},{9,13},{10,... | collective-permute-start | bytes 1769480 | tf_op jit(solution)/shard_map/ppermute | solution.py:829
  181.3 19.4 %collective-permute-start.19 = (bf16[4,384,384]{2,1,0:T(8,128)(2,1)}, bf16[4,384,384]{2,1,0:T(8,128)(2,1)}, u32[]{:S(2)}, u32[]{:S(2)}) collective-permute-start(bf16[4,384,384]{2,1,0:T(8,128)(2,1)} %get-tuple-element.224), channel_id=1, source_target_pairs={{0,8},{1,9},{2,10},{3,11},{4,12},{5,13},{6,14},{7,15},{8,0},{9,1},... | collective-permute-start | bytes 3538952 | tf_op jit(solution)/shard_map/ppermute | solution.py:829
  200.7 50.8 %collective-permute-start.26 = (bf16[512,768]{1,0:T(8,128)(2,1)}, bf16[512,768]{1,0:T(8,128)(2,1)}, u32[]{:S(2)}, u32[]{:S(2)}) collective-permute-start(bf16[512,768]{1,0:T(8,128)(2,1)} %get-tuple-element.246), channel_id=1, source_target_pairs={{0,16},{16,0},{1,17},{17,1},{2,18},{18,2},{3,19},{19,3},{4,20},{20... | collective-permute-start | bytes 2359304 | tf_op jit(solution)/shard_map/ppermute | solution.py:1047
  202.0 48.0 %collective-permute-start.25 = (bf16[5,384,384]{2,1,0:T(8,128)(2,1)}, bf16[5,384,384]{2,1,0:T(8,128)(2,1)}, u32[]{:S(2)}, u32[]{:S(2)}) collective-permute-start(bf16[5,384,384]{2,1,0:T(8,128)(2,1)} %get-tuple-element.220), channel_id=1, source_target_pairs={{0,1},{1,0},{2,3},{3,2},{4,5},{5,4},{6,7},{7,6},{8,9},{9,8},{10,11... | collective-permute-start | bytes 4423688 | tf_op jit(solution)/shard_map/ppermute | solution.py:829
  204.8 49.9 %collective-permute-start.27 = (bf16[512,3072]{1,0:T(8,128)(2,1)}, bf16[512,3072]{1,0:T(8,128)(2,1)}, u32[]{:S(2)}, u32[]{:S(2)}) collective-permute-start(bf16[512,3072]{1,0:T(8,128)(2,1)} %get-tuple-element.231), channel_id=1, source_target_pairs={{0,16},{16,0},{1,17},{17,1},{2,18},{18,2},{3,19},{19,3},{4,20},{20... | collective-permute-start | bytes 9437192 | tf_op jit(solution)/shard_map/ppermute | solution.py:1006
  206.1 21.9 %collective-permute-start.20 = (bf16[768,384]{1,0:T(8,128)(2,1)S(1)}, bf16[768,384]{1,0:T(8,128)(2,1)S(1)}, u32[]{:S(2)}, u32[]{:S(2)}) collective-permute-start(bf16[768,384]{1,0:T(8,128)(2,1)S(1)} %fusion.11), channel_id=1, source_target_pairs={{0,1},{1,0},{2,3},{3,2},{4,5},{5,4},{6,7},{7,6},{8,9},{9,8},{10,11... | collective-permute-start | bytes 1769480 | tf_op jit(solution)/shard_map/ppermute | solution.py:829
  232.6 20.9 %collective-permute-start.29 = (bf16[512,768]{1,0:T(8,128)(2,1)}, bf16[512,768]{1,0:T(8,128)(2,1)}, u32[]{:S(2)}, u32[]{:S(2)}) collective-permute-start(bf16[512,768]{1,0:T(8,128)(2,1)} %get-tuple-element.247), channel_id=1, source_target_pairs={{0,16},{16,0},{1,17},{17,1},{2,18},{18,2},{3,19},{19,3},{4,20},{20... | collective-permute-start | bytes 2359304 | tf_op jit(solution)/shard_map/ppermute | solution.py:1006
  250.0 37.2 %collective-permute-start.34 = (bf16[512,768]{1,0:T(8,128)(2,1)}, bf16[512,768]{1,0:T(8,128)(2,1)}, u32[]{:S(2)}, u32[]{:S(2)}) collective-permute-start(bf16[512,768]{1,0:T(8,128)(2,1)} %get-tuple-element.254), channel_id=1, source_target_pairs={{0,16},{16,0},{1,17},{17,1},{2,18},{18,2},{3,19},{19,3},{4,20},{20... | collective-permute-start | bytes 2359304 | tf_op jit(solution)/shard_map/ppermute | solution.py:1047
  251.5 45.8 %collective-permute-start.31 = (bf16[3,384,384]{2,1,0:T(8,128)(2,1)}, bf16[3,384,384]{2,1,0:T(8,128)(2,1)}, u32[]{:S(2)}, u32[]{:S(2)}) collective-permute-start(bf16[3,384,384]{2,1,0:T(8,128)(2,1)} %get-tuple-element.236), channel_id=1, source_target_pairs={{0,4},{1,5},{2,6},{3,7},{4,0},{5,1},{6,2},{7,3},{8,12},{9,13},{10,... | collective-permute-start | bytes 2654216 | tf_op jit(solution)/shard_map/ppermute | solution.py:829
  252.4 23.5 %collective-permute-start.33 = (bf16[768,384]{1,0:T(8,128)(2,1)S(1)}, bf16[768,384]{1,0:T(8,128)(2,1)}, u32[]{:S(2)}, u32[]{:S(2)}) collective-permute-start(bf16[768,384]{1,0:T(8,128)(2,1)S(1)} %copy-done.10), channel_id=1, source_target_pairs={{0,2},{1,3},{2,0},{3,1},{4,6},{5,7},{6,4},{7,5},{8,10},{9,11},{10,... | collective-permute-start | bytes 1769480 | tf_op jit(solution)/shard_map/ppermute | solution.py:829
  253.5 30.3 %collective-permute-start.32 = (bf16[960,384]{1,0:T(8,128)(2,1)S(1)}, bf16[960,384]{1,0:T(8,128)(2,1)S(1)}, u32[]{:S(2)}, u32[]{:S(2)}) collective-permute-start(bf16[960,384]{1,0:T(8,128)(2,1)S(1)} %fusion), channel_id=1, source_target_pairs={{0,2},{1,3},{2,0},{3,1},{4,6},{5,7},{6,4},{7,5},{8,10},{9,11},{10,... | collective-permute-start | bytes 2211848 | tf_op jit(solution)/shard_map/ppermute | solution.py:829
  254.7 36.0 %collective-permute-start.35 = (bf16[512,2304]{1,0:T(8,128)(2,1)}, bf16[512,2304]{1,0:T(8,128)(2,1)}, u32[]{:S(2)}, u32[]{:S(2)}) collective-permute-start(bf16[512,2304]{1,0:T(8,128)(2,1)} %get-tuple-element.258.d_proj), channel_id=1, source_target_pairs={{0,16},{16,0},{1,17},{17,1},{2,18},{18,2},{3,19},{19,3},{4,20},{20... | collective-permute-start | bytes 7077896 | tf_op jit(solution)/shard_map/ppermute | solution.py:1006
  275.9 42.8 %collective-permute-start.37 = (bf16[768,384]{1,0:T(8,128)(2,1)}, bf16[768,384]{1,0:T(8,128)(2,1)}, u32[]{:S(2)}, u32[]{:S(2)}) collective-permute-start(bf16[768,384]{1,0:T(8,128)(2,1)} %add.227), channel_id=1, source_target_pairs={{0,2},{1,3},{2,0},{3,1},{4,6},{5,7},{6,4},{7,5},{8,10},{9,11},{10,... | collective-permute-start | bytes 1769480 | tf_op jit(solution)/shard_map/ppermute | solution.py:829
  283.8 21.1 %collective-permute-start.30 = (bf16[5,384,384]{2,1,0:T(8,128)(2,1)}, bf16[5,384,384]{2,1,0:T(8,128)(2,1)S(1)}, u32[]{:S(2)}, u32[]{:S(2)}) collective-permute-start(bf16[5,384,384]{2,1,0:T(8,128)(2,1)} %get-tuple-element.249), channel_id=1, source_target_pairs={{0,1},{1,0},{2,3},{3,2},{4,5},{5,4},{6,7},{7,6},{8,9},{9,8},{10,11... | collective-permute-start | bytes 4423688 | tf_op jit(solution)/shard_map/ppermute | solution.py:829
  287.2 48.7 %collective-permute-start.41 = (bf16[768,384]{1,0:T(8,128)(2,1)}, bf16[768,384]{1,0:T(8,128)(2,1)}, u32[]{:S(2)}, u32[]{:S(2)}) collective-permute-start(bf16[768,384]{1,0:T(8,128)(2,1)} %add.234), channel_id=1, source_target_pairs={{0,4},{1,5},{2,6},{3,7},{4,0},{5,1},{6,2},{7,3},{8,12},{9,13},{10,... | collective-permute-start | bytes 1769480 | tf_op jit(solution)/shard_map/ppermute | solution.py:829
  290.6 78.3 %collective-permute-start.46 = (bf16[960,384]{1,0:T(8,128)(2,1)}, bf16[960,384]{1,0:T(8,128)(2,1)}, u32[]{:S(2)}, u32[]{:S(2)}) collective-permute-start(bf16[960,384]{1,0:T(8,128)(2,1)} %fusion.2), channel_id=1, source_target_pairs={{0,4},{1,5},{2,6},{3,7},{4,0},{5,1},{6,2},{7,3},{8,12},{9,13},{10,... | collective-permute-start | bytes 2211848 | tf_op jit(solution)/shard_map/ppermute | solution.py:829
  297.3 25.5 %collective-permute-start.38 = (bf16[3,384,384]{2,1,0:T(8,128)(2,1)}, bf16[3,384,384]{2,1,0:T(8,128)(2,1)}, u32[]{:S(2)}, u32[]{:S(2)}) collective-permute-start(bf16[3,384,384]{2,1,0:T(8,128)(2,1)} %get-tuple-element.255), channel_id=1, source_target_pairs={{0,8},{1,9},{2,10},{3,11},{4,12},{5,13},{6,14},{7,15},{8,0},{9,1},... | collective-permute-start | bytes 2654216 | tf_op jit(solution)/shard_map/ppermute | solution.py:829
  304.9 21.9 %collective-permute-start.39 = (bf16[576,384]{1,0:T(8,128)(2,1)}, bf16[576,384]{1,0:T(8,128)(2,1)}, u32[]{:S(2)}, u32[]{:S(2)}) collective-permute-start(bf16[576,384]{1,0:T(8,128)(2,1)} %fusion.12), channel_id=1, source_target_pairs={{0,8},{1,9},{2,10},{3,11},{4,12},{5,13},{6,14},{7,15},{8,0},{9,1},... | collective-permute-start | bytes 1327112 | tf_op jit(solution)/shard_map/ppermute | solution.py:829
  318.7 13.2 %collective-permute-start.40 = (bf16[960,384]{1,0:T(8,128)(2,1)}, bf16[960,384]{1,0:T(8,128)(2,1)}, u32[]{:S(2)}, u32[]{:S(2)}) collective-permute-start(bf16[960,384]{1,0:T(8,128)(2,1)} %fusion.3), channel_id=1, source_target_pairs={{0,8},{1,9},{2,10},{3,11},{4,12},{5,13},{6,14},{7,15},{8,0},{9,1},... | collective-permute-start | bytes 2211848 | tf_op jit(solution)/shard_map/ppermute | solution.py:829
  322.8 16.6 %collective-permute-start.42 = (bf16[768,384]{1,0:T(8,128)(2,1)}, bf16[768,384]{1,0:T(8,128)(2,1)}, u32[]{:S(2)}, u32[]{:S(2)}) collective-permute-start(bf16[768,384]{1,0:T(8,128)(2,1)} %add.238), channel_id=1, source_target_pairs={{0,1},{1,0},{2,3},{3,2},{4,5},{5,4},{6,7},{7,6},{8,9},{9,8},{10,11... | collective-permute-start | bytes 1769480 | tf_op jit(solution)/shard_map/ppermute | solution.py:829
  326.8 15.9 %collective-permute-start.36 = (bf16[512,768]{1,0:T(8,128)(2,1)}, bf16[512,768]{1,0:T(8,128)(2,1)}, u32[]{:S(2)}, u32[]{:S(2)}) collective-permute-start(bf16[512,768]{1,0:T(8,128)(2,1)} %broadcast_select_fusion), channel_id=1, source_target_pairs={{0,16},{16,0},{1,17},{17,1},{2,18},{18,2},{3,19},{19,3},{4,20},{20... | collective-permute-start | bytes 2359304 | tf_op jit(solution)/shard_map/ppermute | solution.py:1052
  331.9 16.4 %collective-permute-start.43 = (bf16[576,384]{1,0:T(8,128)(2,1)}, bf16[576,384]{1,0:T(8,128)(2,1)}, u32[]{:S(2)}, u32[]{:S(2)}) collective-permute-start(bf16[576,384]{1,0:T(8,128)(2,1)} %fusion.15), channel_id=1, source_target_pairs={{0,1},{1,0},{2,3},{3,2},{4,5},{5,4},{6,7},{7,6},{8,9},{9,8},{10,11... | collective-permute-start | bytes 1327112 | tf_op jit(solution)/shard_map/ppermute | solution.py:829
  336.0 38.3 %collective-permute-start.48 = (bf16[576,384]{1,0:T(8,128)(2,1)}, bf16[576,384]{1,0:T(8,128)(2,1)}, u32[]{:S(2)}, u32[]{:S(2)}) collective-permute-start(bf16[576,384]{1,0:T(8,128)(2,1)} %fusion.13), channel_id=1, source_target_pairs={{0,1},{1,0},{2,3},{3,2},{4,5},{5,4},{6,7},{7,6},{8,9},{9,8},{10,11... | collective-permute-start | bytes 1327112 | tf_op jit(solution)/shard_map/ppermute | solution.py:829
  339.4 15.9 %collective-permute-start.44 = (bf16[768,384]{1,0:T(8,128)(2,1)}, bf16[768,384]{1,0:T(8,128)(2,1)}, u32[]{:S(2)}, u32[]{:S(2)}) collective-permute-start(bf16[768,384]{1,0:T(8,128)(2,1)} %add.245), channel_id=1, source_target_pairs={{0,1},{1,0},{2,3},{3,2},{4,5},{5,4},{6,7},{7,6},{8,9},{9,8},{10,11... | collective-permute-start | bytes 1769480 | tf_op jit(solution)/shard_map/ppermute | solution.py:829
  342.8 22.8 %collective-permute-start.45 = (bf16[960,384]{1,0:T(8,128)(2,1)}, bf16[960,384]{1,0:T(8,128)(2,1)}, u32[]{:S(2)}, u32[]{:S(2)}) collective-permute-start(bf16[960,384]{1,0:T(8,128)(2,1)} %fusion.5), channel_id=1, source_target_pairs={{0,2},{1,3},{2,0},{3,1},{4,6},{5,7},{6,4},{7,5},{8,10},{9,11},{10,... | collective-permute-start | bytes 2211848 | tf_op jit(solution)/shard_map/ppermute | solution.py:829
  348.3 24.7 %collective-permute-start.47 = (bf16[4,384,384]{2,1,0:T(8,128)(2,1)}, bf16[4,384,384]{2,1,0:T(8,128)(2,1)}, u32[]{:S(2)}, u32[]{:S(2)}) collective-permute-start(bf16[4,384,384]{2,1,0:T(8,128)(2,1)} %bitcast.73.refs_4_), channel_id=1, source_target_pairs={{0,8},{1,9},{2,10},{3,11},{4,12},{5,13},{6,14},{7,15},{8,0},{9,1},... | collective-permute-start | bytes 3538952 | tf_op jit(solution)/shard_map/ppermute | solution.py:829
  355.3 86.1 %collective-permute-start.59 = (bf16[4,384,384]{2,1,0:T(8,128)(2,1)}, bf16[4,384,384]{2,1,0:T(8,128)(2,1)}, u32[]{:S(2)}, u32[]{:S(2)}) collective-permute-start(bf16[4,384,384]{2,1,0:T(8,128)(2,1)} %bitcast.73.refs_4_), channel_id=1, source_target_pairs={{0,16},{1,17},{2,18},{3,19},{4,20},{5,21},{6,22},{7,23},{8,24},{9,... | collective-permute-start | bytes 3538952 | tf_op jit(solution)/shard_map/ppermute | solution.py:938
  365.5 12.5 %collective-permute-start.49 = (bf16[576,384]{1,0:T(8,128)(2,1)}, bf16[576,384]{1,0:T(8,128)(2,1)}, u32[]{:S(2)}, u32[]{:S(2)}) collective-permute-start(bf16[576,384]{1,0:T(8,128)(2,1)} %add.246), channel_id=1, source_target_pairs={{0,2},{1,3},{2,0},{3,1},{4,6},{5,7},{6,4},{7,5},{8,10},{9,11},{10,... | collective-permute-start | bytes 1327112 | tf_op jit(solution)/shard_map/ppermute | solution.py:829
  369.0 16.7 %collective-permute-start.50 = (bf16[4,384,384]{2,1,0:T(8,128)(2,1)}, bf16[4,384,384]{2,1,0:T(8,128)(2,1)}, u32[]{:S(2)}, u32[]{:S(2)}) collective-permute-start(bf16[4,384,384]{2,1,0:T(8,128)(2,1)} %bitcast.76.refs_0_), channel_id=1, source_target_pairs={{0,8},{1,9},{2,10},{3,11},{4,12},{5,13},{6,14},{7,15},{8,0},{9,1},... | collective-permute-start | bytes 3538952 | tf_op jit(solution)/shard_map/ppermute | solution.py:829
  373.0 70.4 %collective-permute-start.61 = (bf16[4,384,384]{2,1,0:T(8,128)(2,1)}, bf16[4,384,384]{2,1,0:T(8,128)(2,1)}, u32[]{:S(2)}, u32[]{:S(2)}) collective-permute-start(bf16[4,384,384]{2,1,0:T(8,128)(2,1)} %bitcast.76.refs_0_), channel_id=1, source_target_pairs={{16,0},{17,1},{18,2},{19,3},{20,4},{21,5},{22,6},{23,7},{24,8},{25... | collective-permute-start | bytes 3538952 | tf_op jit(solution)/shard_map/ppermute | solution.py:938
  374.3 19.2 %collective-permute-start.51 = (bf16[960,384]{1,0:T(8,128)(2,1)}, bf16[960,384]{1,0:T(8,128)(2,1)}, u32[]{:S(2)}, u32[]{:S(2)}) collective-permute-start(bf16[960,384]{1,0:T(8,128)(2,1)} %add.248), channel_id=1, source_target_pairs={{0,8},{1,9},{2,10},{3,11},{4,12},{5,13},{6,14},{7,15},{8,0},{9,1},... | collective-permute-start | bytes 2211848 | tf_op jit(solution)/shard_map/ppermute | solution.py:829
  378.0 23.1 %collective-permute-start.52 = (bf16[960,384]{1,0:T(8,128)(2,1)}, bf16[960,384]{1,0:T(8,128)(2,1)}, u32[]{:S(2)}, u32[]{:S(2)}) collective-permute-start(bf16[960,384]{1,0:T(8,128)(2,1)} %add.247), channel_id=1, source_target_pairs={{0,4},{1,5},{2,6},{3,7},{4,0},{5,1},{6,2},{7,3},{8,12},{9,13},{10,... | collective-permute-start | bytes 2211848 | tf_op jit(solution)/shard_map/ppermute | solution.py:829
  385.6 25.2 %collective-permute-start.53 = (bf16[576,384]{1,0:T(8,128)(2,1)}, bf16[576,384]{1,0:T(8,128)(2,1)}, u32[]{:S(2)}, u32[]{:S(2)}) collective-permute-start(bf16[576,384]{1,0:T(8,128)(2,1)} %fusion.17), channel_id=1, source_target_pairs={{0,4},{1,5},{2,6},{3,7},{4,0},{5,1},{6,2},{7,3},{8,12},{9,13},{10,... | collective-permute-start | bytes 1327112 | tf_op jit(solution)/shard_map/ppermute | solution.py:829
  393.6 31.9 %collective-permute-start.55 = (bf16[576,384]{1,0:T(8,128)(2,1)}, bf16[576,384]{1,0:T(8,128)(2,1)}, u32[]{:S(2)}, u32[]{:S(2)}) collective-permute-start(bf16[576,384]{1,0:T(8,128)(2,1)} %add.251), channel_id=1, source_target_pairs={{0,8},{1,9},{2,10},{3,11},{4,12},{5,13},{6,14},{7,15},{8,0},{9,1},... | collective-permute-start | bytes 1327112 | tf_op jit(solution)/shard_map/ppermute | solution.py:829
  401.1 41.4 %collective-permute-start.58 = (bf16[4,384,384]{2,1,0:T(8,128)(2,1)}, bf16[4,384,384]{2,1,0:T(8,128)(2,1)}, u32[]{:S(2)}, u32[]{:S(2)}) collective-permute-start(bf16[4,384,384]{2,1,0:T(8,128)(2,1)} %collective-permute-done.47.refs_5_), channel_id=1, source_target_pairs={{0,16},{1,17},{2,18},{3,19},{4,20},{5,21},{6,22},{7,23},{8,24},{9,... | collective-permute-start | bytes 3538952 | tf_op jit(solution)/shard_map/ppermute | solution.py:938
  410.8 11.8 %collective-permute-start.54 = (bf16[960,384]{1,0:T(8,128)(2,1)}, bf16[960,384]{1,0:T(8,128)(2,1)}, u32[]{:S(2)}, u32[]{:S(2)}) collective-permute-start(bf16[960,384]{1,0:T(8,128)(2,1)} %add.252), channel_id=1, source_target_pairs={{0,2},{1,3},{2,0},{3,1},{4,6},{5,7},{6,4},{7,5},{8,10},{9,11},{10,... | collective-permute-start | bytes 2211848 | tf_op jit(solution)/shard_map/ppermute | solution.py:829
  422.6 11.8 %collective-permute-start.56 = (bf16[960,384]{1,0:T(8,128)(2,1)}, bf16[960,384]{1,0:T(8,128)(2,1)}, u32[]{:S(2)}, u32[]{:S(2)}) collective-permute-start(bf16[960,384]{1,0:T(8,128)(2,1)} %add.253), channel_id=1, source_target_pairs={{0,8},{1,9},{2,10},{3,11},{4,12},{5,13},{6,14},{7,15},{8,0},{9,1},... | collective-permute-start | bytes 2211848 | tf_op jit(solution)/shard_map/ppermute | solution.py:829
  425.4 13.1 %collective-permute-start.57 = (bf16[576,384]{1,0:T(8,128)(2,1)}, bf16[576,384]{1,0:T(8,128)(2,1)}, u32[]{:S(2)}, u32[]{:S(2)}) collective-permute-start(bf16[576,384]{1,0:T(8,128)(2,1)} %add.254), channel_id=1, source_target_pairs={{0,2},{1,3},{2,0},{3,1},{4,6},{5,7},{6,4},{7,5},{8,10},{9,11},{10,... | collective-permute-start | bytes 1327112 | tf_op jit(solution)/shard_map/ppermute | solution.py:829
  440.5 18.2 %collective-permute-start.62 = (bf16[576,384]{1,0:T(8,128)(2,1)}, bf16[576,384]{1,0:T(8,128)(2,1)}, u32[]{:S(2)}, u32[]{:S(2)}) collective-permute-start(bf16[576,384]{1,0:T(8,128)(2,1)} %add.255), channel_id=1, source_target_pairs={{0,1},{1,0},{2,3},{3,2},{4,5},{5,4},{6,7},{7,6},{8,9},{9,8},{10,11... | collective-permute-start | bytes 1327112 | tf_op jit(solution)/shard_map/ppermute | solution.py:829
  441.4 23.8 %collective-permute-start.63 = (bf16[5,384,384]{2,1,0:T(8,128)(2,1)}, bf16[5,384,384]{2,1,0:T(8,128)(2,1)}, u32[]{:S(2)}, u32[]{:S(2)}) collective-permute-start(bf16[5,384,384]{2,1,0:T(8,128)(2,1)} %bitcast.80.refs_4_), channel_id=1, source_target_pairs={{0,1},{1,0},{2,3},{3,2},{4,5},{5,4},{6,7},{7,6},{8,9},{9,8},{10,11... | collective-permute-start | bytes 4423688 | tf_op jit(solution)/shard_map/ppermute | solution.py:829
  442.5 43.5 %collective-permute-start.64 = (bf16[5,384,384]{2,1,0:T(8,128)(2,1)}, bf16[5,384,384]{2,1,0:T(8,128)(2,1)}, u32[]{:S(2)}, u32[]{:S(2)}) collective-permute-start(bf16[5,384,384]{2,1,0:T(8,128)(2,1)} %bitcast.86.refs_0_), channel_id=1, source_target_pairs={{0,1},{1,0},{2,3},{3,2},{4,5},{5,4},{6,7},{7,6},{8,9},{9,8},{10,11... | collective-permute-start | bytes 4423688 | tf_op jit(solution)/shard_map/ppermute | solution.py:829
  443.4 42.8 %collective-permute-start.65 = (bf16[3,384,384]{2,1,0:T(8,128)(2,1)}, bf16[3,384,384]{2,1,0:T(8,128)(2,1)}, u32[]{:S(2)}, u32[]{:S(2)}) collective-permute-start(bf16[3,384,384]{2,1,0:T(8,128)(2,1)} %bitcast.83.refs_4_), channel_id=1, source_target_pairs={{0,4},{1,5},{2,6},{3,7},{4,0},{5,1},{6,2},{7,3},{8,12},{9,13},{10,... | collective-permute-start | bytes 2654216 | tf_op jit(solution)/shard_map/ppermute | solution.py:829
  444.5 44.1 %collective-permute-start.67 = (bf16[5,384,384]{2,1,0:T(8,128)(2,1)}, bf16[5,384,384]{2,1,0:T(8,128)(2,1)}, u32[]{:S(2)}, u32[]{:S(2)}) collective-permute-start(bf16[5,384,384]{2,1,0:T(8,128)(2,1)} %bitcast.80.refs_4_), channel_id=1, source_target_pairs={{0,16},{1,17},{2,18},{3,19},{4,20},{5,21},{6,22},{7,23},{8,24},{9,... | collective-permute-start | bytes 4423688 | tf_op jit(solution)/shard_map/ppermute | solution.py:938
  458.7 33.4 %collective-permute-start.69 = (bf16[5,384,384]{2,1,0:T(8,128)(2,1)}, bf16[5,384,384]{2,1,0:T(8,128)(2,1)}, u32[]{:S(2)}, u32[]{:S(2)}) collective-permute-start(bf16[5,384,384]{2,1,0:T(8,128)(2,1)} %bitcast.86.refs_0_), channel_id=1, source_target_pairs={{16,0},{17,1},{18,2},{19,3},{20,4},{21,5},{22,6},{23,7},{24,8},{25... | collective-permute-start | bytes 4423688 | tf_op jit(solution)/shard_map/ppermute | solution.py:938
  465.1 35.9 %collective-permute-start.71 = (bf16[3,384,384]{2,1,0:T(8,128)(2,1)}, bf16[3,384,384]{2,1,0:T(8,128)(2,1)}, u32[]{:S(2)}, u32[]{:S(2)}) collective-permute-start(bf16[3,384,384]{2,1,0:T(8,128)(2,1)} %bitcast.83.refs_4_), channel_id=1, source_target_pairs={{0,16},{1,17},{2,18},{3,19},{4,20},{5,21},{6,22},{7,23},{8,24},{9,... | collective-permute-start | bytes 2654216 | tf_op jit(solution)/shard_map/ppermute | solution.py:938
  486.1 15.0 %collective-permute-start.72 = (bf16[3,384,384]{2,1,0:T(8,128)(2,1)}, bf16[3,384,384]{2,1,0:T(8,128)(2,1)}, u32[]{:S(2)}, u32[]{:S(2)}) collective-permute-start(bf16[3,384,384]{2,1,0:T(8,128)(2,1)} %bitcast.90.refs_0_), channel_id=1, source_target_pairs={{0,8},{1,9},{2,10},{3,11},{4,12},{5,13},{6,14},{7,15},{8,0},{9,1},... | collective-permute-start | bytes 2654216 | tf_op jit(solution)/shard_map/ppermute | solution.py:829
  488.7 21.3 %collective-permute-start.74 = (bf16[3,384,384]{2,1,0:T(8,128)(2,1)}, bf16[3,384,384]{2,1,0:T(8,128)(2,1)}, u32[]{:S(2)}, u32[]{:S(2)}) collective-permute-start(bf16[3,384,384]{2,1,0:T(8,128)(2,1)} %bitcast.90.refs_0_), channel_id=1, source_target_pairs={{16,0},{17,1},{18,2},{19,3},{20,4},{21,5},{22,6},{23,7},{24,8},{25... | collective-permute-start | bytes 2654216 | tf_op jit(solution)/shard_map/ppermute | solution.py:938
  (41 other events, 306.2 us)
Sparse Core Ops, SparseCore 0:
  342.9 128.6 all-reduce.1

commit v2 on v1

--- a/solution.py
+++ b/solution.py
@@ -935,7 +935,7 @@
         return [send]
 
     def over(self, value):
-        return lax.ppermute(value, "section", [(1 - self.owner, self.owner)])
+        return lax.ppermute(value, "section", SWAP)
 
     def plain(self, came):
         total = jnp.concatenate([self.parts, came], axis=0)
@@ -944,50 +944,46 @@
         return []
 
 
-def finish_kernel(sc, *refs, by_row, dims):
+def finish_kernel(sc, *refs, dims):
     out = refs[-1]
     for layer in range(2):
         for side in range(2):
             half = layer if side == 0 else 1 - layer
-            base = 0 if by_row else half * ROWS
             ends = dims[layer] if side == 0 or dims[layer] is None else dims[layer][::-1]
             for bit in range(2):
                 here = (sc[0] == layer) & (bit_of(sc, ends) == bit)
-                if by_row:
-                    here = here & (pl.program_id(1) == half)
 
                 @pl.when(here)
                 def _():
                     at = 4 * layer + 2 * side
-                    out[base : base + ROWS, :ROWS] = refs[at + bit][0].astype(F32)
-                    out[base : base + ROWS, ROWS:] = refs[at + 1 - bit][0].astype(F32)
+                    out[half, :, :ROWS] = refs[at + bit][0].astype(F32)
+                    out[half, :, ROWS:] = refs[at + 1 - bit][0].astype(F32)
 
 
 def finish(sc, first, second, start, units, by_row, dims):
     spec = lambda layer: pl.BlockSpec(
-        (1, ROWS, ROWS), lambda u, h, s: (start + jnp.where(s[0] == layer, u, 0), 0, 0)
+        (1, ROWS, ROWS), lambda u, s: (start + jnp.where(s[0] == layer, u, 0), 0, 0)
     )
     if by_row:
-        shape, grid = (2 * units * ROWS, UNIT), (units, 2)
-        out = pl.BlockSpec((ROWS, UNIT), lambda u, h, s: (h * units + u, 0))
+        shape, place = (2, units * ROWS, UNIT), lambda u, s: (0, u, 0)
     else:
-        shape, grid = (UNIT, units * UNIT), (units, 1)
-        out = pl.BlockSpec((UNIT, UNIT), lambda u, h, s: (0, u))
-    return pl.pallas_call(
-        partial(finish_kernel, by_row=by_row, dims=dims),
+        shape, place = (2, ROWS, units * UNIT), lambda u, s: (0, 0, u)
+    out = pl.pallas_call(
+        partial(finish_kernel, dims=dims),
         out_shape=jax.ShapeDtypeStruct(shape, F32),
         grid_spec=pltpu.PrefetchScalarGridSpec(
             num_scalar_prefetch=1,
-            grid=grid,
+            grid=(units,),
             in_specs=[spec(0)] * 4 + [spec(1)] * 4,
-            out_specs=out,
+            out_specs=pl.BlockSpec((2, ROWS, UNIT), place),
         ),
         compiler_params=params(),
         cost_estimate=pl.CostEstimate(
             flops=COST * units * UNIT * UNIT, bytes_accessed=COST * units * 8 * UNIT * UNIT, transcendentals=0
         ),
         name="finish",
-    )(sc, *first, *second)[None]
+    )(sc, *first, *second)
+    return out.reshape(1, -1, shape[2])
 
 
 def local(

time: 538 us -> 537 us (level)
  waiting for transfers between devices: 83.6 us -> 109 us
  starting transfers between devices: 101 us -> 79.6 us
    ppermute x12, starting transfers between devices: 38.3 us -> 10.8 us  [over(): return lax.ppermute(value, 'section', SWAP)]
    ppermute x36, waiting for transfers between devices: 80.7 us -> 101 us  [swap(): return lax.ppermute(value, ('section', 'row', 'wide'), pairs)]
    ppermute x36, starting transfers between devices: 48.2 us -> 54.2 us  [swap(): return lax.ppermute(value, ('section', 'row', 'wide'), pairs)]
    ppermute x12, waiting for transfers between devices: 0.81 us -> 6.22 us  [over(): return lax.ppermute(value, 'section', SWAP)]
  transfers between devices with their start and end apart: 76 -> 76, of which waited for: 17 -> 18; matrix products, arithmetic and copies ran while one was open for 15% -> 15% of each run, Pallas kernels for 35% -> 35%
where the time goes in v2:
time: 537 us; the launch traced here: 529 us
  Pallas kernels  235 us (44%)
  waiting for transfers between devices  109 us (20%)
  starting transfers between devices  79.6 us (15%)
  other arithmetic  77 us (14%)
  between operations  17.1 us (3%)
  local copies, waits for them, and re-layouts  11.5 us (2%)
    ppermute x36, waiting for transfers between devices, swap(): return lax.ppermute(value, ('section', 'row', 'wide'), pairs)  101 us
    ppermute x36, starting transfers between devices, swap(): return lax.ppermute(value, ('section', 'row', 'wide'), pairs)  54.2 us
    pallas_call x6, Pallas kernels, weight_grad(): pl.pallas_call(partial(weight_grad_kernel, sizes=sizes, dims=dims), out_s...  47 us
    pallas_call x2, Pallas kernels, forward_outputs(): pl.pallas_call(partial(outputs_kernel, layer=layer), out_shape=[jax.Shape...  40.3 us
    add x18, other arithmetic, add(): return parts[0] + parts[1]  39.2 us
    pallas_call x2, Pallas kernels, attention_back(): pl.pallas_call(partial(attention_back_kernel, layer=layer), out_shape=sha...  38.1 us
    pallas_call x2, Pallas kernels, ffn_back(): pl.pallas_call(partial(ffn_back_kernel, layer=layer), out_shape=[jax.Shap...  35.9 us
    pallas_call x4, Pallas kernels, finish(): pl.pallas_call(partial(finish_kernel, dims=dims), out_shape=jax.ShapeDtyp...  25.5 us
  transfers between devices with their start and end apart: 76, of which 18 were waited for; matrix products, arithmetic and copies ran while one was open for 15% of the time, Pallas kernels for 35%

profile of v2, /device:TPU:0, one launch (start us, length us, event | category | flops | bytes accessed | tf_op | source)
XLA Modules:
  0.0 529.1 jit_solution(8378858028990853745)
XLA Ops:
  18.8 10.9 %attention_inputs.2 = (bf16[512,768]{1,0:T(8,128)(2,1)}, f32[2,512,768]{2,1,0:T(8,128)}, bf16[2,512,384]{2,1,0:T(8,128)(2,1)}, bf16[512,768]{1,0:T(8,128)(2,1)}, bf16[32,1536]{1,0:T(8,128)(2,1)}) custom-call(s32[7]{0:T(128)} %concatenate.6.sc, bf16[2,512,768]{2,1,0:T(8,128)(2,1)} %x.5, f32[1,9984]{1,0:T(1,128)} %get-tuple-element.381.gain.bias.bq.bo.g2.b2.bu.bd, ...), custom_call_target="tpu_custom_call" | custom-call | flops 181193932800 | bytes 294912000 | tf_op jit(solution)/shard_map/attention_inputs/pallas_call | solution.py:219
  29.7 3.0 collective-permute-start.3
  32.7 7.1 %own_half.2 = (f32[512,768]{1,0:T(8,128)}, f32[512,768]{1,0:T(8,128)}) custom-call(bf16[2,512,384]{2,1,0:T(8,128)(2,1)} %get-tuple-element.186.fq.fk.f, bf16[2,512,384]{2,1,0:T(8,128)(2,1)} %get-tuple-element.186.fq.fk.f, bf16[512,768]{1,0:T(8,128)(2,1)} %get-tuple-element.187.vals, s32[512,1]{1,0:T(8,128)} %copy.73.idc, s32[1,512]{1,0:T(1,128)} %dynamic_slice.90.idr), custom_call_target="tpu_custom_call" | custom-call | flops 96636764160 | bytes 141557760 | tf_op jit(solution)/shard_map/own_half/pallas_call | solution.py:291
  40.5 20.2 %attention_out_and_ffn.2 = (bf16[512,768]{1,0:T(8,128)(2,1)}, f32[512,768]{1,0:T(8,128)}, f32[512,768]{1,0:T(8,128)}, bf16[512,768]{1,0:T(8,128)(2,1)}, bf16[2,5...) custom-call(s32[7]{0:T(128)} %concatenate.6.sc, f32[512,768]{1,0:T(8,128)} %get-tuple-element.188.num, ...), custom_call_target="tpu_custom_call" | custom-call | flops 163074539520 | bytes 754974720 | tf_op jit(solution)/shard_map/attention_out_and_ffn/pallas_call | solution.py:392
  60.7 10.9 %attention_inputs.3 = (bf16[512,768]{1,0:T(8,128)(2,1)}, f32[2,512,768]{2,1,0:T(8,128)}, bf16[2,512,384]{2,1,0:T(8,128)(2,1)}, bf16[512,768]{1,0:T(8,128)(2,1)}, bf16[32,1536]{1,0:T(8,128)(2,1)}) custom-call(s32[7]{0:T(128)} %concatenate.6.sc, bf16[1,512,768]{2,1,0:T(8,128)(2,1)} %bitcast.145, ...), custom_call_target="tpu_custom_call" | custom-call | flops 181193932800 | bytes 294912000 | tf_op jit(solution)/shard_map/attention_inputs/pallas_call | solution.py:219
  71.6 7.6 %own_half.3 = (f32[512,768]{1,0:T(8,128)}, f32[512,768]{1,0:T(8,128)}) custom-call(bf16[2,512,384]{2,1,0:T(8,128)(2,1)} %get-tuple-element.192.fq.fk.f, bf16[2,512,384]{2,1,0:T(8,128)(2,1)} %get-tuple-element.192.fq.fk.f, bf16[512,768]{1,0:T(8,128)(2,1)} %get-tuple-element.193.vals, s32[512,1]{1,0:T(8,128)} %copy.73.idc, s32[1,512]{1,0:T(1,128)} %dynamic_slice.90.idr), custom_call_target="tpu_custom_call" | custom-call | flops 96636764160 | bytes 141557760 | tf_op jit(solution)/shard_map/own_half/pallas_call | solution.py:291
  79.9 20.2 %attention_out_and_ffn.3 = (bf16[512,768]{1,0:T(8,128)(2,1)}, f32[512,768]{1,0:T(8,128)}, f32[512,768]{1,0:T(8,128)}, bf16[512,768]{1,0:T(8,128)(2,1)}, bf16[2,5...) custom-call(s32[7]{0:T(128)} %concatenate.6.sc, f32[512,768]{1,0:T(8,128)} %get-tuple-element.194.num, ...), custom_call_target="tpu_custom_call" | custom-call | flops 163074539520 | bytes 754974720 | tf_op jit(solution)/shard_map/attention_out_and_ffn/pallas_call | solution.py:392
  100.1 2.1 broadcast_select_fusion.2
  102.2 18.0 %ffn_back.2 = (bf16[512,3072]{1,0:T(8,128)(2,1)}, f32[512,768]{1,0:T(8,128)}, bf16[512,768]{1,0:T(8,128)(2,1)}, bf16[512,768]{1,0:T(8,128)(2,1)}, bf16[512,768]{...) custom-call(s32[7]{0:T(128)} %concatenate.6.sc, ...), custom_call_target="tpu_custom_call" | custom-call | flops 181193932800 | bytes 754974720 | tf_op jit(solution)/shard_map/ffn_back/pallas_call | solution.py:523
  125.9 7.4 %weight_grad.6 = (bf16[4,384,384]{2,1,0:T(8,128)(2,1)}, bf16[4,384,384]{2,1,0:T(8,128)(2,1)}) custom-call(s32[7]{0:T(128)} %concatenate.6.sc, bf16[2,512,1536]{2,1,0:T(8,128)(2,1)} %get-tuple-element.205.refs_0_, bf16[2,512,1536]{2,1,0:T(8,128)(2,1)} %collective-permute-done.9.refs_1_, bf16[2,512,768]{2,1,0:T(8,128)(2,1)} %refs_3_.3, ...), custom_call_target="tpu_custom_call" | custom-call | flops 72477573120 | bytes 188743680 | tf_op jit(solution)/shard_map/weight_grad/pallas_call | solution.py:787
  134.0 21.3 %attention_back.2 = (bf16[512,2304]{1,0:T(8,128)(2,1)}, f32[1,2304]{1,0:T(1,128)}, bf16[512,768]{1,0:T(8,128)(2,1)}, f32[1,768]{1,0:T(1,128)}, f32[1,768]{1,0:T(1,128)}) custom-call(s32[7]{0:T(128)} %concatenate.6.sc, bf16[2,512,384]{2,1,0:T(8,128)(2,1)} %get-tuple-element.192.fq.fk.f, bf16[512,768]{1,0:T(8,128)(2,1)} %get-tuple-element.193.vals, ...), custom_call_target="tpu_custom_call" | custom-call | flops 289910292480 | bytes 471859200 | tf_op jit(solution)/shard_map/attention_back/pallas_call | solution.py:705
  159.2 9.5 %weight_grad.7 = (bf16[5,384,384]{2,1,0:T(8,128)(2,1)}, bf16[5,384,384]{2,1,0:T(8,128)(2,1)}) custom-call(s32[7]{0:T(128)} %concatenate.6.sc, bf16[1,512,768]{2,1,0:T(8,128)(2,1)} %bitcast.24.refs_0_, bf16[1,512,768]{2,1,0:T(8,128)(2,1)} %bitcast.25.refs_1_, bf16[1,512,3072]{2,1,0:T(8,128)(2,1)} %bitcast.180, bf16[1,512,3072]{2,1,0:T(8,128)(2,1)} %bitcast.27.refs_3_, ...), custom_call_target="tpu_custom_call" | custom-call | flops 90596966400 | bytes 235929600 | tf_op jit(solution)/shard_map/weight_grad/pallas_call | solution.py:787
  168.8 2.1 fusion.7
  170.9 2.6 collective-permute-start.21
  174.4 7.2 %weight_grad.8 = (bf16[4,384,384]{2,1,0:T(8,128)(2,1)}, bf16[4,384,384]{2,1,0:T(8,128)(2,1)}) custom-call(s32[7]{0:T(128)} %concatenate.6.sc, bf16[2,512,1536]{2,1,0:T(8,128)(2,1)} %get-tuple-element.223.refs_0_, bf16[2,512,1536]{2,1,0:T(8,128)(2,1)} %collective-permute-done.17.refs_1_, bf16[1,512,768]{2,1,0:T(8,128)(2,1)} %bitcast.143, ...), custom_call_target="tpu_custom_call" | custom-call | flops 72477573120 | bytes 188743680 | tf_op jit(solution)/shard_map/weight_grad/pallas_call | solution.py:787
  183.0 17.9 %ffn_back.3 = (bf16[512,3072]{1,0:T(8,128)(2,1)}, f32[512,768]{1,0:T(8,128)}, bf16[512,768]{1,0:T(8,128)(2,1)}, bf16[512,768]{1,0:T(8,128)(2,1)}, bf16[512,768]{...) custom-call(s32[7]{0:T(128)} %concatenate.6.sc, ...), custom_call_target="tpu_custom_call" | custom-call | flops 181193932800 | bytes 754974720 | tf_op jit(solution)/shard_map/ffn_back/pallas_call | solution.py:523
  202.9 2.2 add.227
  206.9 6.7 %weight_grad.9 = (bf16[3,384,384]{2,1,0:T(8,128)(2,1)}, bf16[3,384,384]{2,1,0:T(8,128)(2,1)}) custom-call(s32[7]{0:T(128)} %concatenate.6.sc, bf16[1,512,768]{2,1,0:T(8,128)(2,1)} %bitcast.37.refs_0_, bf16[1,512,768]{2,1,0:T(8,128)(2,1)} %bitcast.38.refs_1_, bf16[1,512,2304]{2,1,0:T(8,128)(2,1)} %bitcast.181, bf16[1,512,2304]{2,1,0:T(8,128)(2,1)} %bitcast.40.refs_3_), custom_call_target="tpu_custom_call" | custom-call | flops 54358179840 | bytes 141557760 | tf_op jit(solution)/shard_map/weight_grad/pallas_call | solution.py:787
  213.6 14.7 %collective-permute-done.20 = bf16[768,384]{1,0:T(8,128)(2,1)S(1)} collective-permute-done((bf16[768,384]{1,0:T(8,128)(2,1)S(1)}, bf16[768,384]{1,0:T(8,128)(2,1)S(1)}, u32[]{:S(2)}, u32[]{:S(2)}) %collective-permute-start.20) | collective-permute-done | bytes 589856 | tf_op jit(solution)/shard_map/ppermute | solution.py:829
  228.8 2.1 fusion.10
  233.5 16.8 %attention_back.3 = (bf16[512,2304]{1,0:T(8,128)(2,1)}, f32[1,2304]{1,0:T(1,128)}) custom-call(s32[7]{0:T(128)} %concatenate.6.sc, bf16[2,512,384]{2,1,0:T(8,128)(2,1)} %get-tuple-element.186.fq.fk.f, bf16[512,768]{1,0:T(8,128)(2,1)} %get-tuple-element.187.vals, bf16[512,768]{1,0:T(8,128)(2,1)} %get-tuple-element.238.d_num, ...), custom_call_target="tpu_custom_call" | custom-call | flops 289910292480 | bytes 471859200 | tf_op jit(solution)/shard_map/attention_back/pallas_call | solution.py:705
  254.8 9.4 %weight_grad.10 = (bf16[5,384,384]{2,1,0:T(8,128)(2,1)}, bf16[5,384,384]{2,1,0:T(8,128)(2,1)}) custom-call(s32[7]{0:T(128)} %concatenate.6.sc, bf16[1,512,768]{2,1,0:T(8,128)(2,1)} %bitcast.44.refs_0_, bf16[1,512,768]{2,1,0:T(8,128)(2,1)} %bitcast.45.refs_1_, bf16[1,512,3072]{2,1,0:T(8,128)(2,1)} %bitcast.46.refs_2_, bf16[1,512,3072]{2,1,0:T(8,128)(2,1)} %bitcast.47.refs_3_, ...), custom_call_target="tpu_custom_call" | custom-call | flops 90596966400 | bytes 235929600 | tf_op jit(solution)/shard_map/weight_grad/pallas_call | solution.py:787
  264.2 12.0 %collective-permute-done.33 = bf16[768,384]{1,0:T(8,128)(2,1)} collective-permute-done((bf16[768,384]{1,0:T(8,128)(2,1)S(1)}, bf16[768,384]{1,0:T(8,128)(2,1)}, u32[]{:S(2)}, u32[]{:S(2)}) %collective-permute-start.33) | collective-permute-done | bytes 589856 | tf_op jit(solution)/shard_map/ppermute | solution.py:829
  276.2 2.6 collective-permute-start.37
  278.8 2.0 add.234
  280.8 3.3 collective-permute-done.32
  285.3 2.3 fusion.2
  287.5 3.4 collective-permute-start.41
  291.0 6.8 %weight_grad.11 = (bf16[3,384,384]{2,1,0:T(8,128)(2,1)}, bf16[3,384,384]{2,1,0:T(8,128)(2,1)}) custom-call(s32[7]{0:T(128)} %concatenate.6.sc, bf16[1,512,768]{2,1,0:T(8,128)(2,1)} %bitcast.55.refs_0_, bf16[1,512,768]{2,1,0:T(8,128)(2,1)} %bitcast.56.refs_1_, bf16[1,512,2304]{2,1,0:T(8,128)(2,1)} %bitcast.182, bf16[1,512,2304]{2,1,0:T(8,128)(2,1)} %bitcast.58.refs_3_), custom_call_target="tpu_custom_call" | custom-call | flops 54358179840 | bytes 141557760 | tf_op jit(solution)/shard_map/weight_grad/pallas_call | solution.py:787
  301.0 4.0 collective-permute-done.30
  307.7 8.7 %inputs_back.1 = (bf16[512,768]{1,0:T(8,128)(2,1)}, f32[1,768]{1,0:T(1,128)}, f32[1,768]{1,0:T(1,128)}) custom-call(s32[7]{0:T(128)} %concatenate.6.sc, bf16[512,2304]{1,0:T(8,128)(2,1)} %get-tuple-element.258.d_proj, bf16[2,512,768]{2,1,0:T(8,128)(2,1)} %x.5, f32[1,9984]{1,0:T(1,128)} %get-tuple-element.381.gain.bias.bq.bo.g2.b2.bu.bd, ...), custom_call_target="tpu_custom_call" | custom-call | flops 54358179840 | bytes 188743680 | tf_op jit(solution)/shard_map/inputs_back/pallas_call | solution.py:726
  319.1 2.2 add.238
  322.9 2.1 collective-permute-start.42
  326.9 3.0 collective-permute-start.36
  329.9 2.1 fusion.15
  333.8 2.3 fusion.5
  336.6 2.2 add.245
  342.9 2.9 collective-permute-start.45
  348.4 2.5 collective-permute-start.47
  352.9 2.5 collective-permute-done.44
  355.4 5.0 collective-permute-start.59
  363.9 2.4 add.247
  366.3 4.3 collective-permute-start.50
  370.6 2.4 add.248
  374.3 2.1 fusion.17
  376.4 6.6 %collective-permute-start.52 = (bf16[960,384]{1,0:T(8,128)(2,1)}, bf16[960,384]{1,0:T(8,128)(2,1)}, u32[]{:S(2)}, u32[]{:S(2)}) collective-permute-start(bf16[960,384]{1,0:T(8,128)(2,1)} %add.247), channel_id=1, source_target_pairs={{0,4},{1,5},{2,6},{3,7},{4,0},{5,1},{6,2},{7,3},{8,12},{9,13},{10,... | collective-permute-start | bytes 2211848 | tf_op jit(solution)/shard_map/ppermute | solution.py:829
  385.1 3.6 collective-permute-start.53
  388.7 4.5 collective-permute-done.51
  395.1 2.4 add.252
  397.5 3.6 collective-permute-done.52
  401.1 2.4 add.253
  403.5 6.9 %collective-permute-done.53 = bf16[576,384]{1,0:T(8,128)(2,1)} collective-permute-done((bf16[576,384]{1,0:T(8,128)(2,1)}, bf16[576,384]{1,0:T(8,128)(2,1)}, u32[]{:S(2)}, u32[]{:S(2)}) %collective-permute-start.53) | collective-permute-done | bytes 442400 | tf_op jit(solution)/shard_map/ppermute | solution.py:829
  412.4 9.8 %collective-permute-done.54 = bf16[960,384]{1,0:T(8,128)(2,1)} collective-permute-done((bf16[960,384]{1,0:T(8,128)(2,1)}, bf16[960,384]{1,0:T(8,128)(2,1)}, u32[]{:S(2)}, u32[]{:S(2)}) %collective-permute-start.54) | collective-permute-done | bytes 737312 | tf_op jit(solution)/shard_map/ppermute | solution.py:829
  428.1 5.9 %collective-permute-done.56 = bf16[960,384]{1,0:T(8,128)(2,1)} collective-permute-done((bf16[960,384]{1,0:T(8,128)(2,1)}, bf16[960,384]{1,0:T(8,128)(2,1)}, u32[]{:S(2)}, u32[]{:S(2)}) %collective-permute-start.56) | collective-permute-done | bytes 737312 | tf_op jit(solution)/shard_map/ppermute | solution.py:829
  444.2 7.5 %finish.4 = f32[2,1536,768]{2,1,0:T(8,128)} custom-call(s32[7]{0:T(128)} %concatenate.6.sc, bf16[4,384,384]{2,1,0:T(8,128)(2,1)} %bitcast.76.refs_0_, bf16[4,384,384]{2,1,0:T(8,128)(2,1)} %collective-permute-done.50.refs_1_, bf16[4,384,384]{2,1,0:T(8,128)(2,1)} %collective-permute-done.61.refs_2_, bf16[4,384,384]{2,1,0:T(8,128)(2,1)} %collective-permute-done.60.refs_3_, ...), custom_call_target="tpu_custom_call" | custom-call | flops 70778880 | bytes 566231040 | tf_op jit(solution)/shard_map/finish/pallas_call | solution.py:971
  454.6 10.3 %collective-permute-done.63.refs_5_ = bf16[5,384,384]{2,1,0:T(8,128)(2,1)} collective-permute-done((bf16[5,384,384]{2,1,0:T(8,128)(2,1)}, bf16[5,384,384]{2,1,0:T(8,128)(2,1)}, u32[]{:S(2)}, u32[]{:S(2)}) %collective-permute-start.63) | collective-permute-done | bytes 1474592 | tf_op jit(solution)/shard_map/ppermute | solution.py:829
  464.9 3.9 collective-permute-start.71
  468.8 20.8 %collective-permute-done.64.refs_1_ = bf16[5,384,384]{2,1,0:T(8,128)(2,1)} collective-permute-done((bf16[5,384,384]{2,1,0:T(8,128)(2,1)}, bf16[5,384,384]{2,1,0:T(8,128)(2,1)}, u32[]{:S(2)}, u32[]{:S(2)}) %collective-permute-start.64) | collective-permute-done | bytes 1474592 | tf_op jit(solution)/shard_map/ppermute | solution.py:829
  489.6 2.3 collective-permute-start.72
  492.5 3.1 collective-permute-done.66.refs_7_
  496.1 3.1 collective-permute-done.68.refs_3_
  499.2 4.1 finish.5
  503.5 7.5 %finish.6 = f32[2,384,3072]{2,1,0:T(8,128)} custom-call(s32[7]{0:T(128)} %concatenate.6.sc, bf16[5,384,384]{2,1,0:T(8,128)(2,1)} %bitcast.86.refs_0_, bf16[5,384,384]{2,1,0:T(8,128)(2,1)} %collective-permute-done.64.refs_1_, bf16[5,384,384]{2,1,0:T(8,128)(2,1)} %collective-permute-done.69.refs_2_, bf16[5,384,384]{2,1,0:T(8,128)(2,1)} %collective-permute-done.68.refs_3_, ...), custom_call_target="tpu_custom_call" | custom-call | flops 70778880 | bytes 566231040 | tf_op jit(solution)/shard_map/finish/pallas_call | solution.py:971
  511.1 6.3 %finish.7 = f32[2,384,2304]{2,1,0:T(8,128)} custom-call(s32[7]{0:T(128)} %concatenate.6.sc, bf16[3,384,384]{2,1,0:T(8,128)(2,1)} %bitcast.90.refs_0_, bf16[3,384,384]{2,1,0:T(8,128)(2,1)} %collective-permute-done.72.refs_1_, bf16[3,384,384]{2,1,0:T(8,128)(2,1)} %collective-permute-done.74.refs_2_, bf16[3,384,384]{2,1,0:T(8,128)(2,1)} %collective-permute-done.73.refs_3_, ...), custom_call_target="tpu_custom_call" | custom-call | flops 53084160 | bytes 424673280 | tf_op jit(solution)/shard_map/finish/pallas_call | solution.py:971
  (271 shorter events, 94.4 us)
Async XLA Ops:
  7.2 510.7 %all-reduce.2.cloned.1.call-start = ((), (), s32[]{:S(2)}) async-start(), calls=%async_computation | async-start | bytes 159744 | tf_op jit(solution)/shard_map/psum | solution.py:1140
  11.9 27.9 %collective-permute-start.5 = (bf16[768,3072]{1,0:T(8,128)(2,1)}, bf16[768,3072]{1,0:T(8,128)(2,1)}, u32[]{:S(2)}, u32[]{:S(2)}) collective-permute-start(bf16[768,3072]{1,0:T(8,128)(2,1)} %bitcast.165), channel_id=1, source_target_pairs={{0,16},{16,0},{1,17},{17,1},{2,18},{18,2},{3,19},{19,3},{4,20},{20... | collective-permute-start | bytes 14155784 | tf_op jit(solution)/shard_map/ppermute | solution.py:1002
  12.0 27.9 %collective-permute-start.6 = (bf16[3072,768]{1,0:T(8,128)(2,1)}, bf16[3072,768]{1,0:T(8,128)(2,1)}, u32[]{:S(2)}, u32[]{:S(2)}) collective-permute-start(bf16[3072,768]{1,0:T(8,128)(2,1)} %bitcast.170), channel_id=1, source_target_pairs={{0,16},{16,0},{1,17},{17,1},{2,18},{18,2},{3,19},{19,3},{4,20},{20... | collective-permute-start | bytes 14155784 | tf_op jit(solution)/shard_map/ppermute | solution.py:1002
  16.6 23.3 %collective-permute-start.4 = (bf16[768,768]{1,0:T(8,128)(2,1)}, bf16[768,768]{1,0:T(8,128)(2,1)}, u32[]{:S(2)}, u32[]{:S(2)}) collective-permute-start(bf16[768,768]{1,0:T(8,128)(2,1)} %bitcast.12.wo), channel_id=1, source_target_pairs={{0,16},{16,0},{1,17},{17,1},{2,18},{18,2},{3,19},{19,3},{4,20},{20... | collective-permute-start | bytes 3538952 | tf_op jit(solution)/shard_map/ppermute | solution.py:1002
  100.0 25.6 %collective-permute-start.9 = (bf16[2,512,1536]{2,1,0:T(8,128)(2,1)}, bf16[2,512,1536]{2,1,0:T(8,128)(2,1)}, u32[]{:S(2)}, u32[]{:S(2)}) collective-permute-start(bf16[2,512,1536]{2,1,0:T(8,128)(2,1)} %get-tuple-element.205.refs_0_), channel_id=1, source_target_pairs={{0,16},{16,0},{1,17},{17,1},{2,18},{18,2},{3,19},{19,3},{4,20},{20... | collective-permute-start | bytes 9437192 | tf_op jit(solution)/shard_map/ppermute | solution.py:1043
  102.2 20.6 %collective-permute-start.8 = (bf16[512,768]{1,0:T(8,128)(2,1)}, bf16[512,768]{1,0:T(8,128)(2,1)}, u32[]{:S(2)}, u32[]{:S(2)}) collective-permute-start(bf16[512,768]{1,0:T(8,128)(2,1)} %broadcast_select_fusion.2), channel_id=1, source_target_pairs={{0,16},{16,0},{1,17},{17,1},{2,18},{18,2},{3,19},{19,3},{4,20},{20... | collective-permute-start | bytes 2359304 | tf_op jit(solution)/shard_map/ppermute | solution.py:1048
  120.3 37.8 %collective-permute-start.14 = (bf16[512,3072]{1,0:T(8,128)(2,1)}, bf16[512,3072]{1,0:T(8,128)(2,1)}, u32[]{:S(2)}, u32[]{:S(2)}) collective-permute-start(bf16[512,3072]{1,0:T(8,128)(2,1)} %get-tuple-element.203), channel_id=1, source_target_pairs={{0,16},{16,0},{1,17},{17,1},{2,18},{18,2},{3,19},{19,3},{4,20},{20... | collective-permute-start | bytes 9437192 | tf_op jit(solution)/shard_map/ppermute | solution.py:1002
  120.8 37.2 %collective-permute-start.15 = (bf16[512,768]{1,0:T(8,128)(2,1)}, bf16[512,768]{1,0:T(8,128)(2,1)}, u32[]{:S(2)}, u32[]{:S(2)}) collective-permute-start(bf16[512,768]{1,0:T(8,128)(2,1)} %get-tuple-element.200.att), channel_id=1, source_target_pairs={{0,16},{16,0},{1,17},{17,1},{2,18},{18,2},{3,19},{19,3},{4,20},{20... | collective-permute-start | bytes 2359304 | tf_op jit(solution)/shard_map/ppermute | solution.py:1043
  120.9 12.4 %collective-permute-start.10 = (bf16[32,1536]{1,0:T(8,128)(2,1)}, bf16[32,1536]{1,0:T(8,128)(2,1)S(1)}, u32[]{:S(2)}, u32[]{:S(2)}) collective-permute-start(bf16[32,1536]{1,0:T(8,128)(2,1)} %get-tuple-element.210), channel_id=1, source_target_pairs={{0,8},{8,0},{1,9},{9,1},{2,10},{10,2},{3,11},{11,3},{4,12},{12,4},... | collective-permute-start | bytes 294920 | tf_op jit(solution)/shard_map/ppermute | solution.py:1112
  122.9 34.5 %collective-permute-start.16 = (bf16[512,768]{1,0:T(8,128)(2,1)}, bf16[512,768]{1,0:T(8,128)(2,1)}, u32[]{:S(2)}, u32[]{:S(2)}) collective-permute-start(bf16[512,768]{1,0:T(8,128)(2,1)} %get-tuple-element.219), channel_id=1, source_target_pairs={{0,16},{16,0},{1,17},{17,1},{2,18},{18,2},{3,19},{19,3},{4,20},{20... | collective-permute-start | bytes 2359304 | tf_op jit(solution)/shard_map/ppermute | solution.py:1002
  125.6 31.9 %collective-permute-start.13 = (bf16[512,768]{1,0:T(8,128)(2,1)}, bf16[512,768]{1,0:T(8,128)(2,1)}, u32[]{:S(2)}, u32[]{:S(2)}) collective-permute-start(bf16[512,768]{1,0:T(8,128)(2,1)} %get-tuple-element.218), channel_id=1, source_target_pairs={{0,16},{16,0},{1,17},{17,1},{2,18},{18,2},{3,19},{19,3},{4,20},{20... | collective-permute-start | bytes 2359304 | tf_op jit(solution)/shard_map/ppermute | solution.py:1043
  133.3 22.0 %collective-permute-start.11 = (bf16[4,384,384]{2,1,0:T(8,128)(2,1)}, bf16[4,384,384]{2,1,0:T(8,128)(2,1)}, u32[]{:S(2)}, u32[]{:S(2)}) collective-permute-start(bf16[4,384,384]{2,1,0:T(8,128)(2,1)} %get-tuple-element.206), channel_id=1, source_target_pairs={{0,8},{1,9},{2,10},{3,11},{4,12},{5,13},{6,14},{7,15},{8,0},{9,1},... | collective-permute-start | bytes 3538952 | tf_op jit(solution)/shard_map/ppermute | solution.py:829
  155.3 15.6 %collective-permute-start.17 = (bf16[2,512,1536]{2,1,0:T(8,128)(2,1)}, bf16[2,512,1536]{2,1,0:T(8,128)(2,1)}, u32[]{:S(2)}, u32[]{:S(2)}) collective-permute-start(bf16[2,512,1536]{2,1,0:T(8,128)(2,1)} %get-tuple-element.223.refs_0_), channel_id=1, source_target_pairs={{0,16},{16,0},{1,17},{17,1},{2,18},{18,2},{3,19},{19,3},{4,20},{20... | collective-permute-start | bytes 9437192 | tf_op jit(solution)/shard_map/ppermute | solution.py:1043
  157.4 47.7 %collective-permute-start.22 = (bf16[512,768]{1,0:T(8,128)(2,1)}, bf16[512,768]{1,0:T(8,128)(2,1)}, u32[]{:S(2)}, u32[]{:S(2)}) collective-permute-start(bf16[512,768]{1,0:T(8,128)(2,1)} %get-tuple-element.235), channel_id=1, source_target_pairs={{0,16},{16,0},{1,17},{17,1},{2,18},{18,2},{3,19},{19,3},{4,20},{20... | collective-permute-start | bytes 2359304 | tf_op jit(solution)/shard_map/ppermute | solution.py:1043
  157.6 95.2 %collective-permute-start.28 = (bf16[512,768]{1,0:T(8,128)(2,1)}, bf16[512,768]{1,0:T(8,128)(2,1)}, u32[]{:S(2)}, u32[]{:S(2)}) collective-permute-start(bf16[512,768]{1,0:T(8,128)(2,1)} %get-tuple-element.227.att), channel_id=1, source_target_pairs={{0,16},{16,0},{1,17},{17,1},{2,18},{18,2},{3,19},{19,3},{4,20},{20... | collective-permute-start | bytes 2359304 | tf_op jit(solution)/shard_map/ppermute | solution.py:1043
  158.0 15.5 %collective-permute-start.18 = (bf16[512,768]{1,0:T(8,128)(2,1)S(1)}, bf16[512,768]{1,0:T(8,128)(2,1)S(1)}, u32[]{:S(2)}, u32[]{:S(2)}) collective-permute-start(bf16[512,768]{1,0:T(8,128)(2,1)S(1)} %copy-done.2), channel_id=1, source_target_pairs={{0,16},{16,0},{1,17},{17,1},{2,18},{18,2},{3,19},{19,3},{4,20},{20... | collective-permute-start | bytes 2359304 | tf_op jit(solution)/shard_map/ppermute | solution.py:1002
  168.7 37.7 %collective-permute-start.23 = (bf16[512,2304]{1,0:T(8,128)(2,1)}, bf16[512,2304]{1,0:T(8,128)(2,1)}, u32[]{:S(2)}, u32[]{:S(2)}) collective-permute-start(bf16[512,2304]{1,0:T(8,128)(2,1)} %get-tuple-element.215), channel_id=1, source_target_pairs={{0,16},{16,0},{1,17},{17,1},{2,18},{18,2},{3,19},{19,3},{4,20},{20... | collective-permute-start | bytes 7077896 | tf_op jit(solution)/shard_map/ppermute | solution.py:1002
  170.9 31.4 %collective-permute-start.21 = (bf16[768,384]{1,0:T(8,128)(2,1)}, bf16[768,384]{1,0:T(8,128)(2,1)}, u32[]{:S(2)}, u32[]{:S(2)}) collective-permute-start(bf16[768,384]{1,0:T(8,128)(2,1)} %fusion.7), channel_id=1, source_target_pairs={{0,4},{1,5},{2,6},{3,7},{4,0},{5,1},{6,2},{7,3},{8,12},{9,13},{10,... | collective-permute-start | bytes 1769480 | tf_op jit(solution)/shard_map/ppermute | solution.py:829
  181.6 19.4 %collective-permute-start.19 = (bf16[4,384,384]{2,1,0:T(8,128)(2,1)}, bf16[4,384,384]{2,1,0:T(8,128)(2,1)}, u32[]{:S(2)}, u32[]{:S(2)}) collective-permute-start(bf16[4,384,384]{2,1,0:T(8,128)(2,1)} %get-tuple-element.224), channel_id=1, source_target_pairs={{0,8},{1,9},{2,10},{3,11},{4,12},{5,13},{6,14},{7,15},{8,0},{9,1},... | collective-permute-start | bytes 3538952 | tf_op jit(solution)/shard_map/ppermute | solution.py:829
  201.0 50.8 %collective-permute-start.26 = (bf16[512,768]{1,0:T(8,128)(2,1)}, bf16[512,768]{1,0:T(8,128)(2,1)}, u32[]{:S(2)}, u32[]{:S(2)}) collective-permute-start(bf16[512,768]{1,0:T(8,128)(2,1)} %get-tuple-element.246), channel_id=1, source_target_pairs={{0,16},{16,0},{1,17},{17,1},{2,18},{18,2},{3,19},{19,3},{4,20},{20... | collective-permute-start | bytes 2359304 | tf_op jit(solution)/shard_map/ppermute | solution.py:1043
  202.3 48.0 %collective-permute-start.25 = (bf16[5,384,384]{2,1,0:T(8,128)(2,1)}, bf16[5,384,384]{2,1,0:T(8,128)(2,1)}, u32[]{:S(2)}, u32[]{:S(2)}) collective-permute-start(bf16[5,384,384]{2,1,0:T(8,128)(2,1)} %get-tuple-element.220), channel_id=1, source_target_pairs={{0,1},{1,0},{2,3},{3,2},{4,5},{5,4},{6,7},{7,6},{8,9},{9,8},{10,11... | collective-permute-start | bytes 4423688 | tf_op jit(solution)/shard_map/ppermute | solution.py:829
  205.1 49.7 %collective-permute-start.27 = (bf16[512,3072]{1,0:T(8,128)(2,1)}, bf16[512,3072]{1,0:T(8,128)(2,1)}, u32[]{:S(2)}, u32[]{:S(2)}) collective-permute-start(bf16[512,3072]{1,0:T(8,128)(2,1)} %get-tuple-element.231), channel_id=1, source_target_pairs={{0,16},{16,0},{1,17},{17,1},{2,18},{18,2},{3,19},{19,3},{4,20},{20... | collective-permute-start | bytes 9437192 | tf_op jit(solution)/shard_map/ppermute | solution.py:1002
  206.4 21.9 %collective-permute-start.20 = (bf16[768,384]{1,0:T(8,128)(2,1)S(1)}, bf16[768,384]{1,0:T(8,128)(2,1)S(1)}, u32[]{:S(2)}, u32[]{:S(2)}) collective-permute-start(bf16[768,384]{1,0:T(8,128)(2,1)S(1)} %fusion.11), channel_id=1, source_target_pairs={{0,1},{1,0},{2,3},{3,2},{4,5},{5,4},{6,7},{7,6},{8,9},{9,8},{10,11... | collective-permute-start | bytes 1769480 | tf_op jit(solution)/shard_map/ppermute | solution.py:829
  232.9 20.9 %collective-permute-start.29 = (bf16[512,768]{1,0:T(8,128)(2,1)}, bf16[512,768]{1,0:T(8,128)(2,1)}, u32[]{:S(2)}, u32[]{:S(2)}) collective-permute-start(bf16[512,768]{1,0:T(8,128)(2,1)} %get-tuple-element.247), channel_id=1, source_target_pairs={{0,16},{16,0},{1,17},{17,1},{2,18},{18,2},{3,19},{19,3},{4,20},{20... | collective-permute-start | bytes 2359304 | tf_op jit(solution)/shard_map/ppermute | solution.py:1002
  250.3 37.2 %collective-permute-start.34 = (bf16[512,768]{1,0:T(8,128)(2,1)}, bf16[512,768]{1,0:T(8,128)(2,1)}, u32[]{:S(2)}, u32[]{:S(2)}) collective-permute-start(bf16[512,768]{1,0:T(8,128)(2,1)} %get-tuple-element.254), channel_id=1, source_target_pairs={{0,16},{16,0},{1,17},{17,1},{2,18},{18,2},{3,19},{19,3},{4,20},{20... | collective-permute-start | bytes 2359304 | tf_op jit(solution)/shard_map/ppermute | solution.py:1043
  251.8 46.0 %collective-permute-start.31 = (bf16[3,384,384]{2,1,0:T(8,128)(2,1)}, bf16[3,384,384]{2,1,0:T(8,128)(2,1)}, u32[]{:S(2)}, u32[]{:S(2)}) collective-permute-start(bf16[3,384,384]{2,1,0:T(8,128)(2,1)} %get-tuple-element.236), channel_id=1, source_target_pairs={{0,4},{1,5},{2,6},{3,7},{4,0},{5,1},{6,2},{7,3},{8,12},{9,13},{10,... | collective-permute-start | bytes 2654216 | tf_op jit(solution)/shard_map/ppermute | solution.py:829
  252.7 23.5 %collective-permute-start.33 = (bf16[768,384]{1,0:T(8,128)(2,1)S(1)}, bf16[768,384]{1,0:T(8,128)(2,1)}, u32[]{:S(2)}, u32[]{:S(2)}) collective-permute-start(bf16[768,384]{1,0:T(8,128)(2,1)S(1)} %copy-done.10), channel_id=1, source_target_pairs={{0,2},{1,3},{2,0},{3,1},{4,6},{5,7},{6,4},{7,5},{8,10},{9,11},{10,... | collective-permute-start | bytes 1769480 | tf_op jit(solution)/shard_map/ppermute | solution.py:829
  253.8 30.3 %collective-permute-start.32 = (bf16[960,384]{1,0:T(8,128)(2,1)S(1)}, bf16[960,384]{1,0:T(8,128)(2,1)S(1)}, u32[]{:S(2)}, u32[]{:S(2)}) collective-permute-start(bf16[960,384]{1,0:T(8,128)(2,1)S(1)} %fusion), channel_id=1, source_target_pairs={{0,2},{1,3},{2,0},{3,1},{4,6},{5,7},{6,4},{7,5},{8,10},{9,11},{10,... | collective-permute-start | bytes 2211848 | tf_op jit(solution)/shard_map/ppermute | solution.py:829
  254.8 36.2 %collective-permute-start.35 = (bf16[512,2304]{1,0:T(8,128)(2,1)}, bf16[512,2304]{1,0:T(8,128)(2,1)}, u32[]{:S(2)}, u32[]{:S(2)}) collective-permute-start(bf16[512,2304]{1,0:T(8,128)(2,1)} %get-tuple-element.258.d_proj), channel_id=1, source_target_pairs={{0,16},{16,0},{1,17},{17,1},{2,18},{18,2},{3,19},{19,3},{4,20},{20... | collective-permute-start | bytes 7077896 | tf_op jit(solution)/shard_map/ppermute | solution.py:1002
  276.2 42.6 %collective-permute-start.37 = (bf16[768,384]{1,0:T(8,128)(2,1)}, bf16[768,384]{1,0:T(8,128)(2,1)}, u32[]{:S(2)}, u32[]{:S(2)}) collective-permute-start(bf16[768,384]{1,0:T(8,128)(2,1)} %add.227), channel_id=1, source_target_pairs={{0,2},{1,3},{2,0},{3,1},{4,6},{5,7},{6,4},{7,5},{8,10},{9,11},{10,... | collective-permute-start | bytes 1769480 | tf_op jit(solution)/shard_map/ppermute | solution.py:829
  284.1 20.9 %collective-permute-start.30 = (bf16[5,384,384]{2,1,0:T(8,128)(2,1)}, bf16[5,384,384]{2,1,0:T(8,128)(2,1)S(1)}, u32[]{:S(2)}, u32[]{:S(2)}) collective-permute-start(bf16[5,384,384]{2,1,0:T(8,128)(2,1)} %get-tuple-element.249), channel_id=1, source_target_pairs={{0,1},{1,0},{2,3},{3,2},{4,5},{5,4},{6,7},{7,6},{8,9},{9,8},{10,11... | collective-permute-start | bytes 4423688 | tf_op jit(solution)/shard_map/ppermute | solution.py:829
  287.5 48.6 %collective-permute-start.41 = (bf16[768,384]{1,0:T(8,128)(2,1)}, bf16[768,384]{1,0:T(8,128)(2,1)}, u32[]{:S(2)}, u32[]{:S(2)}) collective-permute-start(bf16[768,384]{1,0:T(8,128)(2,1)} %add.234), channel_id=1, source_target_pairs={{0,4},{1,5},{2,6},{3,7},{4,0},{5,1},{6,2},{7,3},{8,12},{9,13},{10,... | collective-permute-start | bytes 1769480 | tf_op jit(solution)/shard_map/ppermute | solution.py:829
  290.9 75.4 %collective-permute-start.46 = (bf16[960,384]{1,0:T(8,128)(2,1)}, bf16[960,384]{1,0:T(8,128)(2,1)}, u32[]{:S(2)}, u32[]{:S(2)}) collective-permute-start(bf16[960,384]{1,0:T(8,128)(2,1)} %fusion.2), channel_id=1, source_target_pairs={{0,4},{1,5},{2,6},{3,7},{4,0},{5,1},{6,2},{7,3},{8,12},{9,13},{10,... | collective-permute-start | bytes 2211848 | tf_op jit(solution)/shard_map/ppermute | solution.py:829
  297.8 25.1 %collective-permute-start.38 = (bf16[3,384,384]{2,1,0:T(8,128)(2,1)}, bf16[3,384,384]{2,1,0:T(8,128)(2,1)}, u32[]{:S(2)}, u32[]{:S(2)}) collective-permute-start(bf16[3,384,384]{2,1,0:T(8,128)(2,1)} %get-tuple-element.255), channel_id=1, source_target_pairs={{0,8},{1,9},{2,10},{3,11},{4,12},{5,13},{6,14},{7,15},{8,0},{9,1},... | collective-permute-start | bytes 2654216 | tf_op jit(solution)/shard_map/ppermute | solution.py:829
  305.0 21.9 %collective-permute-start.39 = (bf16[576,384]{1,0:T(8,128)(2,1)}, bf16[576,384]{1,0:T(8,128)(2,1)}, u32[]{:S(2)}, u32[]{:S(2)}) collective-permute-start(bf16[576,384]{1,0:T(8,128)(2,1)} %fusion.12), channel_id=1, source_target_pairs={{0,8},{1,9},{2,10},{3,11},{4,12},{5,13},{6,14},{7,15},{8,0},{9,1},... | collective-permute-start | bytes 1327112 | tf_op jit(solution)/shard_map/ppermute | solution.py:829
  318.8 13.2 %collective-permute-start.40 = (bf16[960,384]{1,0:T(8,128)(2,1)}, bf16[960,384]{1,0:T(8,128)(2,1)}, u32[]{:S(2)}, u32[]{:S(2)}) collective-permute-start(bf16[960,384]{1,0:T(8,128)(2,1)} %fusion.3), channel_id=1, source_target_pairs={{0,8},{1,9},{2,10},{3,11},{4,12},{5,13},{6,14},{7,15},{8,0},{9,1},... | collective-permute-start | bytes 2211848 | tf_op jit(solution)/shard_map/ppermute | solution.py:829
  322.9 16.6 %collective-permute-start.42 = (bf16[768,384]{1,0:T(8,128)(2,1)}, bf16[768,384]{1,0:T(8,128)(2,1)}, u32[]{:S(2)}, u32[]{:S(2)}) collective-permute-start(bf16[768,384]{1,0:T(8,128)(2,1)} %add.238), channel_id=1, source_target_pairs={{0,1},{1,0},{2,3},{3,2},{4,5},{5,4},{6,7},{7,6},{8,9},{9,8},{10,11... | collective-permute-start | bytes 1769480 | tf_op jit(solution)/shard_map/ppermute | solution.py:829
  326.9 16.0 %collective-permute-start.36 = (bf16[512,768]{1,0:T(8,128)(2,1)}, bf16[512,768]{1,0:T(8,128)(2,1)}, u32[]{:S(2)}, u32[]{:S(2)}) collective-permute-start(bf16[512,768]{1,0:T(8,128)(2,1)} %broadcast_select_fusion), channel_id=1, source_target_pairs={{0,16},{16,0},{1,17},{17,1},{2,18},{18,2},{3,19},{19,3},{4,20},{20... | collective-permute-start | bytes 2359304 | tf_op jit(solution)/shard_map/ppermute | solution.py:1048
  332.0 16.3 %collective-permute-start.43 = (bf16[576,384]{1,0:T(8,128)(2,1)}, bf16[576,384]{1,0:T(8,128)(2,1)}, u32[]{:S(2)}, u32[]{:S(2)}) collective-permute-start(bf16[576,384]{1,0:T(8,128)(2,1)} %fusion.15), channel_id=1, source_target_pairs={{0,1},{1,0},{2,3},{3,2},{4,5},{5,4},{6,7},{7,6},{8,9},{9,8},{10,11... | collective-permute-start | bytes 1327112 | tf_op jit(solution)/shard_map/ppermute | solution.py:829
  336.1 37.0 %collective-permute-start.48 = (bf16[576,384]{1,0:T(8,128)(2,1)}, bf16[576,384]{1,0:T(8,128)(2,1)}, u32[]{:S(2)}, u32[]{:S(2)}) collective-permute-start(bf16[576,384]{1,0:T(8,128)(2,1)} %fusion.13), channel_id=1, source_target_pairs={{0,1},{1,0},{2,3},{3,2},{4,5},{5,4},{6,7},{7,6},{8,9},{9,8},{10,11... | collective-permute-start | bytes 1327112 | tf_op jit(solution)/shard_map/ppermute | solution.py:829
  339.5 15.9 %collective-permute-start.44 = (bf16[768,384]{1,0:T(8,128)(2,1)}, bf16[768,384]{1,0:T(8,128)(2,1)}, u32[]{:S(2)}, u32[]{:S(2)}) collective-permute-start(bf16[768,384]{1,0:T(8,128)(2,1)} %add.245), channel_id=1, source_target_pairs={{0,1},{1,0},{2,3},{3,2},{4,5},{5,4},{6,7},{7,6},{8,9},{9,8},{10,11... | collective-permute-start | bytes 1769480 | tf_op jit(solution)/shard_map/ppermute | solution.py:829
  342.9 20.0 %collective-permute-start.45 = (bf16[960,384]{1,0:T(8,128)(2,1)}, bf16[960,384]{1,0:T(8,128)(2,1)}, u32[]{:S(2)}, u32[]{:S(2)}) collective-permute-start(bf16[960,384]{1,0:T(8,128)(2,1)} %fusion.5), channel_id=1, source_target_pairs={{0,2},{1,3},{2,0},{3,1},{4,6},{5,7},{6,4},{7,5},{8,10},{9,11},{10,... | collective-permute-start | bytes 2211848 | tf_op jit(solution)/shard_map/ppermute | solution.py:829
  348.4 24.6 %collective-permute-start.47 = (bf16[4,384,384]{2,1,0:T(8,128)(2,1)}, bf16[4,384,384]{2,1,0:T(8,128)(2,1)}, u32[]{:S(2)}, u32[]{:S(2)}) collective-permute-start(bf16[4,384,384]{2,1,0:T(8,128)(2,1)} %bitcast.73.refs_4_), channel_id=1, source_target_pairs={{0,8},{1,9},{2,10},{3,11},{4,12},{5,13},{6,14},{7,15},{8,0},{9,1},... | collective-permute-start | bytes 3538952 | tf_op jit(solution)/shard_map/ppermute | solution.py:829
  355.4 85.2 %collective-permute-start.59 = (bf16[4,384,384]{2,1,0:T(8,128)(2,1)}, bf16[4,384,384]{2,1,0:T(8,128)(2,1)}, u32[]{:S(2)}, u32[]{:S(2)}) collective-permute-start(bf16[4,384,384]{2,1,0:T(8,128)(2,1)} %bitcast.73.refs_4_), channel_id=1, source_target_pairs={{0,16},{16,0},{1,17},{17,1},{2,18},{18,2},{3,19},{19,3},{4,20},{20... | collective-permute-start | bytes 3538952 | tf_op jit(solution)/shard_map/ppermute | solution.py:938
  362.9 13.5 %collective-permute-start.49 = (bf16[576,384]{1,0:T(8,128)(2,1)}, bf16[576,384]{1,0:T(8,128)(2,1)}, u32[]{:S(2)}, u32[]{:S(2)}) collective-permute-start(bf16[576,384]{1,0:T(8,128)(2,1)} %add.246), channel_id=1, source_target_pairs={{0,2},{1,3},{2,0},{3,1},{4,6},{5,7},{6,4},{7,5},{8,10},{9,11},{10,... | collective-permute-start | bytes 1327112 | tf_op jit(solution)/shard_map/ppermute | solution.py:829
  366.3 18.8 %collective-permute-start.50 = (bf16[4,384,384]{2,1,0:T(8,128)(2,1)}, bf16[4,384,384]{2,1,0:T(8,128)(2,1)}, u32[]{:S(2)}, u32[]{:S(2)}) collective-permute-start(bf16[4,384,384]{2,1,0:T(8,128)(2,1)} %bitcast.76.refs_0_), channel_id=1, source_target_pairs={{0,8},{1,9},{2,10},{3,11},{4,12},{5,13},{6,14},{7,15},{8,0},{9,1},... | collective-permute-start | bytes 3538952 | tf_op jit(solution)/shard_map/ppermute | solution.py:829
  373.0 69.6 %collective-permute-start.61 = (bf16[4,384,384]{2,1,0:T(8,128)(2,1)}, bf16[4,384,384]{2,1,0:T(8,128)(2,1)}, u32[]{:S(2)}, u32[]{:S(2)}) collective-permute-start(bf16[4,384,384]{2,1,0:T(8,128)(2,1)} %bitcast.76.refs_0_), channel_id=1, source_target_pairs={{0,16},{16,0},{1,17},{17,1},{2,18},{18,2},{3,19},{19,3},{4,20},{20... | collective-permute-start | bytes 3538952 | tf_op jit(solution)/shard_map/ppermute | solution.py:938
  373.2 20.0 %collective-permute-start.51 = (bf16[960,384]{1,0:T(8,128)(2,1)}, bf16[960,384]{1,0:T(8,128)(2,1)}, u32[]{:S(2)}, u32[]{:S(2)}) collective-permute-start(bf16[960,384]{1,0:T(8,128)(2,1)} %add.248), channel_id=1, source_target_pairs={{0,8},{1,9},{2,10},{3,11},{4,12},{5,13},{6,14},{7,15},{8,0},{9,1},... | collective-permute-start | bytes 2211848 | tf_op jit(solution)/shard_map/ppermute | solution.py:829
  376.4 24.7 %collective-permute-start.52 = (bf16[960,384]{1,0:T(8,128)(2,1)}, bf16[960,384]{1,0:T(8,128)(2,1)}, u32[]{:S(2)}, u32[]{:S(2)}) collective-permute-start(bf16[960,384]{1,0:T(8,128)(2,1)} %add.247), channel_id=1, source_target_pairs={{0,4},{1,5},{2,6},{3,7},{4,0},{5,1},{6,2},{7,3},{8,12},{9,13},{10,... | collective-permute-start | bytes 2211848 | tf_op jit(solution)/shard_map/ppermute | solution.py:829
  385.1 25.3 %collective-permute-start.53 = (bf16[576,384]{1,0:T(8,128)(2,1)}, bf16[576,384]{1,0:T(8,128)(2,1)}, u32[]{:S(2)}, u32[]{:S(2)}) collective-permute-start(bf16[576,384]{1,0:T(8,128)(2,1)} %fusion.17), channel_id=1, source_target_pairs={{0,4},{1,5},{2,6},{3,7},{4,0},{5,1},{6,2},{7,3},{8,12},{9,13},{10,... | collective-permute-start | bytes 1327112 | tf_op jit(solution)/shard_map/ppermute | solution.py:829
  393.2 31.8 %collective-permute-start.55 = (bf16[576,384]{1,0:T(8,128)(2,1)}, bf16[576,384]{1,0:T(8,128)(2,1)}, u32[]{:S(2)}, u32[]{:S(2)}) collective-permute-start(bf16[576,384]{1,0:T(8,128)(2,1)} %add.251), channel_id=1, source_target_pairs={{0,8},{1,9},{2,10},{3,11},{4,12},{5,13},{6,14},{7,15},{8,0},{9,1},... | collective-permute-start | bytes 1327112 | tf_op jit(solution)/shard_map/ppermute | solution.py:829
  401.1 41.2 %collective-permute-start.58 = (bf16[4,384,384]{2,1,0:T(8,128)(2,1)}, bf16[4,384,384]{2,1,0:T(8,128)(2,1)}, u32[]{:S(2)}, u32[]{:S(2)}) collective-permute-start(bf16[4,384,384]{2,1,0:T(8,128)(2,1)} %collective-permute-done.47.refs_5_), channel_id=1, source_target_pairs={{0,16},{16,0},{1,17},{17,1},{2,18},{18,2},{3,19},{19,3},{4,20},{20... | collective-permute-start | bytes 3538952 | tf_op jit(solution)/shard_map/ppermute | solution.py:938
  410.4 11.8 %collective-permute-start.54 = (bf16[960,384]{1,0:T(8,128)(2,1)}, bf16[960,384]{1,0:T(8,128)(2,1)}, u32[]{:S(2)}, u32[]{:S(2)}) collective-permute-start(bf16[960,384]{1,0:T(8,128)(2,1)} %add.252), channel_id=1, source_target_pairs={{0,2},{1,3},{2,0},{3,1},{4,6},{5,7},{6,4},{7,5},{8,10},{9,11},{10,... | collective-permute-start | bytes 2211848 | tf_op jit(solution)/shard_map/ppermute | solution.py:829
  422.2 11.8 %collective-permute-start.56 = (bf16[960,384]{1,0:T(8,128)(2,1)}, bf16[960,384]{1,0:T(8,128)(2,1)}, u32[]{:S(2)}, u32[]{:S(2)}) collective-permute-start(bf16[960,384]{1,0:T(8,128)(2,1)} %add.253), channel_id=1, source_target_pairs={{0,8},{1,9},{2,10},{3,11},{4,12},{5,13},{6,14},{7,15},{8,0},{9,1},... | collective-permute-start | bytes 2211848 | tf_op jit(solution)/shard_map/ppermute | solution.py:829
  425.0 13.3 %collective-permute-start.57 = (bf16[576,384]{1,0:T(8,128)(2,1)}, bf16[576,384]{1,0:T(8,128)(2,1)}, u32[]{:S(2)}, u32[]{:S(2)}) collective-permute-start(bf16[576,384]{1,0:T(8,128)(2,1)} %add.254), channel_id=1, source_target_pairs={{0,2},{1,3},{2,0},{3,1},{4,6},{5,7},{6,4},{7,5},{8,10},{9,11},{10,... | collective-permute-start | bytes 1327112 | tf_op jit(solution)/shard_map/ppermute | solution.py:829
  440.3 11.5 %collective-permute-start.62 = (bf16[576,384]{1,0:T(8,128)(2,1)}, bf16[576,384]{1,0:T(8,128)(2,1)}, u32[]{:S(2)}, u32[]{:S(2)}) collective-permute-start(bf16[576,384]{1,0:T(8,128)(2,1)} %add.255), channel_id=1, source_target_pairs={{0,1},{1,0},{2,3},{3,2},{4,5},{5,4},{6,7},{7,6},{8,9},{9,8},{10,11... | collective-permute-start | bytes 1327112 | tf_op jit(solution)/shard_map/ppermute | solution.py:829
  440.5 24.4 %collective-permute-start.63 = (bf16[5,384,384]{2,1,0:T(8,128)(2,1)}, bf16[5,384,384]{2,1,0:T(8,128)(2,1)}, u32[]{:S(2)}, u32[]{:S(2)}) collective-permute-start(bf16[5,384,384]{2,1,0:T(8,128)(2,1)} %bitcast.80.refs_4_), channel_id=1, source_target_pairs={{0,1},{1,0},{2,3},{3,2},{4,5},{5,4},{6,7},{7,6},{8,9},{9,8},{10,11... | collective-permute-start | bytes 4423688 | tf_op jit(solution)/shard_map/ppermute | solution.py:829
  442.3 47.3 %collective-permute-start.64 = (bf16[5,384,384]{2,1,0:T(8,128)(2,1)}, bf16[5,384,384]{2,1,0:T(8,128)(2,1)}, u32[]{:S(2)}, u32[]{:S(2)}) collective-permute-start(bf16[5,384,384]{2,1,0:T(8,128)(2,1)} %bitcast.86.refs_0_), channel_id=1, source_target_pairs={{0,1},{1,0},{2,3},{3,2},{4,5},{5,4},{6,7},{7,6},{8,9},{9,8},{10,11... | collective-permute-start | bytes 4423688 | tf_op jit(solution)/shard_map/ppermute | solution.py:829
  442.6 49.4 %collective-permute-start.65 = (bf16[3,384,384]{2,1,0:T(8,128)(2,1)}, bf16[3,384,384]{2,1,0:T(8,128)(2,1)}, u32[]{:S(2)}, u32[]{:S(2)}) collective-permute-start(bf16[3,384,384]{2,1,0:T(8,128)(2,1)} %bitcast.83.refs_4_), channel_id=1, source_target_pairs={{0,4},{1,5},{2,6},{3,7},{4,0},{5,1},{6,2},{7,3},{8,12},{9,13},{10,... | collective-permute-start | bytes 2654216 | tf_op jit(solution)/shard_map/ppermute | solution.py:829
  444.2 47.8 %collective-permute-start.67 = (bf16[5,384,384]{2,1,0:T(8,128)(2,1)}, bf16[5,384,384]{2,1,0:T(8,128)(2,1)}, u32[]{:S(2)}, u32[]{:S(2)}) collective-permute-start(bf16[5,384,384]{2,1,0:T(8,128)(2,1)} %bitcast.80.refs_4_), channel_id=1, source_target_pairs={{0,16},{16,0},{1,17},{17,1},{2,18},{18,2},{3,19},{19,3},{4,20},{20... | collective-permute-start | bytes 4423688 | tf_op jit(solution)/shard_map/ppermute | solution.py:938
  451.8 44.0 %collective-permute-start.69 = (bf16[5,384,384]{2,1,0:T(8,128)(2,1)}, bf16[5,384,384]{2,1,0:T(8,128)(2,1)}, u32[]{:S(2)}, u32[]{:S(2)}) collective-permute-start(bf16[5,384,384]{2,1,0:T(8,128)(2,1)} %bitcast.86.refs_0_), channel_id=1, source_target_pairs={{0,16},{16,0},{1,17},{17,1},{2,18},{18,2},{3,19},{19,3},{4,20},{20... | collective-permute-start | bytes 4423688 | tf_op jit(solution)/shard_map/ppermute | solution.py:938
  464.9 38.4 %collective-permute-start.71 = (bf16[3,384,384]{2,1,0:T(8,128)(2,1)}, bf16[3,384,384]{2,1,0:T(8,128)(2,1)}, u32[]{:S(2)}, u32[]{:S(2)}) collective-permute-start(bf16[3,384,384]{2,1,0:T(8,128)(2,1)} %bitcast.83.refs_4_), channel_id=1, source_target_pairs={{0,16},{16,0},{1,17},{17,1},{2,18},{18,2},{3,19},{19,3},{4,20},{20... | collective-permute-start | bytes 2654216 | tf_op jit(solution)/shard_map/ppermute | solution.py:938
  489.6 13.7 %collective-permute-start.72 = (bf16[3,384,384]{2,1,0:T(8,128)(2,1)}, bf16[3,384,384]{2,1,0:T(8,128)(2,1)}, u32[]{:S(2)}, u32[]{:S(2)}) collective-permute-start(bf16[3,384,384]{2,1,0:T(8,128)(2,1)} %bitcast.90.refs_0_), channel_id=1, source_target_pairs={{0,8},{1,9},{2,10},{3,11},{4,12},{5,13},{6,14},{7,15},{8,0},{9,1},... | collective-permute-start | bytes 2654216 | tf_op jit(solution)/shard_map/ppermute | solution.py:829
  492.0 19.1 %collective-permute-start.74 = (bf16[3,384,384]{2,1,0:T(8,128)(2,1)}, bf16[3,384,384]{2,1,0:T(8,128)(2,1)}, u32[]{:S(2)}, u32[]{:S(2)}) collective-permute-start(bf16[3,384,384]{2,1,0:T(8,128)(2,1)} %bitcast.90.refs_0_), channel_id=1, source_target_pairs={{0,16},{16,0},{1,17},{17,1},{2,18},{18,2},{3,19},{19,3},{4,20},{20... | collective-permute-start | bytes 2654216 | tf_op jit(solution)/shard_map/ppermute | solution.py:938
  (41 other events, 300.1 us)
Sparse Core Ops, SparseCore 0:
  343.0 128.6 all-reduce.1

commit v3 on v2

--- a/solution.py
+++ b/solution.py
@@ -18,7 +18,7 @@
 GROUP = 4
 GV = GROUP * HEAD
 GF = GROUP * FEATS
-FCHUNK = 512
+FCHUNK = 768
 COST = 30
 
 

time: 537 us -> 533 us (level)
  transfers between devices with their start and end apart: 76 -> 76, of which waited for: 18 -> 20; matrix products, arithmetic and copies ran while one was open for 15% -> 15% of each run, Pallas kernels for 35% -> 34%
where the time goes in v3:
time: 533 us; the launch traced here: 525 us
  Pallas kernels  232 us (44%)
  waiting for transfers between devices  110 us (21%)
  starting transfers between devices  78.1 us (15%)
  other arithmetic  77 us (14%)
  between operations  17.1 us (3%)
  local copies, waits for them, and re-layouts  11.5 us (2%)
    ppermute x36, waiting for transfers between devices, swap(): return lax.ppermute(value, ('section', 'row', 'wide'), pairs)  102 us
    ppermute x36, starting transfers between devices, swap(): return lax.ppermute(value, ('section', 'row', 'wide'), pairs)  53.4 us
    pallas_call x6, Pallas kernels, weight_grad(): pl.pallas_call(partial(weight_grad_kernel, sizes=sizes, dims=dims), out_s...  46.8 us
    pallas_call x2, Pallas kernels, forward_outputs(): pl.pallas_call(partial(outputs_kernel, layer=layer), out_shape=[jax.Shape...  39.5 us
    add x18, other arithmetic, add(): return parts[0] + parts[1]  39.2 us
    pallas_call x2, Pallas kernels, attention_back(): pl.pallas_call(partial(attention_back_kernel, layer=layer), out_shape=sha...  38.1 us
    pallas_call x2, Pallas kernels, ffn_back(): pl.pallas_call(partial(ffn_back_kernel, layer=layer), out_shape=[jax.Shap...  33.7 us
    pallas_call x4, Pallas kernels, finish(): pl.pallas_call(partial(finish_kernel, dims=dims), out_shape=jax.ShapeDtyp...  25.5 us
  transfers between devices with their start and end apart: 76, of which 20 were waited for; matrix products, arithmetic and copies ran while one was open for 15% of the time, Pallas kernels for 34%

profile of v3, /device:TPU:0, one launch (start us, length us, event | category | flops | bytes accessed | tf_op | source)
XLA Modules:
  0.0 525.3 jit_solution(12788986579301732130)
XLA Ops:
  18.8 10.9 %attention_inputs.2 = (bf16[512,768]{1,0:T(8,128)(2,1)}, f32[2,512,768]{2,1,0:T(8,128)}, bf16[2,512,384]{2,1,0:T(8,128)(2,1)}, bf16[512,768]{1,0:T(8,128)(2,1)}, bf16[32,1536]{1,0:T(8,128)(2,1)}) custom-call(s32[7]{0:T(128)} %concatenate.6.sc, bf16[2,512,768]{2,1,0:T(8,128)(2,1)} %x.5, f32[1,9984]{1,0:T(1,128)} %get-tuple-element.381.gain.bias.bq.bo.g2.b2.bu.bd, ...), custom_call_target="tpu_custom_call" | custom-call | flops 181193932800 | bytes 294912000 | tf_op jit(solution)/shard_map/attention_inputs/pallas_call | solution.py:219
  29.7 3.0 collective-permute-start.3
  32.7 7.1 %own_half.2 = (f32[512,768]{1,0:T(8,128)}, f32[512,768]{1,0:T(8,128)}) custom-call(bf16[2,512,384]{2,1,0:T(8,128)(2,1)} %get-tuple-element.186.fq.fk.f, bf16[2,512,384]{2,1,0:T(8,128)(2,1)} %get-tuple-element.186.fq.fk.f, bf16[512,768]{1,0:T(8,128)(2,1)} %get-tuple-element.187.vals, s32[512,1]{1,0:T(8,128)} %copy.73.idc, s32[1,512]{1,0:T(1,128)} %dynamic_slice.90.idr), custom_call_target="tpu_custom_call" | custom-call | flops 96636764160 | bytes 141557760 | tf_op jit(solution)/shard_map/own_half/pallas_call | solution.py:291
  40.5 19.6 %attention_out_and_ffn.2 = (bf16[512,768]{1,0:T(8,128)(2,1)}, f32[512,768]{1,0:T(8,128)}, f32[512,768]{1,0:T(8,128)}, bf16[512,768]{1,0:T(8,128)(2,1)}, bf16[2,5...) custom-call(s32[7]{0:T(128)} %concatenate.6.sc, f32[512,768]{1,0:T(8,128)} %get-tuple-element.188.num, ...), custom_call_target="tpu_custom_call" | custom-call | flops 163074539520 | bytes 754974720 | tf_op jit(solution)/shard_map/attention_out_and_ffn/pallas_call | solution.py:392
  60.1 11.1 %attention_inputs.3 = (bf16[512,768]{1,0:T(8,128)(2,1)}, f32[2,512,768]{2,1,0:T(8,128)}, bf16[2,512,384]{2,1,0:T(8,128)(2,1)}, bf16[512,768]{1,0:T(8,128)(2,1)}, bf16[32,1536]{1,0:T(8,128)(2,1)}) custom-call(s32[7]{0:T(128)} %concatenate.6.sc, bf16[1,512,768]{2,1,0:T(8,128)(2,1)} %bitcast.145, ...), custom_call_target="tpu_custom_call" | custom-call | flops 181193932800 | bytes 294912000 | tf_op jit(solution)/shard_map/attention_inputs/pallas_call | solution.py:219
  71.3 7.1 %own_half.3 = (f32[512,768]{1,0:T(8,128)}, f32[512,768]{1,0:T(8,128)}) custom-call(bf16[2,512,384]{2,1,0:T(8,128)(2,1)} %get-tuple-element.192.fq.fk.f, bf16[2,512,384]{2,1,0:T(8,128)(2,1)} %get-tuple-element.192.fq.fk.f, bf16[512,768]{1,0:T(8,128)(2,1)} %get-tuple-element.193.vals, s32[512,1]{1,0:T(8,128)} %copy.73.idc, s32[1,512]{1,0:T(1,128)} %dynamic_slice.90.idr), custom_call_target="tpu_custom_call" | custom-call | flops 96636764160 | bytes 141557760 | tf_op jit(solution)/shard_map/own_half/pallas_call | solution.py:291
  79.1 19.9 %attention_out_and_ffn.3 = (bf16[512,768]{1,0:T(8,128)(2,1)}, f32[512,768]{1,0:T(8,128)}, f32[512,768]{1,0:T(8,128)}, bf16[512,768]{1,0:T(8,128)(2,1)}, bf16[2,5...) custom-call(s32[7]{0:T(128)} %concatenate.6.sc, f32[512,768]{1,0:T(8,128)} %get-tuple-element.194.num, ...), custom_call_target="tpu_custom_call" | custom-call | flops 163074539520 | bytes 754974720 | tf_op jit(solution)/shard_map/attention_out_and_ffn/pallas_call | solution.py:392
  99.1 2.1 broadcast_select_fusion.2
  101.2 16.9 %ffn_back.2 = (bf16[512,3072]{1,0:T(8,128)(2,1)}, f32[512,768]{1,0:T(8,128)}, bf16[512,768]{1,0:T(8,128)(2,1)}, bf16[512,768]{1,0:T(8,128)(2,1)}, bf16[512,768]{...) custom-call(s32[7]{0:T(128)} %concatenate.6.sc, ...), custom_call_target="tpu_custom_call" | custom-call | flops 181193932800 | bytes 754974720 | tf_op jit(solution)/shard_map/ffn_back/pallas_call | solution.py:523
  123.8 7.2 %weight_grad.6 = (bf16[4,384,384]{2,1,0:T(8,128)(2,1)}, bf16[4,384,384]{2,1,0:T(8,128)(2,1)}) custom-call(s32[7]{0:T(128)} %concatenate.6.sc, bf16[2,512,1536]{2,1,0:T(8,128)(2,1)} %get-tuple-element.205.refs_0_, bf16[2,512,1536]{2,1,0:T(8,128)(2,1)} %collective-permute-done.9.refs_1_, bf16[2,512,768]{2,1,0:T(8,128)(2,1)} %refs_3_.3, ...), custom_call_target="tpu_custom_call" | custom-call | flops 72477573120 | bytes 188743680 | tf_op jit(solution)/shard_map/weight_grad/pallas_call | solution.py:787
  131.7 21.3 %attention_back.2 = (bf16[512,2304]{1,0:T(8,128)(2,1)}, f32[1,2304]{1,0:T(1,128)}, bf16[512,768]{1,0:T(8,128)(2,1)}, f32[1,768]{1,0:T(1,128)}, f32[1,768]{1,0:T(1,128)}) custom-call(s32[7]{0:T(128)} %concatenate.6.sc, bf16[2,512,384]{2,1,0:T(8,128)(2,1)} %get-tuple-element.192.fq.fk.f, bf16[512,768]{1,0:T(8,128)(2,1)} %get-tuple-element.193.vals, ...), custom_call_target="tpu_custom_call" | custom-call | flops 289910292480 | bytes 471859200 | tf_op jit(solution)/shard_map/attention_back/pallas_call | solution.py:705
  156.9 9.5 %weight_grad.7 = (bf16[5,384,384]{2,1,0:T(8,128)(2,1)}, bf16[5,384,384]{2,1,0:T(8,128)(2,1)}) custom-call(s32[7]{0:T(128)} %concatenate.6.sc, bf16[1,512,768]{2,1,0:T(8,128)(2,1)} %bitcast.24.refs_0_, bf16[1,512,768]{2,1,0:T(8,128)(2,1)} %bitcast.25.refs_1_, bf16[1,512,3072]{2,1,0:T(8,128)(2,1)} %bitcast.180, bf16[1,512,3072]{2,1,0:T(8,128)(2,1)} %bitcast.27.refs_3_, ...), custom_call_target="tpu_custom_call" | custom-call | flops 90596966400 | bytes 235929600 | tf_op jit(solution)/shard_map/weight_grad/pallas_call | solution.py:787
  166.5 2.1 fusion.7
  168.6 2.6 collective-permute-start.21
  172.1 7.2 %weight_grad.8 = (bf16[4,384,384]{2,1,0:T(8,128)(2,1)}, bf16[4,384,384]{2,1,0:T(8,128)(2,1)}) custom-call(s32[7]{0:T(128)} %concatenate.6.sc, bf16[2,512,1536]{2,1,0:T(8,128)(2,1)} %get-tuple-element.223.refs_0_, bf16[2,512,1536]{2,1,0:T(8,128)(2,1)} %collective-permute-done.17.refs_1_, bf16[1,512,768]{2,1,0:T(8,128)(2,1)} %bitcast.143, ...), custom_call_target="tpu_custom_call" | custom-call | flops 72477573120 | bytes 188743680 | tf_op jit(solution)/shard_map/weight_grad/pallas_call | solution.py:787
  180.7 16.8 %ffn_back.3 = (bf16[512,3072]{1,0:T(8,128)(2,1)}, f32[512,768]{1,0:T(8,128)}, bf16[512,768]{1,0:T(8,128)(2,1)}, bf16[512,768]{1,0:T(8,128)(2,1)}, bf16[512,768]{...) custom-call(s32[7]{0:T(128)} %concatenate.6.sc, ...), custom_call_target="tpu_custom_call" | custom-call | flops 181193932800 | bytes 754974720 | tf_op jit(solution)/shard_map/ffn_back/pallas_call | solution.py:523
  199.4 2.2 add.227
  203.5 6.7 %weight_grad.9 = (bf16[3,384,384]{2,1,0:T(8,128)(2,1)}, bf16[3,384,384]{2,1,0:T(8,128)(2,1)}) custom-call(s32[7]{0:T(128)} %concatenate.6.sc, bf16[1,512,768]{2,1,0:T(8,128)(2,1)} %bitcast.37.refs_0_, bf16[1,512,768]{2,1,0:T(8,128)(2,1)} %bitcast.38.refs_1_, bf16[1,512,2304]{2,1,0:T(8,128)(2,1)} %bitcast.181, bf16[1,512,2304]{2,1,0:T(8,128)(2,1)} %bitcast.40.refs_3_), custom_call_target="tpu_custom_call" | custom-call | flops 54358179840 | bytes 141557760 | tf_op jit(solution)/shard_map/weight_grad/pallas_call | solution.py:787
  210.2 14.7 %collective-permute-done.20 = bf16[768,384]{1,0:T(8,128)(2,1)S(1)} collective-permute-done((bf16[768,384]{1,0:T(8,128)(2,1)S(1)}, bf16[768,384]{1,0:T(8,128)(2,1)S(1)}, u32[]{:S(2)}, u32[]{:S(2)}) %collective-permute-start.20) | collective-permute-done | bytes 589856 | tf_op jit(solution)/shard_map/ppermute | solution.py:829
  225.4 2.1 fusion.10
  230.1 16.8 %attention_back.3 = (bf16[512,2304]{1,0:T(8,128)(2,1)}, f32[1,2304]{1,0:T(1,128)}) custom-call(s32[7]{0:T(128)} %concatenate.6.sc, bf16[2,512,384]{2,1,0:T(8,128)(2,1)} %get-tuple-element.186.fq.fk.f, bf16[512,768]{1,0:T(8,128)(2,1)} %get-tuple-element.187.vals, bf16[512,768]{1,0:T(8,128)(2,1)} %get-tuple-element.238.d_num, ...), custom_call_target="tpu_custom_call" | custom-call | flops 289910292480 | bytes 471859200 | tf_op jit(solution)/shard_map/attention_back/pallas_call | solution.py:705
  251.4 9.4 %weight_grad.10 = (bf16[5,384,384]{2,1,0:T(8,128)(2,1)}, bf16[5,384,384]{2,1,0:T(8,128)(2,1)}) custom-call(s32[7]{0:T(128)} %concatenate.6.sc, bf16[1,512,768]{2,1,0:T(8,128)(2,1)} %bitcast.44.refs_0_, bf16[1,512,768]{2,1,0:T(8,128)(2,1)} %bitcast.45.refs_1_, bf16[1,512,3072]{2,1,0:T(8,128)(2,1)} %bitcast.46.refs_2_, bf16[1,512,3072]{2,1,0:T(8,128)(2,1)} %bitcast.47.refs_3_, ...), custom_call_target="tpu_custom_call" | custom-call | flops 90596966400 | bytes 235929600 | tf_op jit(solution)/shard_map/weight_grad/pallas_call | solution.py:787
  260.8 12.0 %collective-permute-done.33 = bf16[768,384]{1,0:T(8,128)(2,1)} collective-permute-done((bf16[768,384]{1,0:T(8,128)(2,1)S(1)}, bf16[768,384]{1,0:T(8,128)(2,1)}, u32[]{:S(2)}, u32[]{:S(2)}) %collective-permute-start.33) | collective-permute-done | bytes 589856 | tf_op jit(solution)/shard_map/ppermute | solution.py:829
  272.8 2.6 collective-permute-start.37
  275.4 2.0 add.234
  277.4 3.3 collective-permute-done.32
  281.9 2.3 fusion.2
  284.1 3.4 collective-permute-start.41
  287.6 6.8 %weight_grad.11 = (bf16[3,384,384]{2,1,0:T(8,128)(2,1)}, bf16[3,384,384]{2,1,0:T(8,128)(2,1)}) custom-call(s32[7]{0:T(128)} %concatenate.6.sc, bf16[1,512,768]{2,1,0:T(8,128)(2,1)} %bitcast.55.refs_0_, bf16[1,512,768]{2,1,0:T(8,128)(2,1)} %bitcast.56.refs_1_, bf16[1,512,2304]{2,1,0:T(8,128)(2,1)} %bitcast.182, bf16[1,512,2304]{2,1,0:T(8,128)(2,1)} %bitcast.58.refs_3_), custom_call_target="tpu_custom_call" | custom-call | flops 54358179840 | bytes 141557760 | tf_op jit(solution)/shard_map/weight_grad/pallas_call | solution.py:787
  297.5 4.1 collective-permute-done.30
  304.4 8.7 %inputs_back.1 = (bf16[512,768]{1,0:T(8,128)(2,1)}, f32[1,768]{1,0:T(1,128)}, f32[1,768]{1,0:T(1,128)}) custom-call(s32[7]{0:T(128)} %concatenate.6.sc, bf16[512,2304]{1,0:T(8,128)(2,1)} %get-tuple-element.258.d_proj, bf16[2,512,768]{2,1,0:T(8,128)(2,1)} %x.5, f32[1,9984]{1,0:T(1,128)} %get-tuple-element.381.gain.bias.bq.bo.g2.b2.bu.bd, ...), custom_call_target="tpu_custom_call" | custom-call | flops 54358179840 | bytes 188743680 | tf_op jit(solution)/shard_map/inputs_back/pallas_call | solution.py:726
  315.7 2.2 add.238
  319.5 2.1 collective-permute-start.42
  323.5 3.0 collective-permute-start.36
  326.6 2.1 fusion.15
  330.4 2.3 fusion.5
  333.2 2.2 add.245
  339.5 3.0 collective-permute-start.45
  345.0 2.5 collective-permute-start.47
  349.5 2.4 collective-permute-done.44
  351.9 4.8 collective-permute-start.59
  360.2 2.4 add.247
  362.6 4.7 collective-permute-start.50
  367.3 2.4 add.248
  370.9 2.1 fusion.17
  373.0 6.5 %collective-permute-start.52 = (bf16[960,384]{1,0:T(8,128)(2,1)}, bf16[960,384]{1,0:T(8,128)(2,1)}, u32[]{:S(2)}, u32[]{:S(2)}) collective-permute-start(bf16[960,384]{1,0:T(8,128)(2,1)} %add.247), channel_id=1, source_target_pairs={{0,4},{1,5},{2,6},{3,7},{4,0},{5,1},{6,2},{7,3},{8,12},{9,13},{10,... | collective-permute-start | bytes 2211848 | tf_op jit(solution)/shard_map/ppermute | solution.py:829
  379.5 2.0 add.251
  381.8 3.7 collective-permute-start.53
  385.5 4.4 collective-permute-done.51
  391.8 2.4 add.252
  394.2 3.4 collective-permute-done.52
  397.6 2.4 add.253
  400.0 6.9 %collective-permute-done.53 = bf16[576,384]{1,0:T(8,128)(2,1)} collective-permute-done((bf16[576,384]{1,0:T(8,128)(2,1)}, bf16[576,384]{1,0:T(8,128)(2,1)}, u32[]{:S(2)}, u32[]{:S(2)}) %collective-permute-start.53) | collective-permute-done | bytes 442400 | tf_op jit(solution)/shard_map/ppermute | solution.py:829
  408.9 9.8 %collective-permute-done.54 = bf16[960,384]{1,0:T(8,128)(2,1)} collective-permute-done((bf16[960,384]{1,0:T(8,128)(2,1)}, bf16[960,384]{1,0:T(8,128)(2,1)}, u32[]{:S(2)}, u32[]{:S(2)}) %collective-permute-start.54) | collective-permute-done | bytes 737312 | tf_op jit(solution)/shard_map/ppermute | solution.py:829
  424.4 6.1 %collective-permute-done.56 = bf16[960,384]{1,0:T(8,128)(2,1)} collective-permute-done((bf16[960,384]{1,0:T(8,128)(2,1)}, bf16[960,384]{1,0:T(8,128)(2,1)}, u32[]{:S(2)}, u32[]{:S(2)}) %collective-permute-start.56) | collective-permute-done | bytes 737312 | tf_op jit(solution)/shard_map/ppermute | solution.py:829
  440.9 7.5 %finish.4 = f32[2,1536,768]{2,1,0:T(8,128)} custom-call(s32[7]{0:T(128)} %concatenate.6.sc, bf16[4,384,384]{2,1,0:T(8,128)(2,1)} %bitcast.76.refs_0_, bf16[4,384,384]{2,1,0:T(8,128)(2,1)} %collective-permute-done.50.refs_1_, bf16[4,384,384]{2,1,0:T(8,128)(2,1)} %collective-permute-done.61.refs_2_, bf16[4,384,384]{2,1,0:T(8,128)(2,1)} %collective-permute-done.60.refs_3_, ...), custom_call_target="tpu_custom_call" | custom-call | flops 70778880 | bytes 566231040 | tf_op jit(solution)/shard_map/finish/pallas_call | solution.py:971
  451.3 10.1 %collective-permute-done.63.refs_5_ = bf16[5,384,384]{2,1,0:T(8,128)(2,1)} collective-permute-done((bf16[5,384,384]{2,1,0:T(8,128)(2,1)}, bf16[5,384,384]{2,1,0:T(8,128)(2,1)}, u32[]{:S(2)}, u32[]{:S(2)}) %collective-permute-start.63) | collective-permute-done | bytes 1474592 | tf_op jit(solution)/shard_map/ppermute | solution.py:829
  461.4 3.6 collective-permute-start.71
  465.0 21.3 %collective-permute-done.64.refs_1_ = bf16[5,384,384]{2,1,0:T(8,128)(2,1)} collective-permute-done((bf16[5,384,384]{2,1,0:T(8,128)(2,1)}, bf16[5,384,384]{2,1,0:T(8,128)(2,1)}, u32[]{:S(2)}, u32[]{:S(2)}) %collective-permute-start.64) | collective-permute-done | bytes 1474592 | tf_op jit(solution)/shard_map/ppermute | solution.py:829
  488.0 3.1 collective-permute-done.66.refs_7_
  491.6 3.1 collective-permute-done.68.refs_3_
  494.7 4.1 finish.5
  499.7 7.5 %finish.6 = f32[2,384,3072]{2,1,0:T(8,128)} custom-call(s32[7]{0:T(128)} %concatenate.6.sc, bf16[5,384,384]{2,1,0:T(8,128)(2,1)} %bitcast.86.refs_0_, bf16[5,384,384]{2,1,0:T(8,128)(2,1)} %collective-permute-done.64.refs_1_, bf16[5,384,384]{2,1,0:T(8,128)(2,1)} %collective-permute-done.69.refs_2_, bf16[5,384,384]{2,1,0:T(8,128)(2,1)} %collective-permute-done.68.refs_3_, ...), custom_call_target="tpu_custom_call" | custom-call | flops 70778880 | bytes 566231040 | tf_op jit(solution)/shard_map/finish/pallas_call | solution.py:971
  507.3 6.3 %finish.7 = f32[2,384,2304]{2,1,0:T(8,128)} custom-call(s32[7]{0:T(128)} %concatenate.6.sc, bf16[3,384,384]{2,1,0:T(8,128)(2,1)} %bitcast.90.refs_0_, bf16[3,384,384]{2,1,0:T(8,128)(2,1)} %collective-permute-done.72.refs_1_, bf16[3,384,384]{2,1,0:T(8,128)(2,1)} %collective-permute-done.74.refs_2_, bf16[3,384,384]{2,1,0:T(8,128)(2,1)} %collective-permute-done.73.refs_3_, ...), custom_call_target="tpu_custom_call" | custom-call | flops 53084160 | bytes 424673280 | tf_op jit(solution)/shard_map/finish/pallas_call | solution.py:971
  (271 shorter events, 94.2 us)
Async XLA Ops:
  7.2 506.9 %all-reduce.2.cloned.1.call-start = ((), (), s32[]{:S(2)}) async-start(), calls=%async_computation | async-start | bytes 159744 | tf_op jit(solution)/shard_map/psum | solution.py:1140
  11.9 27.9 %collective-permute-start.5 = (bf16[768,3072]{1,0:T(8,128)(2,1)}, bf16[768,3072]{1,0:T(8,128)(2,1)}, u32[]{:S(2)}, u32[]{:S(2)}) collective-permute-start(bf16[768,3072]{1,0:T(8,128)(2,1)} %bitcast.165), channel_id=1, source_target_pairs={{0,16},{16,0},{1,17},{17,1},{2,18},{18,2},{3,19},{19,3},{4,20},{20... | collective-permute-start | bytes 14155784 | tf_op jit(solution)/shard_map/ppermute | solution.py:1002
  12.0 27.9 %collective-permute-start.6 = (bf16[3072,768]{1,0:T(8,128)(2,1)}, bf16[3072,768]{1,0:T(8,128)(2,1)}, u32[]{:S(2)}, u32[]{:S(2)}) collective-permute-start(bf16[3072,768]{1,0:T(8,128)(2,1)} %bitcast.170), channel_id=1, source_target_pairs={{0,16},{16,0},{1,17},{17,1},{2,18},{18,2},{3,19},{19,3},{4,20},{20... | collective-permute-start | bytes 14155784 | tf_op jit(solution)/shard_map/ppermute | solution.py:1002
  16.6 23.3 %collective-permute-start.4 = (bf16[768,768]{1,0:T(8,128)(2,1)}, bf16[768,768]{1,0:T(8,128)(2,1)}, u32[]{:S(2)}, u32[]{:S(2)}) collective-permute-start(bf16[768,768]{1,0:T(8,128)(2,1)} %bitcast.12.wo), channel_id=1, source_target_pairs={{0,16},{16,0},{1,17},{17,1},{2,18},{18,2},{3,19},{19,3},{4,20},{20... | collective-permute-start | bytes 3538952 | tf_op jit(solution)/shard_map/ppermute | solution.py:1002
  99.0 24.5 %collective-permute-start.9 = (bf16[2,512,1536]{2,1,0:T(8,128)(2,1)}, bf16[2,512,1536]{2,1,0:T(8,128)(2,1)}, u32[]{:S(2)}, u32[]{:S(2)}) collective-permute-start(bf16[2,512,1536]{2,1,0:T(8,128)(2,1)} %get-tuple-element.205.refs_0_), channel_id=1, source_target_pairs={{0,16},{16,0},{1,17},{17,1},{2,18},{18,2},{3,19},{19,3},{4,20},{20... | collective-permute-start | bytes 9437192 | tf_op jit(solution)/shard_map/ppermute | solution.py:1043
  101.2 19.6 %collective-permute-start.8 = (bf16[512,768]{1,0:T(8,128)(2,1)}, bf16[512,768]{1,0:T(8,128)(2,1)}, u32[]{:S(2)}, u32[]{:S(2)}) collective-permute-start(bf16[512,768]{1,0:T(8,128)(2,1)} %broadcast_select_fusion.2), channel_id=1, source_target_pairs={{0,16},{16,0},{1,17},{17,1},{2,18},{18,2},{3,19},{19,3},{4,20},{20... | collective-permute-start | bytes 2359304 | tf_op jit(solution)/shard_map/ppermute | solution.py:1048
  118.1 37.6 %collective-permute-start.14 = (bf16[512,3072]{1,0:T(8,128)(2,1)}, bf16[512,3072]{1,0:T(8,128)(2,1)}, u32[]{:S(2)}, u32[]{:S(2)}) collective-permute-start(bf16[512,3072]{1,0:T(8,128)(2,1)} %get-tuple-element.203), channel_id=1, source_target_pairs={{0,16},{16,0},{1,17},{17,1},{2,18},{18,2},{3,19},{19,3},{4,20},{20... | collective-permute-start | bytes 9437192 | tf_op jit(solution)/shard_map/ppermute | solution.py:1002
  118.7 37.0 %collective-permute-start.15 = (bf16[512,768]{1,0:T(8,128)(2,1)}, bf16[512,768]{1,0:T(8,128)(2,1)}, u32[]{:S(2)}, u32[]{:S(2)}) collective-permute-start(bf16[512,768]{1,0:T(8,128)(2,1)} %get-tuple-element.200.att), channel_id=1, source_target_pairs={{0,16},{16,0},{1,17},{17,1},{2,18},{18,2},{3,19},{19,3},{4,20},{20... | collective-permute-start | bytes 2359304 | tf_op jit(solution)/shard_map/ppermute | solution.py:1043
  118.8 12.3 %collective-permute-start.10 = (bf16[32,1536]{1,0:T(8,128)(2,1)}, bf16[32,1536]{1,0:T(8,128)(2,1)S(1)}, u32[]{:S(2)}, u32[]{:S(2)}) collective-permute-start(bf16[32,1536]{1,0:T(8,128)(2,1)} %get-tuple-element.210), channel_id=1, source_target_pairs={{0,8},{8,0},{1,9},{9,1},{2,10},{10,2},{3,11},{11,3},{4,12},{12,4},... | collective-permute-start | bytes 294920 | tf_op jit(solution)/shard_map/ppermute | solution.py:1112
  120.8 34.3 %collective-permute-start.16 = (bf16[512,768]{1,0:T(8,128)(2,1)}, bf16[512,768]{1,0:T(8,128)(2,1)}, u32[]{:S(2)}, u32[]{:S(2)}) collective-permute-start(bf16[512,768]{1,0:T(8,128)(2,1)} %get-tuple-element.219), channel_id=1, source_target_pairs={{0,16},{16,0},{1,17},{17,1},{2,18},{18,2},{3,19},{19,3},{4,20},{20... | collective-permute-start | bytes 2359304 | tf_op jit(solution)/shard_map/ppermute | solution.py:1002
  123.5 31.8 %collective-permute-start.13 = (bf16[512,768]{1,0:T(8,128)(2,1)}, bf16[512,768]{1,0:T(8,128)(2,1)}, u32[]{:S(2)}, u32[]{:S(2)}) collective-permute-start(bf16[512,768]{1,0:T(8,128)(2,1)} %get-tuple-element.218), channel_id=1, source_target_pairs={{0,16},{16,0},{1,17},{17,1},{2,18},{18,2},{3,19},{19,3},{4,20},{20... | collective-permute-start | bytes 2359304 | tf_op jit(solution)/shard_map/ppermute | solution.py:1043
  131.0 22.0 %collective-permute-start.11 = (bf16[4,384,384]{2,1,0:T(8,128)(2,1)}, bf16[4,384,384]{2,1,0:T(8,128)(2,1)}, u32[]{:S(2)}, u32[]{:S(2)}) collective-permute-start(bf16[4,384,384]{2,1,0:T(8,128)(2,1)} %get-tuple-element.206), channel_id=1, source_target_pairs={{0,8},{1,9},{2,10},{3,11},{4,12},{5,13},{6,14},{7,15},{8,0},{9,1},... | collective-permute-start | bytes 3538952 | tf_op jit(solution)/shard_map/ppermute | solution.py:829
  153.0 15.6 %collective-permute-start.17 = (bf16[2,512,1536]{2,1,0:T(8,128)(2,1)}, bf16[2,512,1536]{2,1,0:T(8,128)(2,1)}, u32[]{:S(2)}, u32[]{:S(2)}) collective-permute-start(bf16[2,512,1536]{2,1,0:T(8,128)(2,1)} %get-tuple-element.223.refs_0_), channel_id=1, source_target_pairs={{0,16},{16,0},{1,17},{17,1},{2,18},{18,2},{3,19},{19,3},{4,20},{20... | collective-permute-start | bytes 9437192 | tf_op jit(solution)/shard_map/ppermute | solution.py:1043
  155.1 46.6 %collective-permute-start.22 = (bf16[512,768]{1,0:T(8,128)(2,1)}, bf16[512,768]{1,0:T(8,128)(2,1)}, u32[]{:S(2)}, u32[]{:S(2)}) collective-permute-start(bf16[512,768]{1,0:T(8,128)(2,1)} %get-tuple-element.235), channel_id=1, source_target_pairs={{0,16},{16,0},{1,17},{17,1},{2,18},{18,2},{3,19},{19,3},{4,20},{20... | collective-permute-start | bytes 2359304 | tf_op jit(solution)/shard_map/ppermute | solution.py:1043
  155.3 94.1 %collective-permute-start.28 = (bf16[512,768]{1,0:T(8,128)(2,1)}, bf16[512,768]{1,0:T(8,128)(2,1)}, u32[]{:S(2)}, u32[]{:S(2)}) collective-permute-start(bf16[512,768]{1,0:T(8,128)(2,1)} %get-tuple-element.227.att), channel_id=1, source_target_pairs={{0,16},{16,0},{1,17},{17,1},{2,18},{18,2},{3,19},{19,3},{4,20},{20... | collective-permute-start | bytes 2359304 | tf_op jit(solution)/shard_map/ppermute | solution.py:1043
  155.7 15.5 %collective-permute-start.18 = (bf16[512,768]{1,0:T(8,128)(2,1)S(1)}, bf16[512,768]{1,0:T(8,128)(2,1)S(1)}, u32[]{:S(2)}, u32[]{:S(2)}) collective-permute-start(bf16[512,768]{1,0:T(8,128)(2,1)S(1)} %copy-done.2), channel_id=1, source_target_pairs={{0,16},{16,0},{1,17},{17,1},{2,18},{18,2},{3,19},{19,3},{4,20},{20... | collective-permute-start | bytes 2359304 | tf_op jit(solution)/shard_map/ppermute | solution.py:1002
  166.4 36.6 %collective-permute-start.23 = (bf16[512,2304]{1,0:T(8,128)(2,1)}, bf16[512,2304]{1,0:T(8,128)(2,1)}, u32[]{:S(2)}, u32[]{:S(2)}) collective-permute-start(bf16[512,2304]{1,0:T(8,128)(2,1)} %get-tuple-element.215), channel_id=1, source_target_pairs={{0,16},{16,0},{1,17},{17,1},{2,18},{18,2},{3,19},{19,3},{4,20},{20... | collective-permute-start | bytes 7077896 | tf_op jit(solution)/shard_map/ppermute | solution.py:1002
  168.6 30.3 %collective-permute-start.21 = (bf16[768,384]{1,0:T(8,128)(2,1)}, bf16[768,384]{1,0:T(8,128)(2,1)}, u32[]{:S(2)}, u32[]{:S(2)}) collective-permute-start(bf16[768,384]{1,0:T(8,128)(2,1)} %fusion.7), channel_id=1, source_target_pairs={{0,4},{1,5},{2,6},{3,7},{4,0},{5,1},{6,2},{7,3},{8,12},{9,13},{10,... | collective-permute-start | bytes 1769480 | tf_op jit(solution)/shard_map/ppermute | solution.py:829
  179.3 18.3 %collective-permute-start.19 = (bf16[4,384,384]{2,1,0:T(8,128)(2,1)}, bf16[4,384,384]{2,1,0:T(8,128)(2,1)}, u32[]{:S(2)}, u32[]{:S(2)}) collective-permute-start(bf16[4,384,384]{2,1,0:T(8,128)(2,1)} %get-tuple-element.224), channel_id=1, source_target_pairs={{0,8},{1,9},{2,10},{3,11},{4,12},{5,13},{6,14},{7,15},{8,0},{9,1},... | collective-permute-start | bytes 3538952 | tf_op jit(solution)/shard_map/ppermute | solution.py:829
  197.6 50.8 %collective-permute-start.26 = (bf16[512,768]{1,0:T(8,128)(2,1)}, bf16[512,768]{1,0:T(8,128)(2,1)}, u32[]{:S(2)}, u32[]{:S(2)}) collective-permute-start(bf16[512,768]{1,0:T(8,128)(2,1)} %get-tuple-element.246), channel_id=1, source_target_pairs={{0,16},{16,0},{1,17},{17,1},{2,18},{18,2},{3,19},{19,3},{4,20},{20... | collective-permute-start | bytes 2359304 | tf_op jit(solution)/shard_map/ppermute | solution.py:1043
  198.9 48.0 %collective-permute-start.25 = (bf16[5,384,384]{2,1,0:T(8,128)(2,1)}, bf16[5,384,384]{2,1,0:T(8,128)(2,1)}, u32[]{:S(2)}, u32[]{:S(2)}) collective-permute-start(bf16[5,384,384]{2,1,0:T(8,128)(2,1)} %get-tuple-element.220), channel_id=1, source_target_pairs={{0,1},{1,0},{2,3},{3,2},{4,5},{5,4},{6,7},{7,6},{8,9},{9,8},{10,11... | collective-permute-start | bytes 4423688 | tf_op jit(solution)/shard_map/ppermute | solution.py:829
  201.7 49.7 %collective-permute-start.27 = (bf16[512,3072]{1,0:T(8,128)(2,1)}, bf16[512,3072]{1,0:T(8,128)(2,1)}, u32[]{:S(2)}, u32[]{:S(2)}) collective-permute-start(bf16[512,3072]{1,0:T(8,128)(2,1)} %get-tuple-element.231), channel_id=1, source_target_pairs={{0,16},{16,0},{1,17},{17,1},{2,18},{18,2},{3,19},{19,3},{4,20},{20... | collective-permute-start | bytes 9437192 | tf_op jit(solution)/shard_map/ppermute | solution.py:1002
  203.0 21.9 %collective-permute-start.20 = (bf16[768,384]{1,0:T(8,128)(2,1)S(1)}, bf16[768,384]{1,0:T(8,128)(2,1)S(1)}, u32[]{:S(2)}, u32[]{:S(2)}) collective-permute-start(bf16[768,384]{1,0:T(8,128)(2,1)S(1)} %fusion.11), channel_id=1, source_target_pairs={{0,1},{1,0},{2,3},{3,2},{4,5},{5,4},{6,7},{7,6},{8,9},{9,8},{10,11... | collective-permute-start | bytes 1769480 | tf_op jit(solution)/shard_map/ppermute | solution.py:829
  229.5 20.9 %collective-permute-start.29 = (bf16[512,768]{1,0:T(8,128)(2,1)}, bf16[512,768]{1,0:T(8,128)(2,1)}, u32[]{:S(2)}, u32[]{:S(2)}) collective-permute-start(bf16[512,768]{1,0:T(8,128)(2,1)} %get-tuple-element.247), channel_id=1, source_target_pairs={{0,16},{16,0},{1,17},{17,1},{2,18},{18,2},{3,19},{19,3},{4,20},{20... | collective-permute-start | bytes 2359304 | tf_op jit(solution)/shard_map/ppermute | solution.py:1002
  246.9 37.2 %collective-permute-start.34 = (bf16[512,768]{1,0:T(8,128)(2,1)}, bf16[512,768]{1,0:T(8,128)(2,1)}, u32[]{:S(2)}, u32[]{:S(2)}) collective-permute-start(bf16[512,768]{1,0:T(8,128)(2,1)} %get-tuple-element.254), channel_id=1, source_target_pairs={{0,16},{16,0},{1,17},{17,1},{2,18},{18,2},{3,19},{19,3},{4,20},{20... | collective-permute-start | bytes 2359304 | tf_op jit(solution)/shard_map/ppermute | solution.py:1043
  248.4 46.0 %collective-permute-start.31 = (bf16[3,384,384]{2,1,0:T(8,128)(2,1)}, bf16[3,384,384]{2,1,0:T(8,128)(2,1)}, u32[]{:S(2)}, u32[]{:S(2)}) collective-permute-start(bf16[3,384,384]{2,1,0:T(8,128)(2,1)} %get-tuple-element.236), channel_id=1, source_target_pairs={{0,4},{1,5},{2,6},{3,7},{4,0},{5,1},{6,2},{7,3},{8,12},{9,13},{10,... | collective-permute-start | bytes 2654216 | tf_op jit(solution)/shard_map/ppermute | solution.py:829
  249.4 23.4 %collective-permute-start.33 = (bf16[768,384]{1,0:T(8,128)(2,1)S(1)}, bf16[768,384]{1,0:T(8,128)(2,1)}, u32[]{:S(2)}, u32[]{:S(2)}) collective-permute-start(bf16[768,384]{1,0:T(8,128)(2,1)S(1)} %copy-done.10), channel_id=1, source_target_pairs={{0,2},{1,3},{2,0},{3,1},{4,6},{5,7},{6,4},{7,5},{8,10},{9,11},{10,... | collective-permute-start | bytes 1769480 | tf_op jit(solution)/shard_map/ppermute | solution.py:829
  250.4 30.3 %collective-permute-start.32 = (bf16[960,384]{1,0:T(8,128)(2,1)S(1)}, bf16[960,384]{1,0:T(8,128)(2,1)S(1)}, u32[]{:S(2)}, u32[]{:S(2)}) collective-permute-start(bf16[960,384]{1,0:T(8,128)(2,1)S(1)} %fusion), channel_id=1, source_target_pairs={{0,2},{1,3},{2,0},{3,1},{4,6},{5,7},{6,4},{7,5},{8,10},{9,11},{10,... | collective-permute-start | bytes 2211848 | tf_op jit(solution)/shard_map/ppermute | solution.py:829
  251.4 36.1 %collective-permute-start.35 = (bf16[512,2304]{1,0:T(8,128)(2,1)}, bf16[512,2304]{1,0:T(8,128)(2,1)}, u32[]{:S(2)}, u32[]{:S(2)}) collective-permute-start(bf16[512,2304]{1,0:T(8,128)(2,1)} %get-tuple-element.258.d_proj), channel_id=1, source_target_pairs={{0,16},{16,0},{1,17},{17,1},{2,18},{18,2},{3,19},{19,3},{4,20},{20... | collective-permute-start | bytes 7077896 | tf_op jit(solution)/shard_map/ppermute | solution.py:1002
  272.8 42.6 %collective-permute-start.37 = (bf16[768,384]{1,0:T(8,128)(2,1)}, bf16[768,384]{1,0:T(8,128)(2,1)}, u32[]{:S(2)}, u32[]{:S(2)}) collective-permute-start(bf16[768,384]{1,0:T(8,128)(2,1)} %add.227), channel_id=1, source_target_pairs={{0,2},{1,3},{2,0},{3,1},{4,6},{5,7},{6,4},{7,5},{8,10},{9,11},{10,... | collective-permute-start | bytes 1769480 | tf_op jit(solution)/shard_map/ppermute | solution.py:829
  280.7 20.9 %collective-permute-start.30 = (bf16[5,384,384]{2,1,0:T(8,128)(2,1)}, bf16[5,384,384]{2,1,0:T(8,128)(2,1)S(1)}, u32[]{:S(2)}, u32[]{:S(2)}) collective-permute-start(bf16[5,384,384]{2,1,0:T(8,128)(2,1)} %get-tuple-element.249), channel_id=1, source_target_pairs={{0,1},{1,0},{2,3},{3,2},{4,5},{5,4},{6,7},{7,6},{8,9},{9,8},{10,11... | collective-permute-start | bytes 4423688 | tf_op jit(solution)/shard_map/ppermute | solution.py:829
  284.1 48.6 %collective-permute-start.41 = (bf16[768,384]{1,0:T(8,128)(2,1)}, bf16[768,384]{1,0:T(8,128)(2,1)}, u32[]{:S(2)}, u32[]{:S(2)}) collective-permute-start(bf16[768,384]{1,0:T(8,128)(2,1)} %add.234), channel_id=1, source_target_pairs={{0,4},{1,5},{2,6},{3,7},{4,0},{5,1},{6,2},{7,3},{8,12},{9,13},{10,... | collective-permute-start | bytes 1769480 | tf_op jit(solution)/shard_map/ppermute | solution.py:829
  287.5 75.1 %collective-permute-start.46 = (bf16[960,384]{1,0:T(8,128)(2,1)}, bf16[960,384]{1,0:T(8,128)(2,1)}, u32[]{:S(2)}, u32[]{:S(2)}) collective-permute-start(bf16[960,384]{1,0:T(8,128)(2,1)} %fusion.2), channel_id=1, source_target_pairs={{0,4},{1,5},{2,6},{3,7},{4,0},{5,1},{6,2},{7,3},{8,12},{9,13},{10,... | collective-permute-start | bytes 2211848 | tf_op jit(solution)/shard_map/ppermute | solution.py:829
  294.4 25.1 %collective-permute-start.38 = (bf16[3,384,384]{2,1,0:T(8,128)(2,1)}, bf16[3,384,384]{2,1,0:T(8,128)(2,1)}, u32[]{:S(2)}, u32[]{:S(2)}) collective-permute-start(bf16[3,384,384]{2,1,0:T(8,128)(2,1)} %get-tuple-element.255), channel_id=1, source_target_pairs={{0,8},{1,9},{2,10},{3,11},{4,12},{5,13},{6,14},{7,15},{8,0},{9,1},... | collective-permute-start | bytes 2654216 | tf_op jit(solution)/shard_map/ppermute | solution.py:829
  301.6 21.9 %collective-permute-start.39 = (bf16[576,384]{1,0:T(8,128)(2,1)}, bf16[576,384]{1,0:T(8,128)(2,1)}, u32[]{:S(2)}, u32[]{:S(2)}) collective-permute-start(bf16[576,384]{1,0:T(8,128)(2,1)} %fusion.12), channel_id=1, source_target_pairs={{0,8},{1,9},{2,10},{3,11},{4,12},{5,13},{6,14},{7,15},{8,0},{9,1},... | collective-permute-start | bytes 1327112 | tf_op jit(solution)/shard_map/ppermute | solution.py:829
  315.4 13.2 %collective-permute-start.40 = (bf16[960,384]{1,0:T(8,128)(2,1)}, bf16[960,384]{1,0:T(8,128)(2,1)}, u32[]{:S(2)}, u32[]{:S(2)}) collective-permute-start(bf16[960,384]{1,0:T(8,128)(2,1)} %fusion.3), channel_id=1, source_target_pairs={{0,8},{1,9},{2,10},{3,11},{4,12},{5,13},{6,14},{7,15},{8,0},{9,1},... | collective-permute-start | bytes 2211848 | tf_op jit(solution)/shard_map/ppermute | solution.py:829
  319.5 16.5 %collective-permute-start.42 = (bf16[768,384]{1,0:T(8,128)(2,1)}, bf16[768,384]{1,0:T(8,128)(2,1)}, u32[]{:S(2)}, u32[]{:S(2)}) collective-permute-start(bf16[768,384]{1,0:T(8,128)(2,1)} %add.238), channel_id=1, source_target_pairs={{0,1},{1,0},{2,3},{3,2},{4,5},{5,4},{6,7},{7,6},{8,9},{9,8},{10,11... | collective-permute-start | bytes 1769480 | tf_op jit(solution)/shard_map/ppermute | solution.py:829
  323.5 16.0 %collective-permute-start.36 = (bf16[512,768]{1,0:T(8,128)(2,1)}, bf16[512,768]{1,0:T(8,128)(2,1)}, u32[]{:S(2)}, u32[]{:S(2)}) collective-permute-start(bf16[512,768]{1,0:T(8,128)(2,1)} %broadcast_select_fusion), channel_id=1, source_target_pairs={{0,16},{16,0},{1,17},{17,1},{2,18},{18,2},{3,19},{19,3},{4,20},{20... | collective-permute-start | bytes 2359304 | tf_op jit(solution)/shard_map/ppermute | solution.py:1048
  328.6 16.4 %collective-permute-start.43 = (bf16[576,384]{1,0:T(8,128)(2,1)}, bf16[576,384]{1,0:T(8,128)(2,1)}, u32[]{:S(2)}, u32[]{:S(2)}) collective-permute-start(bf16[576,384]{1,0:T(8,128)(2,1)} %fusion.15), channel_id=1, source_target_pairs={{0,1},{1,0},{2,3},{3,2},{4,5},{5,4},{6,7},{7,6},{8,9},{9,8},{10,11... | collective-permute-start | bytes 1327112 | tf_op jit(solution)/shard_map/ppermute | solution.py:829
  332.7 37.0 %collective-permute-start.48 = (bf16[576,384]{1,0:T(8,128)(2,1)}, bf16[576,384]{1,0:T(8,128)(2,1)}, u32[]{:S(2)}, u32[]{:S(2)}) collective-permute-start(bf16[576,384]{1,0:T(8,128)(2,1)} %fusion.13), channel_id=1, source_target_pairs={{0,1},{1,0},{2,3},{3,2},{4,5},{5,4},{6,7},{7,6},{8,9},{9,8},{10,11... | collective-permute-start | bytes 1327112 | tf_op jit(solution)/shard_map/ppermute | solution.py:829
  336.1 15.9 %collective-permute-start.44 = (bf16[768,384]{1,0:T(8,128)(2,1)}, bf16[768,384]{1,0:T(8,128)(2,1)}, u32[]{:S(2)}, u32[]{:S(2)}) collective-permute-start(bf16[768,384]{1,0:T(8,128)(2,1)} %add.245), channel_id=1, source_target_pairs={{0,1},{1,0},{2,3},{3,2},{4,5},{5,4},{6,7},{7,6},{8,9},{9,8},{10,11... | collective-permute-start | bytes 1769480 | tf_op jit(solution)/shard_map/ppermute | solution.py:829
  339.5 19.9 %collective-permute-start.45 = (bf16[960,384]{1,0:T(8,128)(2,1)}, bf16[960,384]{1,0:T(8,128)(2,1)}, u32[]{:S(2)}, u32[]{:S(2)}) collective-permute-start(bf16[960,384]{1,0:T(8,128)(2,1)} %fusion.5), channel_id=1, source_target_pairs={{0,2},{1,3},{2,0},{3,1},{4,6},{5,7},{6,4},{7,5},{8,10},{9,11},{10,... | collective-permute-start | bytes 2211848 | tf_op jit(solution)/shard_map/ppermute | solution.py:829
  345.0 24.6 %collective-permute-start.47 = (bf16[4,384,384]{2,1,0:T(8,128)(2,1)}, bf16[4,384,384]{2,1,0:T(8,128)(2,1)}, u32[]{:S(2)}, u32[]{:S(2)}) collective-permute-start(bf16[4,384,384]{2,1,0:T(8,128)(2,1)} %bitcast.73.refs_4_), channel_id=1, source_target_pairs={{0,8},{1,9},{2,10},{3,11},{4,12},{5,13},{6,14},{7,15},{8,0},{9,1},... | collective-permute-start | bytes 3538952 | tf_op jit(solution)/shard_map/ppermute | solution.py:829
  351.9 85.8 %collective-permute-start.59 = (bf16[4,384,384]{2,1,0:T(8,128)(2,1)}, bf16[4,384,384]{2,1,0:T(8,128)(2,1)}, u32[]{:S(2)}, u32[]{:S(2)}) collective-permute-start(bf16[4,384,384]{2,1,0:T(8,128)(2,1)} %bitcast.73.refs_4_), channel_id=1, source_target_pairs={{0,16},{16,0},{1,17},{17,1},{2,18},{18,2},{3,19},{19,3},{4,20},{20... | collective-permute-start | bytes 3538952 | tf_op jit(solution)/shard_map/ppermute | solution.py:938
  359.4 13.6 %collective-permute-start.49 = (bf16[576,384]{1,0:T(8,128)(2,1)}, bf16[576,384]{1,0:T(8,128)(2,1)}, u32[]{:S(2)}, u32[]{:S(2)}) collective-permute-start(bf16[576,384]{1,0:T(8,128)(2,1)} %add.246), channel_id=1, source_target_pairs={{0,2},{1,3},{2,0},{3,1},{4,6},{5,7},{6,4},{7,5},{8,10},{9,11},{10,... | collective-permute-start | bytes 1327112 | tf_op jit(solution)/shard_map/ppermute | solution.py:829
  362.6 19.2 %collective-permute-start.50 = (bf16[4,384,384]{2,1,0:T(8,128)(2,1)}, bf16[4,384,384]{2,1,0:T(8,128)(2,1)}, u32[]{:S(2)}, u32[]{:S(2)}) collective-permute-start(bf16[4,384,384]{2,1,0:T(8,128)(2,1)} %bitcast.76.refs_0_), channel_id=1, source_target_pairs={{0,8},{1,9},{2,10},{3,11},{4,12},{5,13},{6,14},{7,15},{8,0},{9,1},... | collective-permute-start | bytes 3538952 | tf_op jit(solution)/shard_map/ppermute | solution.py:829
  369.7 70.1 %collective-permute-start.61 = (bf16[4,384,384]{2,1,0:T(8,128)(2,1)}, bf16[4,384,384]{2,1,0:T(8,128)(2,1)}, u32[]{:S(2)}, u32[]{:S(2)}) collective-permute-start(bf16[4,384,384]{2,1,0:T(8,128)(2,1)} %bitcast.76.refs_0_), channel_id=1, source_target_pairs={{0,16},{16,0},{1,17},{17,1},{2,18},{18,2},{3,19},{19,3},{4,20},{20... | collective-permute-start | bytes 3538952 | tf_op jit(solution)/shard_map/ppermute | solution.py:938
  369.7 20.1 %collective-permute-start.51 = (bf16[960,384]{1,0:T(8,128)(2,1)}, bf16[960,384]{1,0:T(8,128)(2,1)}, u32[]{:S(2)}, u32[]{:S(2)}) collective-permute-start(bf16[960,384]{1,0:T(8,128)(2,1)} %add.248), channel_id=1, source_target_pairs={{0,8},{1,9},{2,10},{3,11},{4,12},{5,13},{6,14},{7,15},{8,0},{9,1},... | collective-permute-start | bytes 2211848 | tf_op jit(solution)/shard_map/ppermute | solution.py:829
  373.0 24.6 %collective-permute-start.52 = (bf16[960,384]{1,0:T(8,128)(2,1)}, bf16[960,384]{1,0:T(8,128)(2,1)}, u32[]{:S(2)}, u32[]{:S(2)}) collective-permute-start(bf16[960,384]{1,0:T(8,128)(2,1)} %add.247), channel_id=1, source_target_pairs={{0,4},{1,5},{2,6},{3,7},{4,0},{5,1},{6,2},{7,3},{8,12},{9,13},{10,... | collective-permute-start | bytes 2211848 | tf_op jit(solution)/shard_map/ppermute | solution.py:829
  381.8 25.1 %collective-permute-start.53 = (bf16[576,384]{1,0:T(8,128)(2,1)}, bf16[576,384]{1,0:T(8,128)(2,1)}, u32[]{:S(2)}, u32[]{:S(2)}) collective-permute-start(bf16[576,384]{1,0:T(8,128)(2,1)} %fusion.17), channel_id=1, source_target_pairs={{0,4},{1,5},{2,6},{3,7},{4,0},{5,1},{6,2},{7,3},{8,12},{9,13},{10,... | collective-permute-start | bytes 1327112 | tf_op jit(solution)/shard_map/ppermute | solution.py:829
  389.9 31.7 %collective-permute-start.55 = (bf16[576,384]{1,0:T(8,128)(2,1)}, bf16[576,384]{1,0:T(8,128)(2,1)}, u32[]{:S(2)}, u32[]{:S(2)}) collective-permute-start(bf16[576,384]{1,0:T(8,128)(2,1)} %add.251), channel_id=1, source_target_pairs={{0,8},{1,9},{2,10},{3,11},{4,12},{5,13},{6,14},{7,15},{8,0},{9,1},... | collective-permute-start | bytes 1327112 | tf_op jit(solution)/shard_map/ppermute | solution.py:829
  397.6 41.2 %collective-permute-start.58 = (bf16[4,384,384]{2,1,0:T(8,128)(2,1)}, bf16[4,384,384]{2,1,0:T(8,128)(2,1)}, u32[]{:S(2)}, u32[]{:S(2)}) collective-permute-start(bf16[4,384,384]{2,1,0:T(8,128)(2,1)} %collective-permute-done.47.refs_5_), channel_id=1, source_target_pairs={{0,16},{16,0},{1,17},{17,1},{2,18},{18,2},{3,19},{19,3},{4,20},{20... | collective-permute-start | bytes 3538952 | tf_op jit(solution)/shard_map/ppermute | solution.py:938
  406.9 11.8 %collective-permute-start.54 = (bf16[960,384]{1,0:T(8,128)(2,1)}, bf16[960,384]{1,0:T(8,128)(2,1)}, u32[]{:S(2)}, u32[]{:S(2)}) collective-permute-start(bf16[960,384]{1,0:T(8,128)(2,1)} %add.252), channel_id=1, source_target_pairs={{0,2},{1,3},{2,0},{3,1},{4,6},{5,7},{6,4},{7,5},{8,10},{9,11},{10,... | collective-permute-start | bytes 2211848 | tf_op jit(solution)/shard_map/ppermute | solution.py:829
  418.8 11.8 %collective-permute-start.56 = (bf16[960,384]{1,0:T(8,128)(2,1)}, bf16[960,384]{1,0:T(8,128)(2,1)}, u32[]{:S(2)}, u32[]{:S(2)}) collective-permute-start(bf16[960,384]{1,0:T(8,128)(2,1)} %add.253), channel_id=1, source_target_pairs={{0,8},{1,9},{2,10},{3,11},{4,12},{5,13},{6,14},{7,15},{8,0},{9,1},... | collective-permute-start | bytes 2211848 | tf_op jit(solution)/shard_map/ppermute | solution.py:829
  421.5 13.2 %collective-permute-start.57 = (bf16[576,384]{1,0:T(8,128)(2,1)}, bf16[576,384]{1,0:T(8,128)(2,1)}, u32[]{:S(2)}, u32[]{:S(2)}) collective-permute-start(bf16[576,384]{1,0:T(8,128)(2,1)} %add.254), channel_id=1, source_target_pairs={{0,2},{1,3},{2,0},{3,1},{4,6},{5,7},{6,4},{7,5},{8,10},{9,11},{10,... | collective-permute-start | bytes 1327112 | tf_op jit(solution)/shard_map/ppermute | solution.py:829
  436.8 11.7 %collective-permute-start.62 = (bf16[576,384]{1,0:T(8,128)(2,1)}, bf16[576,384]{1,0:T(8,128)(2,1)}, u32[]{:S(2)}, u32[]{:S(2)}) collective-permute-start(bf16[576,384]{1,0:T(8,128)(2,1)} %add.255), channel_id=1, source_target_pairs={{0,1},{1,0},{2,3},{3,2},{4,5},{5,4},{6,7},{7,6},{8,9},{9,8},{10,11... | collective-permute-start | bytes 1327112 | tf_op jit(solution)/shard_map/ppermute | solution.py:829
  437.7 23.7 %collective-permute-start.63 = (bf16[5,384,384]{2,1,0:T(8,128)(2,1)}, bf16[5,384,384]{2,1,0:T(8,128)(2,1)}, u32[]{:S(2)}, u32[]{:S(2)}) collective-permute-start(bf16[5,384,384]{2,1,0:T(8,128)(2,1)} %bitcast.80.refs_4_), channel_id=1, source_target_pairs={{0,1},{1,0},{2,3},{3,2},{4,5},{5,4},{6,7},{7,6},{8,9},{9,8},{10,11... | collective-permute-start | bytes 4423688 | tf_op jit(solution)/shard_map/ppermute | solution.py:829
  438.8 47.5 %collective-permute-start.64 = (bf16[5,384,384]{2,1,0:T(8,128)(2,1)}, bf16[5,384,384]{2,1,0:T(8,128)(2,1)}, u32[]{:S(2)}, u32[]{:S(2)}) collective-permute-start(bf16[5,384,384]{2,1,0:T(8,128)(2,1)} %bitcast.86.refs_0_), channel_id=1, source_target_pairs={{0,1},{1,0},{2,3},{3,2},{4,5},{5,4},{6,7},{7,6},{8,9},{9,8},{10,11... | collective-permute-start | bytes 4423688 | tf_op jit(solution)/shard_map/ppermute | solution.py:829
  439.7 47.7 %collective-permute-start.65 = (bf16[3,384,384]{2,1,0:T(8,128)(2,1)}, bf16[3,384,384]{2,1,0:T(8,128)(2,1)}, u32[]{:S(2)}, u32[]{:S(2)}) collective-permute-start(bf16[3,384,384]{2,1,0:T(8,128)(2,1)} %bitcast.83.refs_4_), channel_id=1, source_target_pairs={{0,4},{1,5},{2,6},{3,7},{4,0},{5,1},{6,2},{7,3},{8,12},{9,13},{10,... | collective-permute-start | bytes 2654216 | tf_op jit(solution)/shard_map/ppermute | solution.py:829
  440.9 46.5 %collective-permute-start.67 = (bf16[5,384,384]{2,1,0:T(8,128)(2,1)}, bf16[5,384,384]{2,1,0:T(8,128)(2,1)}, u32[]{:S(2)}, u32[]{:S(2)}) collective-permute-start(bf16[5,384,384]{2,1,0:T(8,128)(2,1)} %bitcast.80.refs_4_), channel_id=1, source_target_pairs={{0,16},{16,0},{1,17},{17,1},{2,18},{18,2},{3,19},{19,3},{4,20},{20... | collective-permute-start | bytes 4423688 | tf_op jit(solution)/shard_map/ppermute | solution.py:938
  448.5 42.8 %collective-permute-start.69 = (bf16[5,384,384]{2,1,0:T(8,128)(2,1)}, bf16[5,384,384]{2,1,0:T(8,128)(2,1)}, u32[]{:S(2)}, u32[]{:S(2)}) collective-permute-start(bf16[5,384,384]{2,1,0:T(8,128)(2,1)} %bitcast.86.refs_0_), channel_id=1, source_target_pairs={{0,16},{16,0},{1,17},{17,1},{2,18},{18,2},{3,19},{19,3},{4,20},{20... | collective-permute-start | bytes 4423688 | tf_op jit(solution)/shard_map/ppermute | solution.py:938
  461.4 37.4 %collective-permute-start.71 = (bf16[3,384,384]{2,1,0:T(8,128)(2,1)}, bf16[3,384,384]{2,1,0:T(8,128)(2,1)}, u32[]{:S(2)}, u32[]{:S(2)}) collective-permute-start(bf16[3,384,384]{2,1,0:T(8,128)(2,1)} %bitcast.83.refs_4_), channel_id=1, source_target_pairs={{0,16},{16,0},{1,17},{17,1},{2,18},{18,2},{3,19},{19,3},{4,20},{20... | collective-permute-start | bytes 2654216 | tf_op jit(solution)/shard_map/ppermute | solution.py:938
  486.3 13.4 %collective-permute-start.72 = (bf16[3,384,384]{2,1,0:T(8,128)(2,1)}, bf16[3,384,384]{2,1,0:T(8,128)(2,1)}, u32[]{:S(2)}, u32[]{:S(2)}) collective-permute-start(bf16[3,384,384]{2,1,0:T(8,128)(2,1)} %bitcast.90.refs_0_), channel_id=1, source_target_pairs={{0,8},{1,9},{2,10},{3,11},{4,12},{5,13},{6,14},{7,15},{8,0},{9,1},... | collective-permute-start | bytes 2654216 | tf_op jit(solution)/shard_map/ppermute | solution.py:829
  487.5 19.8 %collective-permute-start.74 = (bf16[3,384,384]{2,1,0:T(8,128)(2,1)}, bf16[3,384,384]{2,1,0:T(8,128)(2,1)}, u32[]{:S(2)}, u32[]{:S(2)}) collective-permute-start(bf16[3,384,384]{2,1,0:T(8,128)(2,1)} %bitcast.90.refs_0_), channel_id=1, source_target_pairs={{0,16},{16,0},{1,17},{17,1},{2,18},{18,2},{3,19},{19,3},{4,20},{20... | collective-permute-start | bytes 2654216 | tf_op jit(solution)/shard_map/ppermute | solution.py:938
  (41 other events, 296.3 us)
Sparse Core Ops, SparseCore 0:
  339.6 128.8 all-reduce.1
